TPU v7x, 32 devices: a whole 2x2x4 slice. The times are simulated.
32 devices in a mesh: dp: 16 (over z, x, core), tensor: 2 (over y).
Axes of the slice: x: 2, y: 2, z: 4, core: 2. Of those that a mesh axis runs over, the one named last changes fastest.
Arguments:
- tokens: bfloat16 [4096, 2048], P('dp'), may hold values from -6 to 6
- lengths: int32 [16, 4], P('dp'), may hold values from 1 to 128, 256 in all within a row
- routes: int32 [4096, 6], P('dp'), may hold values from 0 to 15, all different within a row; in each aligned block of 256 rows (0 to 255, 256 to 511, ...) at most 128 rows name the same one
- grad_out: bfloat16 [4096, 2048], P('dp'), may hold values from -6 to 6
- g_attn: float32 [2048], replicated, may hold values from 0.5 to 1.5
- w_query: bfloat16 [2048, 3072], P(None, 'tensor')
- key_value_down_weight: bfloat16 [2048, 576], replicated, may hold values from -0.125 to 0.125
- latent_norm_gain: float32 [512], replicated, may hold values from 0.5 to 1.5
- key_value_up_weight: bfloat16 [512, 4096], P(None, 'tensor'), may hold values from -0.25 to 0.25
- w_out: bfloat16 [2048, 2048], P(None, 'tensor'), may hold values from -1 to 1
- g_ffn: float32 [2048], replicated, may hold values from 0.5 to 1.5
- router: float32 [2048, 16], replicated
- shared_gate: bfloat16 [2048, 2816], P(None, 'tensor'), may hold values from -0.125 to 0.125
- shared_up: bfloat16 [2048, 2816], P(None, 'tensor'), may hold values from -0.125 to 0.125
- shared_down: bfloat16 [2048, 2816], P(None, 'tensor'), may hold values from -0.109375 to 0.109375
- expert_gate: bfloat16 [16, 2048, 1408], P('dp', None, 'tensor'), may hold values from -0.125 to 0.125
- expert_up: bfloat16 [16, 2048, 1408], P('dp', None, 'tensor'), may hold values from -0.125 to 0.125
- expert_down: bfloat16 [16, 2048, 1408], P('dp', None, 'tensor'), may hold values from -0.625 to 0.625
Outputs:
- output: bfloat16 [4096, 2048], P('dp')
- grad_tokens: float32 [4096, 2048], P('dp')
- grad_g_attn: float32 [2048], P('dp')
- grad_w_query: float32 [2048, 3072], P('dp', 'tensor')
- grad_w_kv_down: float32 [2048, 576], P('dp', 'tensor')
- grad_g_kv: float32 [512], P(('dp', 'tensor'))
- grad_w_kv_up: float32 [512, 4096], P('dp', 'tensor')
- grad_w_out: float32 [2048, 2048], P('dp', 'tensor')
- grad_g_ffn: float32 [2048], P('dp')
- grad_router: float32 [2048, 16], P(('dp', 'tensor'))
- grad_shared_gate: float32 [2048, 2816], P('dp', 'tensor')
- grad_shared_up: float32 [2048, 2816], P('dp', 'tensor')
- grad_shared_down: float32 [2048, 2816], P('dp', 'tensor')
- grad_expert_gate: float32 [16, 2048, 1408], P('dp', None, 'tensor')
- grad_expert_up: float32 [16, 2048, 1408], P('dp', None, 'tensor')
- grad_expert_down: float32 [16, 2048, 1408], P('dp', None, 'tensor')
Inputs may be any that keep to these rules, and one draw needn't show every extreme that they name: `lengths`: each device's documents sum to 256 tokens and the longest is exactly 128. `routes`: a token names 6 different experts; among the tokens of one device no expert is named more than 128 times, a bound that some block reaches.
All inputs are finite; a program needn't handle non-finite values.
Results may differ from a plain program's by a relative error of at most 0.025.
Values may be sent and summed in bfloat16 or wider, within the bound.
A program may use at most 320 MiB of HBM per device.

v0:
```python
import jax
import jax.numpy as jnp
from jax import lax
from jax.sharding import PartitionSpec as P

PLAIN_HEAD_SIZE = 128
VALUE_HEAD_SIZE = 128
QK = 192
LATENT_RANK = 512
TOPK = 6


epsilon = 1e-06


def rms_normalize_pieces(values, gain):
    factor = lax.rsqrt(jnp.mean(values * values, axis=-1, keepdims=True) + epsilon)
    unit = values * factor
    return (unit * gain, unit, factor)


def normalize_back(grad, unit, factor, gain):
    inner = grad * gain
    return factor * (inner - unit * jnp.mean(inner * unit, axis=-1, keepdims=True))


def apply_rotation(values, token_position):
    half = values.shape[-1] // 2
    freqs = 10000.0 ** (-jnp.arange(half, dtype=jnp.float32) / half)
    angles = token_position.astype(jnp.float32)[:, None] * freqs[None, :]
    shape = (angles.shape[0],) + (1,) * (values.ndim - 2) + (half,)
    cosine = jnp.cos(angles).reshape(shape)
    sine = jnp.sin(angles).reshape(shape)
    first = values[..., :half]
    second = values[..., half:]
    return jnp.concatenate(
        [first * cosine - second * sine, second * cosine + first * sine], axis=-1
    )


def doc_layout(lengths_row, rows_here):
    ends = jnp.cumsum(lengths_row)
    starts = ends - lengths_row
    places = jnp.arange(rows_here, dtype=jnp.int32)
    segment = jnp.sum((places[:, None] >= ends[None, :]).astype(jnp.int32), axis=1)
    member = segment[:, None] == jnp.arange(lengths_row.shape[0], dtype=jnp.int32)[None, :]
    begins = jnp.sum(jnp.where(member, starts[None, :], 0), axis=1)
    return (segment, places - begins)


def contract_last(left, right, precision=None):
    return lax.dot_general(
        left,
        right,
        (((1,), (1,)), ((), ())),
        precision=precision,
        preferred_element_type=jnp.float32,
    )


def contract_first(left, right, precision=None):
    return lax.dot_general(
        left,
        right,
        (((0,), (0,)), ((), ())),
        precision=precision,
        preferred_element_type=jnp.float32,
    )


def swish_parts(gate_pre):
    sigma = jax.nn.sigmoid(gate_pre)
    return (gate_pre * sigma, sigma * (1.0 + gate_pre * (1.0 - sigma)))


def shards(
    tokens,
    lengths,
    routes,
    grad_out,
    g_attn,
    w_query,
    key_value_down_weight,
    latent_norm_gain,
    key_value_up_weight,
    w_out,
    g_ffn,
    router,
    shared_gate,
    shared_up,
    shared_down,
    expert_gate,
    expert_up,
    expert_down,
):
    rows_here = tokens.shape[0]
    features = tokens.shape[1]
    heads_local = w_out.shape[1] // VALUE_HEAD_SIZE
    devices = lax.axis_size("dp")
    capacity = rows_here * TOPK * 4 // (3 * devices)
    experts = router.shape[1]
    highest = lax.Precision.HIGHEST
    softmax_scale = QK ** (-0.5)
    segment, token_position = doc_layout(lengths[0], rows_here)
    places = jnp.arange(rows_here, dtype=jnp.int32)
    allowed = (segment[:, None] == segment[None, :]) & (places[None, :] <= places[:, None])
    tokens_f = tokens.astype(jnp.float32)
    attn_normed, attn_unit, attn_factor = rms_normalize_pieces(tokens_f, g_attn)
    normed_bf = attn_normed.astype(jnp.bfloat16)
    query_full = jnp.dot(normed_bf, w_query, preferred_element_type=jnp.float32).reshape(
        rows_here, heads_local, QK
    )
    query_bf = jnp.concatenate(
        [
            query_full[..., :PLAIN_HEAD_SIZE],
            apply_rotation(query_full[..., PLAIN_HEAD_SIZE:], token_position),
        ],
        axis=-1,
    ).astype(jnp.bfloat16)
    latent_with_key = jnp.dot(normed_bf, key_value_down_weight, preferred_element_type=jnp.float32)
    key_turned_part = apply_rotation(latent_with_key[:, LATENT_RANK:], token_position).astype(
        jnp.bfloat16
    )
    latent_after_norm, latent_unit_scale, latent_norm_factor = rms_normalize_pieces(
        latent_with_key[:, :LATENT_RANK], latent_norm_gain
    )
    latent_bf = latent_after_norm.astype(jnp.bfloat16)
    key_value = (
        jnp.dot(latent_bf, key_value_up_weight, preferred_element_type=jnp.float32)
        .astype(jnp.bfloat16)
        .reshape(rows_here, heads_local, PLAIN_HEAD_SIZE + VALUE_HEAD_SIZE)
    )
    key_nope = key_value[..., :PLAIN_HEAD_SIZE]
    value = key_value[..., PLAIN_HEAD_SIZE:]

    def masked_scores():
        raw = jnp.einsum(
            "thd,shd->hts",
            query_bf[..., :PLAIN_HEAD_SIZE],
            key_nope,
            preferred_element_type=jnp.float32,
        )
        raw = raw + jnp.einsum(
            "thd,sd->hts",
            query_bf[..., PLAIN_HEAD_SIZE:],
            key_turned_part,
            preferred_element_type=jnp.float32,
        )
        return jnp.where(allowed[None], raw * softmax_scale, -jnp.inf)

    scores = masked_scores()
    top_score = jnp.max(scores, axis=-1, keepdims=True)
    expo = jnp.exp(scores - top_score)
    total = jnp.sum(expo, axis=-1, keepdims=True)
    log_total = top_score + jnp.log(total)
    attn_weights = (expo / total).astype(jnp.bfloat16)
    context = jnp.einsum("hts,shd->thd", attn_weights, value, preferred_element_type=jnp.float32)
    context = context.astype(jnp.bfloat16).reshape(rows_here, heads_local * VALUE_HEAD_SIZE)
    attn = lax.psum(contract_last(context, w_out).astype(jnp.bfloat16), "tensor").astype(
        jnp.float32
    )
    hidden = tokens_f + attn
    ffn_normed, ffn_unit, ffn_factor = rms_normalize_pieces(hidden, g_ffn)
    ffn_bf = ffn_normed.astype(jnp.bfloat16)
    router_probs = jax.nn.softmax(jnp.dot(ffn_normed, router, precision=highest), axis=-1)
    expert_ids = jnp.arange(experts, dtype=jnp.int32)
    onehot_f = (routes[:, :, None] == expert_ids[None, None, :]).astype(jnp.float32)
    gates = jnp.sum(router_probs[:, None, :] * onehot_f, axis=2)
    flat_routes = routes.reshape(-1)
    onehot_i = (flat_routes[:, None] == expert_ids[None, :]).astype(jnp.int32)
    running = jnp.cumsum(onehot_i, axis=0)
    slot = jnp.sum(running * onehot_i, axis=1) - 1
    place = flat_routes * capacity + slot
    send_buffer = (
        jnp.zeros((experts * capacity, features), jnp.bfloat16)
        .at[place]
        .set(jnp.repeat(ffn_bf, TOPK, axis=0))
    )
    send_buffer = send_buffer.reshape(experts, capacity, features)
    received = lax.all_to_all(send_buffer, "dp", split_axis=0, concat_axis=0, tiled=True)
    expert_rows = received.reshape(devices * capacity, features)
    gate_pre = jnp.dot(expert_rows, expert_gate[0], preferred_element_type=jnp.float32)
    up_pre = jnp.dot(expert_rows, expert_up[0], preferred_element_type=jnp.float32)
    gate_act, gate_slope = swish_parts(gate_pre)
    expert_hidden = (gate_act * up_pre).astype(jnp.bfloat16)
    expert_result = contract_last(expert_hidden, expert_down[0])
    shared_pre_gate = jnp.dot(ffn_bf, shared_gate, preferred_element_type=jnp.float32)
    shared_pre_up = jnp.dot(ffn_bf, shared_up, preferred_element_type=jnp.float32)
    shared_act, shared_slope = swish_parts(shared_pre_gate)
    shared_hidden = (shared_act * shared_pre_up).astype(jnp.bfloat16)
    shared_result = contract_last(shared_hidden, shared_down)
    grad_top = grad_out.astype(jnp.float32)
    returned = lax.all_to_all(
        expert_result.reshape(devices, capacity, features).astype(jnp.bfloat16),
        "dp",
        split_axis=0,
        concat_axis=0,
        tiled=True,
    ).astype(jnp.float32)
    pair_result = jnp.take(returned.reshape(-1, features), place, axis=0).reshape(
        rows_here, TOPK, features
    )
    routed = jnp.sum(gates[:, :, None] * pair_result, axis=1)
    ffn_total = lax.psum((routed + shared_result).astype(jnp.bfloat16), "tensor").astype(
        jnp.float32
    )
    output = (hidden + ffn_total).astype(jnp.bfloat16)
    grad_shared_down = contract_first(grad_out, shared_hidden)
    grad_shared_hidden = jnp.dot(grad_out, shared_down, preferred_element_type=jnp.float32)
    grad_shared_gate_pre = (grad_shared_hidden * shared_pre_up * shared_slope).astype(jnp.bfloat16)
    grad_shared_up_pre = (grad_shared_hidden * shared_act).astype(jnp.bfloat16)
    grad_shared_gate = contract_first(ffn_bf, grad_shared_gate_pre)
    grad_shared_up = contract_first(ffn_bf, grad_shared_up_pre)
    grad_ffn_in = contract_last(grad_shared_gate_pre, shared_gate) + contract_last(
        grad_shared_up_pre, shared_up
    )
    grad_gates = jnp.sum(grad_top[:, None, :] * pair_result, axis=-1)
    dense_grad = jnp.sum(onehot_f * grad_gates[:, :, None], axis=1)
    grad_logits = router_probs * (
        dense_grad - jnp.sum(router_probs * dense_grad, axis=-1, keepdims=True)
    )
    grad_router_in = contract_last(grad_logits, router, highest)
    grad_router_part = contract_first(ffn_normed, grad_logits, highest)
    pair_grad = (
        (gates[:, :, None] * grad_top[:, None, :])
        .astype(jnp.bfloat16)
        .reshape(rows_here * TOPK, features)
    )
    grad_buffer = jnp.zeros((experts * capacity, features), jnp.bfloat16).at[place].set(pair_grad)
    grad_buffer = grad_buffer.reshape(experts, capacity, features)
    grad_received = lax.all_to_all(grad_buffer, "dp", split_axis=0, concat_axis=0, tiled=True)
    grad_rows = grad_received.reshape(devices * capacity, features)
    grad_expert_down = contract_first(grad_rows, expert_hidden)[None]
    grad_expert_hidden = jnp.dot(grad_rows, expert_down[0], preferred_element_type=jnp.float32)
    grad_gate_pre = (grad_expert_hidden * up_pre * gate_slope).astype(jnp.bfloat16)
    grad_up_pre = (grad_expert_hidden * gate_act).astype(jnp.bfloat16)
    grad_expert_gate = contract_first(expert_rows, grad_gate_pre)[None]
    grad_expert_up = contract_first(expert_rows, grad_up_pre)[None]
    grad_rows_in = contract_last(grad_gate_pre, expert_gate[0]) + contract_last(
        grad_up_pre, expert_up[0]
    )
    grad_back = lax.all_to_all(
        grad_rows_in.reshape(devices, capacity, features).astype(jnp.bfloat16),
        "dp",
        split_axis=0,
        concat_axis=0,
        tiled=True,
    ).astype(jnp.float32)
    grad_routed = jnp.sum(
        jnp.take(grad_back.reshape(-1, features), place, axis=0).reshape(rows_here, TOPK, features),
        axis=1,
    )
    grad_ffn_total = lax.psum(
        (grad_ffn_in + grad_routed + grad_router_in).astype(jnp.bfloat16), "tensor"
    ).astype(jnp.float32)
    grad_g_ffn = jnp.sum(grad_ffn_total * ffn_unit, axis=0)
    grad_hidden = grad_top + normalize_back(grad_ffn_total, ffn_unit, ffn_factor, g_ffn)
    grad_hidden_bf = grad_hidden.astype(jnp.bfloat16)
    grad_w_out = contract_first(grad_hidden_bf, context)
    grad_context = jnp.dot(grad_hidden_bf, w_out, preferred_element_type=jnp.float32).astype(
        jnp.bfloat16
    )
    grad_context = grad_context.reshape(rows_here, heads_local, VALUE_HEAD_SIZE)
    redone = jnp.exp(masked_scores() - log_total)
    redone_bf = redone.astype(jnp.bfloat16)
    grad_weights = jnp.einsum(
        "thd,shd->hts", grad_context, value, preferred_element_type=jnp.float32
    )
    grad_value = jnp.einsum(
        "hts,thd->shd", redone_bf, grad_context, preferred_element_type=jnp.float32
    )
    row_inner = jnp.sum(redone * grad_weights, axis=-1, keepdims=True)
    grad_raw = (redone * (grad_weights - row_inner) * softmax_scale).astype(jnp.bfloat16)
    grad_query_nope = jnp.einsum(
        "hts,shd->thd", grad_raw, key_nope, preferred_element_type=jnp.float32
    )
    grad_query_rot = jnp.einsum(
        "hts,sd->thd", grad_raw, key_turned_part, preferred_element_type=jnp.float32
    )
    grad_key_nope = jnp.einsum(
        "hts,thd->shd",
        grad_raw,
        query_bf[..., :PLAIN_HEAD_SIZE],
        preferred_element_type=jnp.float32,
    )
    grad_key_rot = jnp.einsum(
        "hts,thd->sd", grad_raw, query_bf[..., PLAIN_HEAD_SIZE:], preferred_element_type=jnp.float32
    )
    grad_query = jnp.concatenate(
        [grad_query_nope, apply_rotation(grad_query_rot, -token_position)], axis=-1
    )
    grad_query = grad_query.reshape(rows_here, heads_local * QK).astype(jnp.bfloat16)
    grad_w_query = contract_first(normed_bf, grad_query)
    grad_in_query = contract_last(grad_query, w_query)
    grad_key_value = (
        jnp.concatenate([grad_key_nope, grad_value], axis=-1)
        .reshape(rows_here, heads_local * (PLAIN_HEAD_SIZE + VALUE_HEAD_SIZE))
        .astype(jnp.bfloat16)
    )
    grad_w_kv_up = contract_first(latent_bf, grad_key_value)
    grad_latent_normed = contract_last(grad_key_value, key_value_up_weight)
    grad_g_kv_part = jnp.sum(grad_latent_normed * latent_unit_scale, axis=0)
    grad_latent = normalize_back(
        grad_latent_normed, latent_unit_scale, latent_norm_factor, latent_norm_gain
    )
    grad_down_part = jnp.concatenate(
        [grad_latent, apply_rotation(grad_key_rot, -token_position)], axis=1
    )
    grad_in_summed, grad_down = (
        lax.psum(grad_in_query.astype(jnp.bfloat16), "tensor").astype(jnp.float32),
        lax.psum(grad_down_part.astype(jnp.bfloat16), "tensor").astype(jnp.float32),
    )
    grad_down_bf = grad_down.astype(jnp.bfloat16)
    share = grad_down.shape[1] // lax.axis_size("tensor")
    grad_columns = lax.dynamic_slice_in_dim(
        grad_down_bf, lax.axis_index("tensor") * share, share, 1
    )
    grad_w_kv_down = contract_first(normed_bf, grad_columns)
    grad_attn_in = grad_in_summed + contract_last(grad_down_bf, key_value_down_weight)
    grad_g_attn = jnp.sum(grad_attn_in * attn_unit, axis=0)
    grad_tokens = grad_hidden + normalize_back(grad_attn_in, attn_unit, attn_factor, g_attn)
    summed = (
        lax.psum_scatter(
            grad_w_query.astype(jnp.bfloat16), "dp", scatter_dimension=0, tiled=True
        ).astype(jnp.float32),
        lax.psum_scatter(
            grad_w_kv_down.astype(jnp.bfloat16), "dp", scatter_dimension=0, tiled=True
        ).astype(jnp.float32),
        lax.psum_scatter(
            grad_w_kv_up.astype(jnp.bfloat16), "dp", scatter_dimension=0, tiled=True
        ).astype(jnp.float32),
        lax.psum_scatter(
            grad_w_out.astype(jnp.bfloat16), "dp", scatter_dimension=0, tiled=True
        ).astype(jnp.float32),
        lax.psum_scatter(
            grad_shared_gate.astype(jnp.bfloat16), "dp", scatter_dimension=0, tiled=True
        ).astype(jnp.float32),
        lax.psum_scatter(
            grad_shared_up.astype(jnp.bfloat16), "dp", scatter_dimension=0, tiled=True
        ).astype(jnp.float32),
        lax.psum_scatter(
            grad_shared_down.astype(jnp.bfloat16), "dp", scatter_dimension=0, tiled=True
        ).astype(jnp.float32),
        lax.psum_scatter(
            grad_g_attn.astype(jnp.bfloat16), "dp", scatter_dimension=0, tiled=True
        ).astype(jnp.float32),
        lax.psum_scatter(
            grad_g_ffn.astype(jnp.bfloat16), "dp", scatter_dimension=0, tiled=True
        ).astype(jnp.float32),
    )
    everywhere = (
        lax.psum_scatter(grad_router_part, ("dp", "tensor"), scatter_dimension=0, tiled=True),
        lax.psum_scatter(grad_g_kv_part, ("dp", "tensor"), scatter_dimension=0, tiled=True),
    )
    return (
        output,
        grad_tokens,
        summed[7],
        summed[0],
        summed[1],
        everywhere[1],
        summed[2],
        summed[3],
        summed[8],
        everywhere[0],
        summed[4],
        summed[5],
        summed[6],
        grad_expert_gate,
        grad_expert_up,
        grad_expert_down,
    )


def solution(mesh):
    in_specs = (
        P("dp", None),
        P("dp", None),
        P("dp", None),
        P("dp", None),
        P(),
        P(None, "tensor"),
        P(),
        P(),
        P(None, "tensor"),
        P(None, "tensor"),
        P(),
        P(),
        P(None, "tensor"),
        P(None, "tensor"),
        P(None, "tensor"),
        P("dp", None, "tensor"),
        P("dp", None, "tensor"),
        P("dp", None, "tensor"),
    )
    out_specs = (
        P("dp", None),
        P("dp", None),
        P("dp"),
        P("dp", "tensor"),
        P("dp", "tensor"),
        P(("dp", "tensor")),
        P("dp", "tensor"),
        P("dp", "tensor"),
        P("dp"),
        P(("dp", "tensor"), None),
        P("dp", "tensor"),
        P("dp", "tensor"),
        P("dp", "tensor"),
        P("dp", None, "tensor"),
        P("dp", None, "tensor"),
        P("dp", None, "tensor"),
    )
    return jax.shard_map(shards, mesh=mesh, in_specs=in_specs, out_specs=out_specs, check_vma=False)
```

profile of v0, /device:TPU:0, one launch (start us, length us, event | category | flops | bytes accessed | tf_op | source)
XLA Modules:
  0.0 1902.0 jit_solution(4956213607235852434)
XLA Ops:
  39.6 36.5 %all-reduce.9.cloned.1.call-done = bf16[256,2048]{1,0:T(8,128)(2,1)} async-done(((bf16[256,2048]{1,0:T(8,128)(2,1)}), bf16[256,2048]{1,0:T(8,128)(2,1)}) %all-reduce.9.cloned.1.call-update) | async-done | bytes 1048592 | tf_op jit(solution)/shard_map/psum | solution.py:159
  85.7 11.1 reshape.414
  96.7 15.1 scatter_custom_fusion
  111.8 188.5 %all_to_all.20 = bf16[16,128,2048]{2,1,0:T(8,128)(2,1)S(1)} all-to-all(bf16[16,128,2048]{2,1,0:T(8,128)(2,1)} %bitcast.152), channel_id=1, replica_groups=mesh['dp'=16,'tensor'=2] {'dp'}, dimensions={0} | all-to-all | bytes 16777216 | tf_op jit(solution)/shard_map/all_to_all | solution.py:180
  340.6 15.7 mul.458
  360.0 122.2 %all-to-all-done.1 = bf16[16,128,2048]{2,1,0:T(8,128)(2,1)} async-done(((bf16[16,128,2048]{2,1,0:T(8,128)(2,1)}), bf16[16,128,2048]{2,1,0:T(8,128)(2,1)}, u32[]{:S(2)}, u32[]{:S(2)}) %all-to-all-start.1) | async-done | bytes 8388640 | tf_op jit(solution)/shard_map/all_to_all | solution.py:193
  482.2 11.3 bitcast_convert_fusion.1
  493.4 18.3 gather_fusion
  511.7 14.0 multiply_reduce_fusion.1
  526.3 16.5 scatter_custom_fusion.1
  542.8 218.6 %all_to_all.21 = bf16[16,128,2048]{2,1,0:T(8,128)(2,1)S(1)} all-to-all(bf16[16,128,2048]{2,1,0:T(8,128)(2,1)} %bitcast.151), channel_id=1, replica_groups=mesh['dp'=16,'tensor'=2] {'dp'}, dimensions={0} | all-to-all | bytes 16777216 | tf_op jit(solution)/shard_map/all_to_all | solution.py:231
  761.4 14.1 multiply_convert_fusion.2
  775.6 10.3 fusion.20
  785.9 12.6 add_convert_fusion
  820.2 15.0 reshape.383
  835.2 119.9 %all-to-all-done.3 = bf16[16,128,2048]{2,1,0:T(8,128)(2,1)} async-done(((bf16[16,128,2048]{2,1,0:T(8,128)(2,1)}), bf16[16,128,2048]{2,1,0:T(8,128)(2,1)}, u32[]{:S(2)}, u32[]{:S(2)}) %all-to-all-start.3) | async-done | bytes 8388640 | tf_op jit(solution)/shard_map/all_to_all | solution.py:242
  955.1 11.2 bitcast_convert_fusion
  966.3 18.3 gather_fusion.1
  994.5 15.0 reshape.388
  1043.6 55.5 %all-reduce.11.cloned.1.call-done = bf16[256,2048]{1,0:T(8,128)(2,1)} async-done(((bf16[256,2048]{1,0:T(8,128)(2,1)}), bf16[256,2048]{1,0:T(8,128)(2,1)}) %all-reduce.11.cloned.1.call-update) | async-done | bytes 1048592 | tf_op jit(solution)/shard_map/psum | solution.py:253
  1175.9 35.6 %all-reduce.13.cloned.1.call-done = (bf16[256,2048]{1,0:T(8,128)(2,1)}, bf16[256,576]{0,1:T(8,128)(2,1)}, bf16[256,2048]{1,0:T(8,128)(2,1)}) async-done(((bf16[256,2048]{1,0:T(8,128)(2,1)}, bf16[256,576]{0,1:T(8,128)(2,1)}, bf16[256,2048]{1,0:T(8,128)(2,1)}), (bf16[256,2048]{1,0:T(8,128)(2,1)}, bf16[256,576]{0,1:T(8,128)(2,1)}, bf16[256,2048]{1,0:T(8,128)(2,1)})) %all-reduce.13.cloned.1.call-update) | async-done | bytes 2392080 | tf_op jit(solution)/shard_map/psum | solution.py:204
  1230.4 67.1 %reduce-scatter.29.cloned.1.call-done = bf16[128,1408]{1,0:T(8,128)(2,1)} async-done(((bf16[2048,1408]{1,0:T(8,128)(2,1)}), bf16[128,1408]{1,0:T(8,128)(2,1)}) %reduce-scatter.29.cloned.1.call-update) | async-done | bytes 360464
  1299.7 82.8 %reduce-scatter.21.cloned.1.call-done = bf16[128,1408]{1,0:T(8,128)(2,1)} async-done(((bf16[2048,1408]{1,0:T(8,128)(2,1)}), bf16[128,1408]{1,0:T(8,128)(2,1)}) %reduce-scatter.21.cloned.1.call-update) | async-done | bytes 360464 | tf_op jit(solution)/shard_map/reduce_scatter | solution.py:335
  1384.4 83.2 %reduce-scatter.23.cloned.1.call-done = bf16[128,1408]{1,0:T(8,128)(2,1)} async-done(((bf16[2048,1408]{1,0:T(8,128)(2,1)}), bf16[128,1408]{1,0:T(8,128)(2,1)}) %reduce-scatter.23.cloned.1.call-update) | async-done | bytes 360464 | tf_op jit(solution)/shard_map/reduce_scatter | solution.py:338
  1469.5 134.8 %reduce-scatter.27.cloned.1.call-done = f32[64,16]{1,0:T(8,128)} async-done(((f32[2048,16]{1,0:T(8,128)}), f32[64,16]{1,0:T(8,128)}) %reduce-scatter.27.cloned.1.call-update) | async-done | bytes 4112
  1605.7 11.1 convolution_bitcast_fusion.2
  1616.8 10.3 convolution_bitcast_fusion.1
  1635.1 37.5 %all-reduce.1 = f32[512]{0:T(512)S(1)} all-reduce(f32[512]{0:T(512)S(1)} %get-tuple-element.101), channel_id=5, replica_groups=mesh['dp'=16,'tensor'=2] {'dp','tensor'}, use_global_device_ids=true, to_apply=%region_35.37.clone | all-reduce | flops 512 | bytes 4096
  1677.5 31.5 %all-reduce.3 = (bf16[2048]{0:T(1024)(128)(2,1)S(1)}, bf16[2048]{0:T(1024)(128)(2,1)S(1)}) all-reduce(bf16[2048]{0:T(1024)(128)(2,1)S(1)} %get-tuple-element.99, bf16[2048]{0:T(1024)(128)(2,1)S(1)} %get-tuple-element.97), channel_id=2, replica_groups=mesh['dp'=16,'tensor'=2] {'dp'}, use_global_device_ids=true, to_apply=%region_31.33.clone | all-reduce | flops 4096 | bytes 16384
  1717.9 11.5 reduce-scatter.25.cloned.1.call-done
  1731.0 74.0 %reduce-scatter.19.cloned.1.call-done = bf16[128,1024]{1,0:T(8,128)(2,1)} async-done(((bf16[2048,1024]{1,0:T(8,128)(2,1)}), bf16[128,1024]{1,0:T(8,128)(2,1)}) %reduce-scatter.19.cloned.1.call-update) | async-done | bytes 262160 | tf_op jit(solution)/shard_map/reduce_scatter | solution.py:332
  1806.8 86.4 %reduce-scatter.15.cloned.1.call-done = bf16[128,1536]{1,0:T(8,128)(2,1)} async-done(((bf16[2048,1536]{1,0:T(8,128)(2,1)}), bf16[128,1536]{1,0:T(8,128)(2,1)}) %reduce-scatter.15.cloned.1.call-update) | async-done | bytes 393232 | tf_op jit(solution)/shard_map/reduce_scatter | solution.py:323
  (318 shorter events, 280.6 us)
Async XLA Ops:
  7.2 309.4 %copy-start = (bf16[1,2048,704]{1,2,0:T(8,128)(2,1)S(1)}, bf16[1,2048,704]{1,2,0:T(8,128)(2,1)}, u32[]{:S(2)}) copy-start(bf16[1,2048,704]{1,2,0:T(8,128)(2,1)} %param.37) | copy-start | bytes 8650756
  7.2 68.9 %all-reduce.9.cloned.1.call-start = ((), (), s32[]{:S(2)}) async-start(), calls=%async_computation.12 | async-start | bytes 2097152 | tf_op jit(solution)/shard_map/psum | solution.py:159
  7.3 17.2 copy-start.65
  33.2 45.0 %copy-start.43 = (f32[2048]{0:T(1024)S(1)}, f32[2048]{0:T(1024)}, u32[]{:S(2)}) copy-start(f32[2048]{0:T(1024)} %param.30) | copy-start | bytes 24580
  78.3 278.1 %copy-start.60 = (f32[256]{0:T(256)}, f32[256]{0:T(256)S(1)}, u32[]{:S(2)}) copy-start(f32[256]{0:T(256)S(1)} %add_rsqrt_fusion) | copy-start | bytes 3076
  111.8 188.6 %copy-start.68 = (bf16[1,2048,704]{1,2,0:T(8,128)(2,1)S(1)}, bf16[1,2048,704]{1,2,0:T(8,128)(2,1)}, u32[]{:S(2)}) copy-start(bf16[1,2048,704]{1,2,0:T(8,128)(2,1)} %param.35) | copy-start | bytes 8650756
  325.6 156.6 %all-to-all-start.1 = ((bf16[16,128,2048]{2,1,0:T(8,128)(2,1)}), bf16[16,128,2048]{2,1,0:T(8,128)(2,1)}, u32[]{:S(2)}, u32[]{:S(2)}) async-start(bf16[16,128,2048]{2,1,0:T(8,128)(2,1)} %convolution_convert_fusion.4), calls=%async_computation.1 | async-start | bytes 16777216 | tf_op jit(solution)/shard_map/all_to_all | solution.py:193
  340.6 15.8 copy-start.45
  360.0 166.0 %copy-start.41 = (f32[256,16]{0,1:T(8,128)}, f32[256,16]{0,1:T(8,128)S(1)}, u32[]{:S(2)}) copy-start(f32[256,16]{0,1:T(8,128)S(1)} %fusion.110) | copy-start | bytes 49156
  526.1 16.7 copy-start.28
  798.5 156.6 %all-to-all-start.3 = ((bf16[16,128,2048]{2,1,0:T(8,128)(2,1)}), bf16[16,128,2048]{2,1,0:T(8,128)(2,1)}, u32[]{:S(2)}, u32[]{:S(2)}) async-start(bf16[16,128,2048]{2,1,0:T(8,128)(2,1)} %bitcast.161), calls=%async_computation.3 | async-start | bytes 16777216 | tf_op jit(solution)/shard_map/all_to_all | solution.py:242
  804.4 294.7 %all-reduce.11.cloned.1.call-start = ((), (), s32[]{:S(2)}) async-start(), calls=%async_computation.13 | async-start | bytes 2097152 | tf_op jit(solution)/shard_map/psum | solution.py:253
  817.0 202.4 %copy-start.19 = (bf16[256,1408]{1,0:T(8,128)(2,1)}, bf16[256,1408]{1,0:T(8,128)(2,1)S(1)}, u32[]{:S(2)}) copy-start(bf16[256,1408]{1,0:T(8,128)(2,1)S(1)} %get-tuple-element.116) | copy-start | bytes 2162692
  1028.0 183.5 %all-reduce.13.cloned.1.call-start = ((), (), s32[]{:S(2)}) async-start(), calls=%async_computation.22 | async-start | bytes 4784128 | tf_op jit(solution)/shard_map/psum | solution.py:204
  1037.9 61.2 %copy-start.3 = (bf16[256,2048]{1,0:T(8,128)(2,1)S(1)}, bf16[256,2048]{1,0:T(8,128)(2,1)}, u32[]{:S(2)}) copy-start(bf16[256,2048]{1,0:T(8,128)(2,1)} %param.20) | copy-start | bytes 3145732
  1037.9 61.2 %copy-start.5 = (bf16[256,2048]{1,0:T(8,128)(2,1)S(1)}, bf16[256,2048]{1,0:T(8,128)(2,1)}, u32[]{:S(2)}) copy-start(bf16[256,2048]{1,0:T(8,128)(2,1)} %all-reduce.9.cloned.1.call-done) | copy-start | bytes 3145732
  1037.9 61.1 %copy-start.44 = (f32[2048]{0:T(1024)S(1)}, f32[2048]{0:T(1024)}, u32[]{:S(2)}) copy-start(f32[2048]{0:T(1024)} %param.30) | copy-start | bytes 24580
  1038.0 61.1 %copy-start.61 = (f32[256]{0:T(256)S(1)}, f32[256]{0:T(256)}, u32[]{:S(2)}) copy-start(f32[256]{0:T(256)} %copy-done.60) | copy-start | bytes 3076
  1141.7 155.8 %reduce-scatter.29.cloned.1.call-start = ((), (), s32[]{:S(2)}) async-start(), calls=%async_computation.21 | async-start | bytes 6127616
  1156.1 226.4 %reduce-scatter.21.cloned.1.call-start = ((), (), s32[]{:S(2)}) async-start(), calls=%async_computation.17 | async-start | bytes 6127616 | tf_op jit(solution)/shard_map/reduce_scatter | solution.py:335
  1162.0 305.6 %reduce-scatter.23.cloned.1.call-start = ((), (), s32[]{:S(2)}) async-start(), calls=%async_computation.18 | async-start | bytes 6127616 | tf_op jit(solution)/shard_map/reduce_scatter | solution.py:338
  1167.9 436.4 %reduce-scatter.27.cloned.1.call-start = ((), (), s32[]{:S(2)}) async-start(), calls=%async_computation.20 | async-start | bytes 1081344
  1172.4 39.1 %copy-start.40 = (f32[2048]{0:T(1024)S(1)}, f32[2048]{0:T(1024)}, u32[]{:S(2)}) copy-start(f32[2048]{0:T(1024)} %param.24) | copy-start | bytes 24580
  1172.4 39.1 %copy-start.55 = (f32[256]{0:T(256)S(1)}, f32[256]{0:T(256)}, u32[]{:S(2)}) copy-start(f32[256]{0:T(256)} %copy-done.54) | copy-start | bytes 3076
  1172.4 543.8 %reduce-scatter.17.cloned.1.call-start = ((), (), s32[]{:S(2)}) async-start(), calls=%async_computation.15 | async-start | bytes 2228224 | tf_op jit(solution)/shard_map/reduce_scatter | solution.py:329
  1175.9 553.5 %reduce-scatter.25.cloned.1.call-start = ((), (), s32[]{:S(2)}) async-start(), calls=%async_computation.19 | async-start | bytes 1671168
  1216.7 588.3 %reduce-scatter.19.cloned.1.call-start = ((), (), s32[]{:S(2)}) async-start(), calls=%async_computation.16 | async-start | bytes 4456448 | tf_op jit(solution)/shard_map/reduce_scatter | solution.py:332
  1222.7 670.5 %reduce-scatter.15.cloned.1.call-start = ((), (), s32[]{:S(2)}) async-start(), calls=%async_computation.14 | async-start | bytes 6684672 | tf_op jit(solution)/shard_map/reduce_scatter | solution.py:323
  1605.7 21.5 %slice-start = ((s8[8388608]{0:T(1024)(128)(4,1)}), s8[4194304]{0:T(1024)(128)(4,1)S(1)}, s32[]{:S(2)}) async-start(s8[8388608]{0:T(1024)(128)(4,1)} %bitcast.158), calls=%async_computation.23 | async-start | bytes 8388608
  1627.2 46.0 %copy-start.30 = (bf16[256,2048]{1,0:T(8,128)(2,1)S(1)}, bf16[256,2048]{1,0:T(8,128)(2,1)}, u32[]{:S(2)}) copy-start(bf16[256,2048]{1,0:T(8,128)(2,1)} %get-tuple-element.109) | copy-start | bytes 3145732
  1627.2 46.0 %copy-start.38 = (bf16[256,576]{0,1:T(8,128)(2,1)S(1)}, bf16[256,576]{0,1:T(8,128)(2,1)}, u32[]{:S(2)}) copy-start(bf16[256,576]{0,1:T(8,128)(2,1)} %get-tuple-element.108) | copy-start | bytes 884740
  1709.7 185.5 %copy-start.1 = (bf16[1,2048,704]{1,2,0:T(8,128)(2,1)S(1)}, bf16[1,2048,704]{1,2,0:T(8,128)(2,1)}, u32[]{:S(2)}) copy-start(bf16[1,2048,704]{1,2,0:T(8,128)(2,1)} %param.37) | copy-start | bytes 8650756
  (69 other events, 322.6 us)
Sparse Core Ops, SparseCore 0:
  33.3 42.7 all-reduce.8
  1028.1 70.9 all-reduce.10
  1141.8 69.6 all-reduce.12
  1215.9 81.5 reduce-scatter.28
  1301.8 80.6 reduce-scatter.20
  1386.8 80.6 reduce-scatter.22
  1470.4 133.8 reduce-scatter.26
  1608.5 58.3 reduce-scatter.16
  1670.6 58.6 reduce-scatter.24
  1733.5 71.4 reduce-scatter.18
  1808.9 84.2 reduce-scatter.14
where the time goes:
time: 1910 us; the launch traced here: 1900 us
  waiting for transfers between devices  910 us (48%)
  blocking collectives  476 us (25%)
  matrix products  216 us (11%)
  local copies, waits for them, and re-layouts  154 us (8%)
  other arithmetic  118 us (6%)
    all_to_all x1, blocking collectives, shards(): lax.all_to_all(grad_buffer, 'dp', split_axis=0, concat_axis=0, tiled=True)  219 us
    unnamed x14, waiting for transfers between devices  214 us
    all_to_all x1, blocking collectives, shards(): lax.all_to_all(send_buffer, 'dp', split_axis=0, concat_axis=0, tiled=True)  189 us
    all_to_all x1, waiting for transfers between devices, shards(): lax.all_to_all(expert_result.reshape(devices, capacity, features).astype(...  122 us
    all_to_all x1, waiting for transfers between devices, shards(): lax.all_to_all(grad_rows_in.reshape(devices, capacity, features).astype(j...  120 us
    reduce_scatter x1, waiting for transfers between devices, shards(): lax.psum_scatter(grad_w_query.astype(jnp.bfloat16), 'dp', scatter_dimensi...  86.4 us
    reduce_scatter x1, waiting for transfers between devices, shards(): lax.psum_scatter(grad_shared_up.astype(jnp.bfloat16), 'dp', scatter_dimen...  83.2 us
    reduce_scatter x1, waiting for transfers between devices, shards(): lax.psum_scatter(grad_shared_gate.astype(jnp.bfloat16), 'dp', scatter_dim...  82.8 us
  transfers between devices with their start and end apart: 13, of which 12 were waited for; matrix products, arithmetic and copies ran while one was open for 10% of the time, Pallas kernels for 0%

commit v1 on v0

--- a/solution.py
+++ b/solution.py
@@ -163,73 +163,59 @@
     ffn_normed, ffn_unit, ffn_factor = rms_normalize_pieces(hidden, g_ffn)
     ffn_bf = ffn_normed.astype(jnp.bfloat16)
     router_probs = jax.nn.softmax(jnp.dot(ffn_normed, router, precision=highest), axis=-1)
-    expert_ids = jnp.arange(experts, dtype=jnp.int32)
-    onehot_f = (routes[:, :, None] == expert_ids[None, None, :]).astype(jnp.float32)
-    gates = jnp.sum(router_probs[:, None, :] * onehot_f, axis=2)
-    flat_routes = routes.reshape(-1)
-    onehot_i = (flat_routes[:, None] == expert_ids[None, :]).astype(jnp.int32)
-    running = jnp.cumsum(onehot_i, axis=0)
-    slot = jnp.sum(running * onehot_i, axis=1) - 1
-    place = flat_routes * capacity + slot
-    send_buffer = (
-        jnp.zeros((experts * capacity, features), jnp.bfloat16)
-        .at[place]
-        .set(jnp.repeat(ffn_bf, TOPK, axis=0))
-    )
-    send_buffer = send_buffer.reshape(experts, capacity, features)
-    received = lax.all_to_all(send_buffer, "dp", split_axis=0, concat_axis=0, tiled=True)
-    expert_rows = received.reshape(devices * capacity, features)
+    own = lax.axis_index("dp")
+
+    everyone_grad = lax.all_gather(grad_out, "dp", tiled=True)
+    everyone_routes = lax.all_gather(routes, "dp", tiled=True)
+    everyone_ffn = lax.all_gather(ffn_bf, "dp", tiled=True)
+    everyone_probs = lax.all_gather(router_probs, "dp", tiled=True)
+    chooses = jnp.any(everyone_routes == own, axis=1).reshape(devices, rows_here)
+    own_probs = lax.dynamic_slice_in_dim(everyone_probs, own, 1, 1).reshape(devices, rows_here)
+    own_gates = jnp.where(chooses, own_probs, 0.0)
+    upto = (places[:, None] <= places[None, :]).astype(jnp.bfloat16)
+    slot = jnp.dot(chooses.astype(jnp.bfloat16), upto, preferred_element_type=jnp.float32) - 1.0
+    slots = jnp.arange(capacity, dtype=jnp.float32)
+    picked = chooses[:, None, :] & (slot[:, None, :] == slots[None, :, None])
+    pick = picked.astype(jnp.bfloat16)
+    slot_gates = jnp.sum(jnp.where(picked, own_gates[:, None, :], 0.0), axis=2).reshape(-1, 1)
+
+    def pick_rows(values):
+        blocks = values.reshape(devices, rows_here, features)
+        return jnp.einsum(
+            "jst,jtc->jsc", pick, blocks, preferred_element_type=jnp.float32
+        ).astype(jnp.bfloat16).reshape(devices * capacity, features)
+
+    def put_rows(values, hidden_parts, weights):
+        blocks = values.astype(jnp.bfloat16).reshape(devices, capacity, features)
+        left = jnp.concatenate(
+            [pick.transpose(0, 2, 1)]
+            + [h.reshape(devices, rows_here, h.shape[1]) for h in hidden_parts],
+            axis=2,
+        )
+        right = jnp.concatenate(
+            [blocks]
+            + [
+                jnp.broadcast_to(w.T[None], (devices, w.shape[1], features))
+                for w in weights
+            ],
+            axis=1,
+        )
+        return (
+            jnp.einsum("jtk,jkc->jtc", left, right, preferred_element_type=jnp.float32)
+            .astype(jnp.bfloat16)
+            .reshape(devices * rows_here, features)
+        )
+
+    expert_rows = pick_rows(everyone_ffn)
+    grad_picked = pick_rows(everyone_grad)
+    grad_rows = (slot_gates * grad_picked.astype(jnp.float32)).astype(jnp.bfloat16)
+
     gate_pre = jnp.dot(expert_rows, expert_gate[0], preferred_element_type=jnp.float32)
     up_pre = jnp.dot(expert_rows, expert_up[0], preferred_element_type=jnp.float32)
     gate_act, gate_slope = swish_parts(gate_pre)
     expert_hidden = (gate_act * up_pre).astype(jnp.bfloat16)
     expert_result = contract_last(expert_hidden, expert_down[0])
-    shared_pre_gate = jnp.dot(ffn_bf, shared_gate, preferred_element_type=jnp.float32)
-    shared_pre_up = jnp.dot(ffn_bf, shared_up, preferred_element_type=jnp.float32)
-    shared_act, shared_slope = swish_parts(shared_pre_gate)
-    shared_hidden = (shared_act * shared_pre_up).astype(jnp.bfloat16)
-    shared_result = contract_last(shared_hidden, shared_down)
-    grad_top = grad_out.astype(jnp.float32)
-    returned = lax.all_to_all(
-        expert_result.reshape(devices, capacity, features).astype(jnp.bfloat16),
-        "dp",
-        split_axis=0,
-        concat_axis=0,
-        tiled=True,
-    ).astype(jnp.float32)
-    pair_result = jnp.take(returned.reshape(-1, features), place, axis=0).reshape(
-        rows_here, TOPK, features
-    )
-    routed = jnp.sum(gates[:, :, None] * pair_result, axis=1)
-    ffn_total = lax.psum((routed + shared_result).astype(jnp.bfloat16), "tensor").astype(
-        jnp.float32
-    )
-    output = (hidden + ffn_total).astype(jnp.bfloat16)
-    grad_shared_down = contract_first(grad_out, shared_hidden)
-    grad_shared_hidden = jnp.dot(grad_out, shared_down, preferred_element_type=jnp.float32)
-    grad_shared_gate_pre = (grad_shared_hidden * shared_pre_up * shared_slope).astype(jnp.bfloat16)
-    grad_shared_up_pre = (grad_shared_hidden * shared_act).astype(jnp.bfloat16)
-    grad_shared_gate = contract_first(ffn_bf, grad_shared_gate_pre)
-    grad_shared_up = contract_first(ffn_bf, grad_shared_up_pre)
-    grad_ffn_in = contract_last(grad_shared_gate_pre, shared_gate) + contract_last(
-        grad_shared_up_pre, shared_up
-    )
-    grad_gates = jnp.sum(grad_top[:, None, :] * pair_result, axis=-1)
-    dense_grad = jnp.sum(onehot_f * grad_gates[:, :, None], axis=1)
-    grad_logits = router_probs * (
-        dense_grad - jnp.sum(router_probs * dense_grad, axis=-1, keepdims=True)
-    )
-    grad_router_in = contract_last(grad_logits, router, highest)
-    grad_router_part = contract_first(ffn_normed, grad_logits, highest)
-    pair_grad = (
-        (gates[:, :, None] * grad_top[:, None, :])
-        .astype(jnp.bfloat16)
-        .reshape(rows_here * TOPK, features)
-    )
-    grad_buffer = jnp.zeros((experts * capacity, features), jnp.bfloat16).at[place].set(pair_grad)
-    grad_buffer = grad_buffer.reshape(experts, capacity, features)
-    grad_received = lax.all_to_all(grad_buffer, "dp", split_axis=0, concat_axis=0, tiled=True)
-    grad_rows = grad_received.reshape(devices * capacity, features)
+    slot_grads = jnp.sum(grad_picked.astype(jnp.float32) * expert_result, axis=1)
     grad_expert_down = contract_first(grad_rows, expert_hidden)[None]
     grad_expert_hidden = jnp.dot(grad_rows, expert_down[0], preferred_element_type=jnp.float32)
     grad_gate_pre = (grad_expert_hidden * up_pre * gate_slope).astype(jnp.bfloat16)
@@ -239,20 +225,72 @@
     grad_rows_in = contract_last(grad_gate_pre, expert_gate[0]) + contract_last(
         grad_up_pre, expert_up[0]
     )
-    grad_back = lax.all_to_all(
-        grad_rows_in.reshape(devices, capacity, features).astype(jnp.bfloat16),
+
+    part = shared_gate.shape[1] // devices
+    part_gate = lax.dynamic_slice_in_dim(shared_gate, own * part, part, 1)
+    part_up = lax.dynamic_slice_in_dim(shared_up, own * part, part, 1)
+    part_down = lax.dynamic_slice_in_dim(shared_down, own * part, part, 1)
+    shared_pre_gate = jnp.dot(everyone_ffn, part_gate, preferred_element_type=jnp.float32)
+    shared_pre_up = jnp.dot(everyone_ffn, part_up, preferred_element_type=jnp.float32)
+    shared_act, shared_slope = swish_parts(shared_pre_gate)
+    shared_hidden = (shared_act * shared_pre_up).astype(jnp.bfloat16)
+    grad_shared_hidden = jnp.dot(everyone_grad, part_down, preferred_element_type=jnp.float32)
+    grad_shared_gate_pre = (grad_shared_hidden * shared_pre_up * shared_slope).astype(jnp.bfloat16)
+    grad_shared_up_pre = (grad_shared_hidden * shared_act).astype(jnp.bfloat16)
+    shared_grads = jnp.concatenate(
+        [
+            contract_first(everyone_ffn, grad_shared_gate_pre),
+            contract_first(everyone_ffn, grad_shared_up_pre),
+            contract_first(everyone_grad, shared_hidden),
+        ],
+        axis=1,
+    ).astype(jnp.bfloat16)
+    share_rows = features // devices
+    shared_grads = lax.all_to_all(
+        shared_grads.reshape(devices, share_rows, 3 * part), "dp", split_axis=0, concat_axis=0
+    ).astype(jnp.float32)
+    grad_shared_gate, grad_shared_up, grad_shared_down = (
+        shared_grads[:, :, i * part : (i + 1) * part]
+        .transpose(1, 0, 2)
+        .reshape(share_rows, devices * part)
+        for i in range(3)
+    )
+
+    grad_top = grad_out.astype(jnp.float32)
+    ffn_part = put_rows(slot_gates * expert_result, [shared_hidden], [part_down])
+    ffn_total = lax.psum_scatter(ffn_part, "dp", scatter_dimension=0, tiled=True)
+    ffn_total = lax.psum(ffn_total, "tensor").astype(jnp.float32)
+    output = (hidden + ffn_total).astype(jnp.bfloat16)
+    pair_grads = jnp.sum(
+        jnp.where(picked, slot_grads.reshape(devices, capacity, 1), 0.0), axis=1
+    ).reshape(devices * rows_here, 1)
+    pair_high = pair_grads.astype(jnp.bfloat16).astype(jnp.float32)
+    column = jnp.arange(128, dtype=jnp.int32)[None, :]
+    pair_columns = jnp.where(
+        column == own,
+        pair_high,
+        jnp.where(column == own + experts, pair_grads - pair_high, 0.0),
+    )
+    grad_ffn_in = put_rows(
+        grad_rows_in, [grad_shared_gate_pre, grad_shared_up_pre], [part_gate, part_up]
+    )
+    grad_ffn_sum = lax.psum_scatter(
+        jnp.concatenate([grad_ffn_in, pair_columns.astype(jnp.bfloat16)], axis=1),
         "dp",
-        split_axis=0,
-        concat_axis=0,
+        scatter_dimension=0,
         tiled=True,
-    ).astype(jnp.float32)
-    grad_routed = jnp.sum(
-        jnp.take(grad_back.reshape(-1, features), place, axis=0).reshape(rows_here, TOPK, features),
-        axis=1,
-    )
-    grad_ffn_total = lax.psum(
-        (grad_ffn_in + grad_routed + grad_router_in).astype(jnp.bfloat16), "tensor"
-    ).astype(jnp.float32)
+    )
+    grad_ffn_sum = lax.psum(grad_ffn_sum.astype(jnp.float32), "tensor")
+    dense_grad = (
+        grad_ffn_sum[:, features : features + experts]
+        + grad_ffn_sum[:, features + experts : features + 2 * experts]
+    )
+    grad_logits = router_probs * (
+        dense_grad - jnp.sum(router_probs * dense_grad, axis=-1, keepdims=True)
+    )
+    grad_router_in = contract_last(grad_logits, router, highest)
+    grad_router_part = contract_first(ffn_normed, grad_logits, highest) / lax.axis_size("tensor")
+    grad_ffn_total = grad_ffn_sum[:, :features] + grad_router_in
     grad_g_ffn = jnp.sum(grad_ffn_total * ffn_unit, axis=0)
     grad_hidden = grad_top + normalize_back(grad_ffn_total, ffn_unit, ffn_factor, g_ffn)
     grad_hidden_bf = grad_hidden.astype(jnp.bfloat16)
@@ -333,15 +371,6 @@
             grad_w_out.astype(jnp.bfloat16), "dp", scatter_dimension=0, tiled=True
         ).astype(jnp.float32),
         lax.psum_scatter(
-            grad_shared_gate.astype(jnp.bfloat16), "dp", scatter_dimension=0, tiled=True
-        ).astype(jnp.float32),
-        lax.psum_scatter(
-            grad_shared_up.astype(jnp.bfloat16), "dp", scatter_dimension=0, tiled=True
-        ).astype(jnp.float32),
-        lax.psum_scatter(
-            grad_shared_down.astype(jnp.bfloat16), "dp", scatter_dimension=0, tiled=True
-        ).astype(jnp.float32),
-        lax.psum_scatter(
             grad_g_attn.astype(jnp.bfloat16), "dp", scatter_dimension=0, tiled=True
         ).astype(jnp.float32),
         lax.psum_scatter(
@@ -355,17 +384,17 @@
     return (
         output,
         grad_tokens,
-        summed[7],
+        summed[4],
         summed[0],
         summed[1],
         everywhere[1],
         summed[2],
         summed[3],
-        summed[8],
+        summed[5],
         everywhere[0],
-        summed[4],
-        summed[5],
-        summed[6],
+        grad_shared_gate,
+        grad_shared_up,
+        grad_shared_down,
         grad_expert_gate,
         grad_expert_up,
         grad_expert_down,

time: 1910 us -> 1350 us (0.71)
  blocking collectives: 476 us -> 188 us
  waiting for transfers between devices: 910 us -> 712 us
  local copies, waits for them, and re-layouts: 154 us -> 48.5 us
  matrix products: 216 us -> 295 us
  other arithmetic: 118 us -> 76.7 us
    all_to_all x2 -> x0, blocking collectives: 407 us -> none  [the longest x1 219 us: shards(): lax.all_to_all(grad_buffer, 'dp', split_axis=0, concat_axis=0, tiled=True)]
    all_to_all x2 -> x1, waiting for transfers between devices: 242 us -> 0.01 us  [shards(): lax.all_to_all(shared_grads.reshape(devices, share_rows, 3 * part), 'dp',...]
    unnamed x14 -> x13, waiting for transfers between devices: 214 us -> 74.6 us
    all_gather x0 -> x2, waiting for transfers between devices: none -> 134 us  [the longest x1 104 us: shards(): everyone_ffn = lax.all_gather(ffn_bf, 'dp', tiled=True)]
    dot_general x3 -> x8, matrix products: 12.2 us -> 92.1 us  [the longest x2 31.3 us: put_rows(): jnp.einsum('jtk,jkc->jtc', left, right, preferred_element_type=jnp.float32)]
    all_gather x0 -> x2, blocking collectives: none -> 61.4 us  [the longest x1 39 us: shards(): everyone_probs = lax.all_gather(router_probs, 'dp', tiled=True)]
    psum x0 -> x1, blocking collectives: none -> 56.6 us  [shards(): grad_ffn_sum = lax.psum(grad_ffn_sum.astype(jnp.float32), 'tensor')]
    reduce_scatter x2, waiting for transfers between devices: 166 us -> 219 us  [the longest x1 148 us: shards(): lax.psum_scatter(jnp.concatenate([grad_ffn_in, pair_columns.astype(jnp.bf...]
  transfers between devices with their start and end apart: 13 -> 12, of which waited for: 12 -> 11; matrix products, arithmetic and copies ran while one was open for 10% -> 17% of each run, Pallas kernels for 0% -> 0%
where the time goes in v1:
time: 1350 us; the launch traced here: 1340 us
  waiting for transfers between devices  712 us (53%)
  matrix products  295 us (22%)
  blocking collectives  188 us (14%)
  other arithmetic  76.7 us (6%)
  local copies, waits for them, and re-layouts  48.5 us (4%)
  between operations  17.8 us (1%)
    reduce_scatter x1, waiting for transfers between devices, shards(): lax.psum_scatter(jnp.concatenate([grad_ffn_in, pair_columns.astype(jnp.bf...  148 us
    all_gather x1, waiting for transfers between devices, shards(): everyone_ffn = lax.all_gather(ffn_bf, 'dp', tiled=True)  104 us
    reduce_scatter x1, waiting for transfers between devices, shards(): lax.psum_scatter(grad_w_query.astype(jnp.bfloat16), 'dp', scatter_dimensi...  87 us
    unnamed x13, waiting for transfers between devices  74.6 us
    reduce_scatter x1, waiting for transfers between devices, shards(): lax.psum_scatter(grad_w_out.astype(jnp.bfloat16), 'dp', scatter_dimension...  73.7 us
    reduce_scatter x1, waiting for transfers between devices, shards(): lax.psum_scatter(ffn_part, 'dp', scatter_dimension=0, tiled=True)  71.8 us
    dot_general x11, matrix products, contract_first(): lax.dot_general(left, right, (((0,), (0,)), ((), ())), precision=precisio...  71 us
    unnamed x2, blocking collectives  70.1 us
  transfers between devices with their start and end apart: 12, of which 11 were waited for; matrix products, arithmetic and copies ran while one was open for 17% of the time, Pallas kernels for 0%

profile of v1, /device:TPU:0, one launch (start us, length us, event | category | flops | bytes accessed | tf_op | source)
XLA Modules:
  0.0 1344.3 jit_solution(16500887333205340176)
XLA Ops:
  36.0 42.3 %all-reduce.9.cloned.1.call-done = bf16[256,2048]{1,0:T(8,128)(2,1)} async-done(((bf16[256,2048]{1,0:T(8,128)(2,1)}), bf16[256,2048]{1,0:T(8,128)(2,1)}) %all-reduce.9.cloned.1.call-update) | async-done | bytes 1048592 | tf_op jit(solution)/shard_map/psum | solution.py:159
  82.1 22.4 %all_gather.12 = s32[4096,6]{0,1:T(8,128)S(1)} all-gather(s32[256,6]{0,1:T(8,128)S(1)} %copy-done.73), channel_id=1, replica_groups=mesh['dp'=16,'tensor'=2] {'dp'}, dimensions={0}, use_global_device_ids=true | all-gather | bytes 104448 | tf_op jit(solution)/shard_map/all_gather | solution.py:169
  117.2 39.0 %all_gather.14 = f32[4096,16]{1,0:T(8,128)S(1)} all-gather(f32[256,16]{1,0:T(8,128)S(1)} %fusion.134), channel_id=1, replica_groups=mesh['dp'=16,'tensor'=2] {'dp'}, dimensions={0}, use_global_device_ids=true | all-gather | bytes 278528 | tf_op jit(solution)/shard_map/all_gather | solution.py:171
  157.5 30.0 %all-gather.5.cloned.1.call-done = bf16[4096,2048]{1,0:T(8,128)(2,1)} async-done(((bf16[256,2048]{1,0:T(8,128)(2,1)}), bf16[4096,2048]{1,0:T(8,128)(2,1)}) %all-gather.5.cloned.1.call-update) | async-done | bytes 16777232 | tf_op jit(solution)/shard_map/all_gather | solution.py:168
  187.5 12.8 convolution_bitcast_fusion
  200.3 11.4 convolution_convert_fusion.1
  211.7 103.7 %all-gather.3.cloned.1.call-done = bf16[4096,2048]{1,0:T(8,128)(2,1)} async-done(((bf16[256,2048]{1,0:T(8,128)(2,1)}), bf16[4096,2048]{1,0:T(8,128)(2,1)}) %all-gather.3.cloned.1.call-update) | async-done | bytes 16777232 | tf_op jit(solution)/shard_map/all_gather | solution.py:170
  315.4 11.5 convolution_convert_fusion.2
  326.9 11.1 fusion.34
  338.1 10.4 multiply_convert_fusion.3
  348.5 11.2 fusion.8
  368.9 13.7 %multiply_convert_fusion.1 = (bf16[2048,704]{0,1:T(8,128)(2,1)S(1)}, bf16[2048,704]{0,1:T(8,128)(2,1)S(1)}) fusion(f32[2048,704]{0,1:T(8,128)} %fusion.34, f32[2048,704]{0,1:T(8,128)} %get-tuple-element.128, bf16[2048,2048]{1,0:T(8,128)(2,1)} %bitcast.182, bf16[1,2048,704]{1,2,0:T(8,128)(2,1)S(1)} %copy-done), kind=kOutput, calls=%fused_computation.23 | convolution fusion | flops 5924323328 | bytes 28573696 | tf_op jit(solution)/shard_map/dot_general | solution.py:220
  382.7 10.3 fusion.32
  393.0 12.7 add_convert_fusion
  405.8 12.4 fusion.127
  418.2 12.5 multiply_convert_fusion.7
  441.3 18.1 %fusion.17 = bf16[16,256,2048]{2,1,0:T(8,128)(2,1)} fusion(bf16[16,88,2048]{2,1,0:T(8,128)(2,1)} %broadcast_in_dim.116, bf16[16,88,2048]{2,1,0:T(8,128)(2,1)} %broadcast_in_dim.115, bf16[16,128,2048]{2,1,0:T(8,128)(2,1)} %bitcast.213, bf16[16,256,88]{1,2,0:T(8,128)(2,1)} %get-tuple-element.138, bf16[16,256,88]{1,2,0:T(8,128)(2,1)} %get-tuple-element.139, ...), kind=kOutput, calls=%fused_computation.21 | convolution fusion | flops 5175902208 | bytes 39190528 | tf_op jit(solution)/shard_map/jtk,jkc->jtc/dot_general | solution.py:204
  459.4 15.6 %pad_maximum_fusion = bf16[4096,2176]{1,0:T(8,128)(2,1)} fusion(bf16[4096,128]{1,0:T(8,128)(2,1)S(1)} %select_convert_fusion, bf16[4096,2048]{1,0:T(8,128)(2,1)} %bitcast.181), kind=kLoop, calls=%fused_computation.7 | loop fusion | flops 35651584 | bytes 35651584 | tf_op jit(solution)/shard_map/concatenate | solution.py:278
  476.3 16.4 %fusion.9 = (bf16[2048,2048]{1,0:T(8,128)(2,1)}, bf16[2048,2048]{1,0:T(8,128)(2,1)S(1)}) fusion(bf16[16,128,2048]{2,1,0:T(8,128)(2,1)} %convolution_convert_fusion.1, f32[2048]{0:T(1024)S(1)} %bitcast.209, f32[2048,2048]{1,0:T(8,128)} %get-tuple-element.130), kind=kLoop, calls=%fused_computation.13 | loop fusion | flops 20971520 | bytes 41951232 | tf_op jit(solution)/shard_map/convert_element_type | solution.py:211
  496.7 13.2 fusion.14
  510.6 147.7 %reduce-scatter.14.cloned.1.call-done = bf16[256,2176]{1,0:T(8,128)(2,1)} async-done(((bf16[4096,2176]{1,0:T(8,128)(2,1)}), bf16[256,2176]{1,0:T(8,128)(2,1)}) %reduce-scatter.14.cloned.1.call-update) | async-done | bytes 1114128 | tf_op jit(solution)/shard_map/reduce_scatter | solution.py:277
  658.3 56.6 %all-reduce.12 = f32[256,2176]{1,0:T(8,128)} all-reduce(bf16[256,2176]{1,0:T(8,128)(2,1)} %reduce-scatter.14.cloned.1.call-done), channel_id=1, replica_groups=mesh['dp'=16,'tensor'=2] {'tensor'}, use_global_device_ids=true, to_apply=%region_18.19 | all-reduce | flops 557056 | bytes 3342336 | tf_op jit(solution)/shard_map/psum | solution.py:283
  766.9 71.8 %reduce-scatter.12.cloned.1.call-done = bf16[256,2048]{1,0:T(8,128)(2,1)} async-done(((bf16[4096,2048]{1,0:T(8,128)(2,1)}), bf16[256,2048]{1,0:T(8,128)(2,1)}) %reduce-scatter.12.cloned.1.call-update) | async-done | bytes 1048592 | tf_op jit(solution)/shard_map/reduce_scatter | solution.py:261
  845.1 62.6 %all-reduce.11.cloned.1.call-done = (bf16[256,2048]{1,0:T(8,128)(2,1)}, bf16[256,576]{0,1:T(8,128)(2,1)}, bf16[256,2048]{1,0:T(8,128)(2,1)}) async-done(((bf16[256,2048]{1,0:T(8,128)(2,1)}, bf16[256,576]{0,1:T(8,128)(2,1)}, bf16[256,2048]{1,0:T(8,128)(2,1)}), (bf16[256,2048]{1,0:T(8,128)(2,1)}, bf16[256,576]{0,1:T(8,128)(2,1)}, bf16[256,2048]{1,0:T(8,128)(2,1)})) %all-reduce.11.cloned.1.call-update) | async-done | bytes 2392080 | tf_op jit(solution)/shard_map/psum | solution.py:262
  956.8 11.1 convolution_bitcast_fusion.2
  993.0 40.0 %all-reduce.1 = f32[512]{0:T(512)S(1)} all-reduce(f32[512]{0:T(512)S(1)} %copy-done.78), channel_id=7, replica_groups=mesh['dp'=16,'tensor'=2] {'dp','tensor'}, use_global_device_ids=true, to_apply=%region_31.32.clone | all-reduce | flops 512 | bytes 4096
  1033.5 13.1 reduce-scatter.24.cloned.1.call-done
  1052.4 30.2 %all-reduce.3 = (bf16[2048]{0:T(1024)(128)(2,1)S(1)}, bf16[2048]{0:T(1024)(128)(2,1)S(1)}) all-reduce(bf16[2048]{0:T(1024)(128)(2,1)S(1)} %get-tuple-element.82, bf16[2048]{0:T(1024)(128)(2,1)S(1)} %copy-done.75), channel_id=4, replica_groups=mesh['dp'=16,'tensor'=2] {'dp'}, use_global_device_ids=true, to_apply=%region_27.28.clone | all-reduce | flops 4096 | bytes 16384
  1089.8 18.1 %reduce-scatter.18.cloned.1.call-done = bf16[32,2048]{1,0:T(8,128)(2,1)} async-done(((bf16[512,2048]{1,0:T(8,128)(2,1)}), bf16[32,2048]{1,0:T(8,128)(2,1)}) %reduce-scatter.18.cloned.1.call-update) | async-done | bytes 131088 | tf_op jit(solution)/shard_map/reduce_scatter | solution.py:367
  1109.5 60.8 %reduce-scatter.22.cloned.1.call-done = bf16[128,288]{1,0:T(8,128)(2,1)} async-done(((bf16[2048,288]{1,0:T(8,128)(2,1)}), bf16[128,288]{1,0:T(8,128)(2,1)}) %reduce-scatter.22.cloned.1.call-update) | async-done | bytes 73744
  1172.0 73.7 %reduce-scatter.20.cloned.1.call-done = bf16[128,1024]{1,0:T(8,128)(2,1)} async-done(((bf16[2048,1024]{1,0:T(8,128)(2,1)}), bf16[128,1024]{1,0:T(8,128)(2,1)}) %reduce-scatter.20.cloned.1.call-update) | async-done | bytes 262160 | tf_op jit(solution)/shard_map/reduce_scatter | solution.py:370
  1247.5 87.0 %reduce-scatter.16.cloned.1.call-done = bf16[128,1536]{1,0:T(8,128)(2,1)} async-done(((bf16[2048,1536]{1,0:T(8,128)(2,1)}), bf16[128,1536]{1,0:T(8,128)(2,1)}) %reduce-scatter.16.cloned.1.call-update) | async-done | bytes 393232 | tf_op jit(solution)/shard_map/reduce_scatter | solution.py:361
  (333 shorter events, 223.0 us)
Async XLA Ops:
  8.0 340.4 %copy-start = (bf16[1,2048,704]{1,2,0:T(8,128)(2,1)S(1)}, bf16[1,2048,704]{1,2,0:T(8,128)(2,1)}, u32[]{:S(2)}) copy-start(bf16[1,2048,704]{1,2,0:T(8,128)(2,1)} %param.35) | copy-start | bytes 8650756
  8.0 70.3 %all-reduce.9.cloned.1.call-start = ((), (), s32[]{:S(2)}) async-start(), calls=%async_computation.8 | async-start | bytes 2097152 | tf_op jit(solution)/shard_map/psum | solution.py:159
  35.4 45.1 %copy-start.56 = (f32[2048]{0:T(1024)S(1)}, f32[2048]{0:T(1024)}, u32[]{:S(2)}) copy-start(f32[2048]{0:T(1024)} %param.28) | copy-start | bytes 24580
  35.4 152.1 %all-gather.5.cloned.1.call-start = ((), (), s32[]{:S(2)}) async-start(), calls=%async_computation.11 | async-start | bytes 17825792 | tf_op jit(solution)/shard_map/all_gather | solution.py:168
  36.0 279.4 %all-gather.3.cloned.1.call-start = ((), (), s32[]{:S(2)}) async-start(), calls=%async_computation.9 | async-start | bytes 17825792 | tf_op jit(solution)/shard_map/all_gather | solution.py:170
  82.0 576.3 %reduce-scatter.14.cloned.1.call-start = ((), (), s32[]{:S(2)}) async-start(), calls=%async_computation.12 | async-start | bytes 18939904 | tf_op jit(solution)/shard_map/reduce_scatter | solution.py:277
  115.8 41.6 %copy-start.24 = (f32[256,16]{1,0:T(8,128)}, f32[256,16]{1,0:T(8,128)S(1)}, u32[]{:S(2)}) copy-start(f32[256,16]{1,0:T(8,128)S(1)} %copy.158) | copy-start | bytes 49156
  430.7 45.5 %copy-start.15 = (bf16[4096,88]{0,1:T(8,128)(2,1)}, bf16[4096,88]{0,1:T(8,128)(2,1)S(1)}, u32[]{:S(2)}) copy-start(bf16[4096,88]{0,1:T(8,128)(2,1)S(1)} %get-tuple-element.97) | copy-start | bytes 2162692
  475.0 363.6 %reduce-scatter.12.cloned.1.call-start = ((), (), s32[]{:S(2)}) async-start(), calls=%async_computation.10 | async-start | bytes 17825792 | tf_op jit(solution)/shard_map/reduce_scatter | solution.py:261
  509.9 205.0 %copy-start.25 = (f32[256,16]{1,0:T(8,128)S(1)}, f32[256,16]{1,0:T(8,128)}, u32[]{:S(2)}) copy-start(f32[256,16]{1,0:T(8,128)} %copy-done.24) | copy-start | bytes 49156
  509.9 205.0 %copy-start.67 = (f32[256]{0:T(256)S(1)}, f32[256]{0:T(256)}, u32[]{:S(2)}) copy-start(f32[256]{0:T(256)} %copy-done.66) | copy-start | bytes 3076
  509.9 205.0 %copy-start.69 = (f32[256]{0:T(256)S(1)}, f32[256]{0:T(256)}, u32[]{:S(2)}) copy-start(f32[256]{0:T(256)} %copy-done.68) | copy-start | bytes 3076
  509.9 206.2 %copy-start.4 = (bf16[256,2048]{1,0:T(8,128)(2,1)S(1)}, bf16[256,2048]{1,0:T(8,128)(2,1)}, u32[]{:S(2)}) copy-start(bf16[256,2048]{1,0:T(8,128)(2,1)} %param.18) | copy-start | bytes 3145732
  509.9 206.2 %copy-start.9 = (bf16[256,2048]{1,0:T(8,128)(2,1)S(1)}, bf16[256,2048]{1,0:T(8,128)(2,1)}, u32[]{:S(2)}) copy-start(bf16[256,2048]{1,0:T(8,128)(2,1)} %all-reduce.9.cloned.1.call-done) | copy-start | bytes 3145732
  510.0 206.2 %copy-start.40 = (f32[256,16]{1,0:T(8,128)S(1)}, f32[256,16]{1,0:T(8,128)}, u32[]{:S(2)}) copy-start(f32[256,16]{1,0:T(8,128)} %copy-done.39) | copy-start | bytes 49156
  510.0 206.2 %copy-start.57 = (f32[2048]{0:T(1024)S(1)}, f32[2048]{0:T(1024)}, u32[]{:S(2)}) copy-start(f32[2048]{0:T(1024)} %param.28) | copy-start | bytes 24580
  510.0 206.2 %copy-start.71 = (f32[256]{0:T(256)S(1)}, f32[256]{0:T(256)}, u32[]{:S(2)}) copy-start(f32[256]{0:T(256)} %copy-done.70) | copy-start | bytes 3076
  510.0 206.2 %copy-start.88 = (f32[2048,16]{0,1:T(8,128)S(1)}, f32[2048,16]{0,1:T(8,128)}, u32[]{:S(2)}) copy-start(f32[2048,16]{0,1:T(8,128)} %param.29) | copy-start | bytes 393220
  510.0 397.7 %all-reduce.11.cloned.1.call-start = ((), (), s32[]{:S(2)}) async-start(), calls=%async_computation.18 | async-start | bytes 4784128 | tf_op jit(solution)/shard_map/psum | solution.py:262
  766.9 72.1 %copy-start.72 = (f32[256]{0:T(256)S(1)}, f32[256]{0:T(256)}, u32[]{:S(2)}) copy-start(f32[256]{0:T(256)} %copy-done.70) | copy-start | bytes 3076
  766.9 72.1 %copy-start.80 = (f32[256]{0:T(256)S(1)}, f32[256]{0:T(256)}, u32[]{:S(2)}) copy-start(f32[256]{0:T(256)} %copy-done.79) | copy-start | bytes 3076
  838.7 207.9 %reduce-scatter.24.cloned.1.call-start = ((), (), s32[]{:S(2)}) async-start(), calls=%async_computation.17 | async-start | bytes 1081344
  842.9 64.8 %copy-start.46 = (f32[2048]{0:T(1024)S(1)}, f32[2048]{0:T(1024)}, u32[]{:S(2)}) copy-start(f32[2048]{0:T(1024)} %param.22) | copy-start | bytes 24580
  842.9 64.8 %copy-start.55 = (f32[256]{0:T(256)S(1)}, f32[256]{0:T(256)}, u32[]{:S(2)}) copy-start(f32[256]{0:T(256)} %copy-done.54) | copy-start | bytes 3076
  842.9 265.0 %reduce-scatter.18.cloned.1.call-start = ((), (), s32[]{:S(2)}) async-start(), calls=%async_computation.14 | async-start | bytes 2228224 | tf_op jit(solution)/shard_map/reduce_scatter | solution.py:367
  845.0 325.2 %reduce-scatter.22.cloned.1.call-start = ((), (), s32[]{:S(2)}) async-start(), calls=%async_computation.16 | async-start | bytes 1671168
  910.8 334.9 %reduce-scatter.20.cloned.1.call-start = ((), (), s32[]{:S(2)}) async-start(), calls=%async_computation.15 | async-start | bytes 4456448 | tf_op jit(solution)/shard_map/reduce_scatter | solution.py:370
  915.8 418.7 %reduce-scatter.16.cloned.1.call-start = ((), (), s32[]{:S(2)}) async-start(), calls=%async_computation.13 | async-start | bytes 6684672 | tf_op jit(solution)/shard_map/reduce_scatter | solution.py:361
  950.8 35.2 %all-to-all-start = ((bf16[16,128,264]{1,2,0:T(8,128)(2,1)}), bf16[16,128,264]{1,2,0:T(8,128)(2,1)S(1)}, u32[]{:S(2)}, u32[]{:S(2)}) async-start(bf16[16,128,264]{1,2,0:T(8,128)(2,1)} %pad_maximum_fusion.1), calls=%async_computation.5 | async-start | bytes 2162688 | tf_op jit(solution)/shard_map/all_to_all | solution.py:249
  987.3 60.8 %copy-start.36 = (bf16[256,2048]{1,0:T(8,128)(2,1)S(1)}, bf16[256,2048]{1,0:T(8,128)(2,1)}, u32[]{:S(2)}) copy-start(bf16[256,2048]{1,0:T(8,128)(2,1)} %get-tuple-element.92) | copy-start | bytes 3145732
  987.3 60.8 %copy-start.44 = (bf16[256,576]{0,1:T(8,128)(2,1)S(1)}, bf16[256,576]{0,1:T(8,128)(2,1)}, u32[]{:S(2)}) copy-start(bf16[256,576]{0,1:T(8,128)(2,1)} %get-tuple-element.91) | copy-start | bytes 884740
  1083.8 252.7 %copy-start.1 = (bf16[1,2048,704]{1,2,0:T(8,128)(2,1)S(1)}, bf16[1,2048,704]{1,2,0:T(8,128)(2,1)}, u32[]{:S(2)}) copy-start(bf16[1,2048,704]{1,2,0:T(8,128)(2,1)} %param.35) | copy-start | bytes 8650756
  (79 other events, 452.3 us)
Sparse Core Ops, SparseCore 0:
  35.5 42.7 all-reduce.8
  838.8 68.8 all-reduce.10
  910.0 136.5 reduce-scatter.23
  1050.3 57.5 reduce-scatter.17
  1111.9 58.3 reduce-scatter.21
  1174.0 71.6 reduce-scatter.19
  1250.2 84.3 reduce-scatter.15
Sparse Core Ops, SparseCore 1:
  38.3 149.1 all-gather.4
  190.3 125.0 all-gather.2
  475.1 183.1 reduce-scatter.13
  663.0 175.7 reduce-scatter.11

commit v2 on v1

--- a/solution.py
+++ b/solution.py
@@ -1,6 +1,10 @@
+import functools
+
 import jax
 import jax.numpy as jnp
 from jax import lax
+from jax.experimental import pallas as pl
+from jax.experimental.pallas import tpu as pltpu
 from jax.sharding import PartitionSpec as P
 
 PLAIN_HEAD_SIZE = 128
@@ -71,6 +75,423 @@
 def swish_parts(gate_pre):
     sigma = jax.nn.sigmoid(gate_pre)
     return (gate_pre * sigma, sigma * (1.0 + gate_pre * (1.0 - sigma)))
+
+
+VMEM_LIMIT = 60 * 1024 * 1024
+
+
+def place_of(x_size):
+    me = lax.axis_index("dp")
+    core = me % 2
+    x = (me // 2) % x_size
+    z = me // (2 * x_size)
+    return z, x, core
+
+
+def index_of(z, x, core, x_size):
+    return (z * x_size + x) * 2 + core
+
+
+def remote(src, dst, send_sem, recv_sem, target):
+    return pltpu.make_async_remote_copy(
+        src_ref=src,
+        dst_ref=dst,
+        send_sem=send_sem,
+        recv_sem=recv_sem,
+        device_id={"dp": target},
+        device_id_type=pl.DeviceIdType.MESH,
+    )
+
+
+def greet(z, x, core, z_size, x_size, pair=False):
+    barrier = pltpu.get_barrier_semaphore()
+
+    def tell(target):
+        pl.semaphore_signal(
+            barrier, inc=1, device_id={"dp": target}, device_id_type=pl.DeviceIdType.MESH
+        )
+
+    tell(index_of(z, x, 1 - core, x_size))
+    tell(index_of(z, 1 - x, core, x_size))
+
+    @pl.when(z > 0)
+    def _():
+        tell(index_of(z - 1, x, core, x_size))
+
+    @pl.when(z < z_size - 1)
+    def _():
+        tell(index_of(z + 1, x, core, x_size))
+
+    inner = (z + z_size - 1) // z_size - z // (z_size - 1)
+    if pair:
+        pl.semaphore_signal(
+            barrier,
+            inc=1,
+            device_id={"tensor": 1 - lax.axis_index("tensor")},
+            device_id_type=pl.DeviceIdType.MESH,
+        )
+    pl.semaphore_wait(barrier, 3 + inner + (1 if pair else 0))
+
+
+def gather_kernel(z_size, x_size, count, *refs):
+    ins, outs = refs[:count], refs[count : 2 * count]
+    own_sem, up_s, up_r, dn_s, dn_r, x_s, x_r, c_s, c_r = refs[2 * count :]
+    z, x, core = place_of(x_size)
+    greet(z, x, core, z_size, x_size)
+    at = functools.partial(index_of, x_size=x_size)
+    keep = [
+        pltpu.make_async_copy(ins[a], outs[a].at[at(z, x, core)], own_sem.at[a])
+        for a in range(count)
+    ]
+    for copy in keep:
+        copy.start()
+
+    def up(a, d):
+        block = outs[a].at[at(z - d, x, core)]
+        src = ins[a] if d == 0 else block
+        return remote(src, block, up_s.at[a, d], up_r.at[a, d], at(z + 1, x, core))
+
+    def down(a, d):
+        block = outs[a].at[at(z + d, x, core)]
+        src = ins[a] if d == 0 else block
+        return remote(src, block, dn_s.at[a, d], dn_r.at[a, d], at(z - 1, x, core))
+
+    def across(a, w, own=False):
+        block = outs[a].at[at(w, x, core)]
+        return remote(ins[a] if own else block, block, x_s.at[a, w], x_r.at[a, w], at(z, 1 - x, core))
+
+    def beside(a, w, v, own=False):
+        block = outs[a].at[at(w, v, core)]
+        return remote(
+            ins[a] if own else block, block, c_s.at[a, w, v], c_r.at[a, w, v], at(z, x, 1 - core)
+        )
+
+    def each(do):
+        for a in range(count):
+            do(a)
+
+    def from_across(w):
+        def do(a):
+            across(a, w).wait_recv()
+            beside(a, w, 1 - x).start()
+
+        each(do)
+
+    def when_up(d, do):
+        pl.when(z >= d)(lambda: each(do))
+
+    def when_down(d, do):
+        pl.when(z + d < z_size)(lambda: each(do))
+
+    def first(a):
+        across(a, z, True).start()
+        pl.when(z < z_size - 1)(lambda: up(a, 0).start())
+        pl.when(z > 0)(lambda: down(a, 0).start())
+        beside(a, z, x, True).start()
+
+    each(first)
+    for d in range(1, z_size):
+
+        def passed_up(a):
+            up(a, d - 1).wait_recv()
+            pl.when(z < z_size - 1)(lambda: up(a, d).start())
+            across(a, z - d).start()
+            beside(a, z - d, x).start()
+
+        def passed_down(a):
+            down(a, d - 1).wait_recv()
+            pl.when(z > 0)(lambda: down(a, d).start())
+            across(a, z + d).start()
+            beside(a, z + d, x).start()
+
+        when_up(d, passed_up)
+        when_down(d, passed_down)
+        if d == 1:
+            from_across(z)
+        else:
+            pl.when(z >= d - 1)(lambda: from_across(z - (d - 1)))
+            pl.when(z + d - 1 < z_size)(lambda: from_across(z + (d - 1)))
+    pl.when(z >= z_size - 1)(lambda: from_across(z - (z_size - 1)))
+    pl.when(z < 1)(lambda: from_across(z + (z_size - 1)))
+    for a in range(count):
+        for w in range(z_size):
+            for v in range(x_size):
+                beside(a, w, v).wait()
+            across(a, w).wait_send()
+    for d in range(z_size):
+        pl.when((z >= d) & (z < z_size - 1))(lambda: each(lambda a: up(a, d).wait_send()))
+        pl.when((z + d < z_size) & (z > 0))(lambda: each(lambda a: down(a, d).wait_send()))
+    for copy in keep:
+        copy.wait()
+
+
+def gather_rows(arrays, z_size, x_size, collective_id):
+    count = len(arrays)
+    n = 2 * z_size * x_size
+    dma = pltpu.SemaphoreType.DMA
+    outs = pl.pallas_call(
+        functools.partial(gather_kernel, z_size, x_size, count),
+        out_shape=[jax.ShapeDtypeStruct((n,) + a.shape, a.dtype) for a in arrays],
+        in_specs=[pl.BlockSpec(memory_space=pl.ANY)] * count,
+        out_specs=[pl.BlockSpec(memory_space=pl.ANY)] * count,
+        scratch_shapes=[dma((count,))]
+        + [dma((count, z_size))] * 6
+        + [dma((count, z_size, x_size))] * 2,
+        compiler_params=pltpu.CompilerParams(
+            collective_id=collective_id, has_side_effects=True, vmem_limit_bytes=VMEM_LIMIT
+        ),
+        name="gather_rows",
+    )(*arrays)
+    return outs
+
+
+def add_into(dst, *srcs):
+    rows = dst.shape[0]
+    step = 32 if rows % 32 == 0 else 16
+
+    def body(i, _):
+        here = pl.ds(pl.multiple_of(i * step, step), step)
+        total = dst[here, :].astype(jnp.float32)
+        for src in srcs:
+            total = total + src[here, :].astype(jnp.float32)
+        dst[here, :] = total.astype(dst.dtype)
+        return 0
+
+    lax.fori_loop(0, rows // step, body, 0)
+
+
+def scatter_kernel(x_size, parts, pair, *refs):
+    z_size = 4
+    ins, outs, refs = refs[:parts], refs[parts : 2 * parts], refs[2 * parts :]
+    own, c_buf, x_buf, z_buf = (refs[i * parts : (i + 1) * parts] for i in range(4))
+    refs = refs[4 * parts :]
+    y_buf = None
+    if pair:
+        y_buf, y_s, y_r, refs = refs[:parts], refs[parts], refs[parts + 1], refs[parts + 2 :]
+    l_sem, c_s, c_r, x_s, x_r, z_s, z_r = refs
+    z, x, core = place_of(x_size)
+    at = functools.partial(index_of, x_size=x_size)
+    half = z // 2
+    inner = ((z + 3) // 4) * ((6 - z) // 4)
+    order = [3 - 3 * half, 2 - half, 1 - z + 4 * half, z]
+    load = lambda p, w, v: pltpu.make_async_copy(
+        ins[p].at[at(w, v, core)], own[p].at[w, v], l_sem.at[p, w, v]
+    )
+    beside = lambda p, w, v: remote(
+        ins[p].at[at(w, v, 1 - core)],
+        c_buf[p].at[w, v],
+        c_s.at[p, w, v],
+        c_r.at[p, w, v],
+        at(z, x, 1 - core),
+    )
+    across = lambda p, w: remote(
+        c_buf[p].at[w, 1 - x], x_buf[p].at[w], x_s.at[p, w], x_r.at[p, w], at(z, 1 - x, core)
+    )
+
+    def along(p, w, slot, target):
+        return remote(
+            c_buf[p].at[w, x], z_buf[p].at[slot], z_s.at[p, w], z_r.at[p, slot], at(target, x, core)
+        )
+
+    twin = lambda p: pltpu.make_async_remote_copy(
+        src_ref=c_buf[p].at[z, x],
+        dst_ref=y_buf[p],
+        send_sem=y_s.at[p],
+        recv_sem=y_r.at[p],
+        device_id={"tensor": 1 - lax.axis_index("tensor")},
+        device_id_type=pl.DeviceIdType.MESH,
+    )
+
+    for v in (1 - x, x):
+        for w in order:
+            for p in range(parts):
+                load(p, w, v).start()
+    greet(z, x, core, z_size, x_size, pair)
+    for v in (1 - x, x):
+        for w in order:
+            for p in range(parts):
+                beside(p, w, v).start()
+    for w in order:
+        for p in range(parts):
+            load(p, w, 1 - x).wait()
+            beside(p, w, 1 - x).wait_recv()
+            add_into(c_buf[p].at[w, 1 - x], own[p].at[w, 1 - x])
+            across(p, w).start()
+    for k, w in enumerate(order):
+        for p in range(parts):
+            load(p, w, x).wait()
+            beside(p, w, x).wait_recv()
+            add_into(c_buf[p].at[w, x], own[p].at[w, x])
+            across(p, w).wait_recv()
+            if k < 3:
+
+                @pl.when(inner == 1)
+                def _():
+                    along(p, w, w, z).wait_recv()
+                    add_into(c_buf[p].at[w, x], x_buf[p].at[w], z_buf[p].at[w])
+
+                @pl.when(inner == 0)
+                def _():
+                    add_into(c_buf[p].at[w, x], x_buf[p].at[w])
+
+                @pl.when(w > z)
+                def _():
+                    along(p, w, w, z + 1).start()
+
+                @pl.when(w < z - 1)
+                def _():
+                    along(p, w, w, z - 1).start()
+
+                @pl.when(w == z - 1)
+                def _():
+                    along(p, w, z_size, z - 1).start()
+
+            else:
+                add_into(c_buf[p].at[w, x], x_buf[p].at[w])
+
+                @pl.when(z > 0)
+                def _():
+                    along(p, w, z, z).wait_recv()
+                    add_into(c_buf[p].at[w, x], z_buf[p].at[z])
+
+                @pl.when(z < z_size - 1)
+                def _():
+                    along(p, w, z_size, z).wait_recv()
+                    add_into(c_buf[p].at[w, x], z_buf[p].at[z_size])
+
+                if pair:
+                    twin(p).start()
+                else:
+                    outs[p][...] = c_buf[p][z, x].astype(outs[p].dtype)
+    if pair:
+        for p in range(parts):
+            twin(p).wait()
+            outs[p][...] = (
+                c_buf[p][z, x].astype(jnp.float32) + y_buf[p][...].astype(jnp.float32)
+            ).astype(outs[p].dtype)
+    for w in range(z_size):
+        for p in range(parts):
+            for v in range(x_size):
+                beside(p, w, v).wait_send()
+            across(p, w).wait_send()
+
+            @pl.when(z != w)
+            def _():
+                along(p, w, w, z).wait_send()
+
+
+def scatter_sums(arrays, x_size, collective_id, out_dtype, pair=False):
+    parts = len(arrays)
+    dma = pltpu.SemaphoreType.DMA
+    blocks = [a.shape[1:] for a in arrays]
+    return pl.pallas_call(
+        functools.partial(scatter_kernel, x_size, parts, pair),
+        out_shape=[jax.ShapeDtypeStruct(b, out_dtype) for b in blocks],
+        in_specs=[pl.BlockSpec(memory_space=pl.ANY)] * parts,
+        out_specs=[pl.BlockSpec(memory_space=pltpu.VMEM)] * parts,
+        scratch_shapes=[pltpu.VMEM((4, x_size) + b, a.dtype) for a, b in zip(arrays, blocks)]
+        + [pltpu.VMEM((4, x_size) + b, a.dtype) for a, b in zip(arrays, blocks)]
+        + [pltpu.VMEM((4,) + b, a.dtype) for a, b in zip(arrays, blocks)]
+        + [pltpu.VMEM((5,) + b, a.dtype) for a, b in zip(arrays, blocks)]
+        + ([pltpu.VMEM(b, a.dtype) for a, b in zip(arrays, blocks)] + [dma((parts,))] * 2 if pair else [])
+        + [dma((parts, 4, x_size))] * 3
+        + [dma((parts, 4))] * 3
+        + [dma((parts, 5))],
+        compiler_params=pltpu.CompilerParams(
+            collective_id=collective_id, has_side_effects=True, vmem_limit_bytes=VMEM_LIMIT
+        ),
+        name="scatter_sums",
+    )(*arrays)
+
+
+def pair_kernel(chunks, extras, left, right, *refs):
+    ins, total, outs = refs[:extras], refs[extras], refs[extras + 1 : 2 * extras + 1]
+    sent, got, refs = refs[2 * extras + 1], refs[2 * extras + 2], refs[2 * extras + 3 :]
+    e_got, (s_sem, r_sem, es_sem, er_sem) = refs[:extras], refs[extras:]
+    width = total.shape[1] // chunks
+    other = {"tensor": 1 - lax.axis_index("tensor")}
+    barrier = pltpu.get_barrier_semaphore()
+    pl.semaphore_signal(barrier, inc=1, device_id=other, device_id_type=pl.DeviceIdType.MESH)
+    pl.semaphore_wait(barrier, 1)
+
+    def copy(src, dst, send_sem, recv_sem):
+        return pltpu.make_async_remote_copy(
+            src_ref=src,
+            dst_ref=dst,
+            send_sem=send_sem,
+            recv_sem=recv_sem,
+            device_id=other,
+            device_id_type=pl.DeviceIdType.MESH,
+        )
+
+    chunk = lambda i: copy(sent.at[i], got.at[i], s_sem.at[i], r_sem.at[i])
+    extra = lambda i: copy(ins[i], e_got[i], es_sem.at[i], er_sem.at[i])
+    for i in range(extras):
+        extra(i).start()
+    for i in range(chunks):
+        sent[i] = lax.dot_general(
+            left[...],
+            right[pl.ds(i * width, width), :],
+            (((1,), (1,)), ((), ())),
+            preferred_element_type=jnp.float32,
+        ).astype(jnp.bfloat16)
+        chunk(i).start()
+    for i in range(extras):
+        extra(i).wait()
+        outs[i][...] = ins[i][...].astype(jnp.float32) + e_got[i][...].astype(jnp.float32)
+    for i in range(chunks):
+        chunk(i).wait()
+        total[:, pl.ds(i * width, width)] = sent[i].astype(jnp.float32) + got[i].astype(
+            jnp.float32
+        )
+
+
+def pair_product(left, right, extras, collective_id, chunks=8):
+    rows, columns = left.shape[0], right.shape[0]
+    dma = pltpu.SemaphoreType.DMA
+    vmem = pl.BlockSpec(memory_space=pltpu.VMEM)
+    block = pltpu.VMEM((chunks, rows, columns // chunks), jnp.bfloat16)
+    return pl.pallas_call(
+        functools.partial(pair_kernel, chunks, len(extras)),
+        out_shape=[jax.ShapeDtypeStruct((rows, columns), jnp.float32)]
+        + [jax.ShapeDtypeStruct(e.shape, jnp.float32) for e in extras],
+        in_specs=[vmem] * (2 + len(extras)),
+        out_specs=[vmem] * (1 + len(extras)),
+        scratch_shapes=[block, block]
+        + [pltpu.VMEM(e.shape, e.dtype) for e in extras]
+        + [dma((chunks,))] * 2
+        + [dma((max(1, len(extras)),))] * 2,
+        compiler_params=pltpu.CompilerParams(
+            collective_id=collective_id, has_side_effects=True, vmem_limit_bytes=VMEM_LIMIT
+        ),
+        name="pair_product",
+    )(left, right, *extras)
+
+
+def tuned():
+    return lax.axis_size("dp") == 16 and lax.axis_size("tensor") == 2
+
+
+def gather_all(arrays):
+    if tuned():
+        return gather_rows(arrays, 4, 2, 1)
+    return [lax.all_gather(a, "dp") for a in arrays]
+
+
+def sum_home(arrays, collective_id, pair=False):
+    if tuned():
+        return scatter_sums(arrays, 2, collective_id, jnp.float32, pair)
+    sums = [lax.psum_scatter(a, "dp", scatter_dimension=0) for a in arrays]
+    if pair:
+        sums = [lax.psum(a.astype(jnp.float32), "tensor") for a in sums]
+    return [a.astype(jnp.float32) for a in sums]
+
+
+def product_sum(left, right, extras, collective_id):
+    if tuned():
+        return pair_product(left, right, extras, collective_id)
+    product = contract_last(left, right).astype(jnp.bfloat16)
+    return [lax.psum(a, "tensor").astype(jnp.float32) for a in [product] + extras]
 
 
 def shards(
@@ -156,9 +577,7 @@
     attn_weights = (expo / total).astype(jnp.bfloat16)
     context = jnp.einsum("hts,shd->thd", attn_weights, value, preferred_element_type=jnp.float32)
     context = context.astype(jnp.bfloat16).reshape(rows_here, heads_local * VALUE_HEAD_SIZE)
-    attn = lax.psum(contract_last(context, w_out).astype(jnp.bfloat16), "tensor").astype(
-        jnp.float32
-    )
+    (attn,) = product_sum(context, w_out, [], 2)
     hidden = tokens_f + attn
     ffn_normed, ffn_unit, ffn_factor = rms_normalize_pieces(hidden, g_ffn)
     ffn_bf = ffn_normed.astype(jnp.bfloat16)
@@ -166,11 +585,14 @@
     own = lax.axis_index("dp")
 
     everyone_grad = lax.all_gather(grad_out, "dp", tiled=True)
-    everyone_routes = lax.all_gather(routes, "dp", tiled=True)
-    everyone_ffn = lax.all_gather(ffn_bf, "dp", tiled=True)
-    everyone_probs = lax.all_gather(router_probs, "dp", tiled=True)
-    chooses = jnp.any(everyone_routes == own, axis=1).reshape(devices, rows_here)
-    own_probs = lax.dynamic_slice_in_dim(everyone_probs, own, 1, 1).reshape(devices, rows_here)
+    named = jnp.any(routes[:, :, None] == jnp.arange(128, dtype=jnp.int32)[None, None, :], axis=1)
+    dense_gates = jnp.where(
+        named, jnp.pad(router_probs, ((0, 0), (0, 128 - experts))), -1.0
+    )
+    everyone_ffn, everyone_gates = gather_all([ffn_bf, dense_gates])
+    everyone_ffn = everyone_ffn.reshape(devices * rows_here, features)
+    own_probs = lax.dynamic_slice_in_dim(everyone_gates, own, 1, 2).reshape(devices, rows_here)
+    chooses = own_probs >= 0.0
     own_gates = jnp.where(chooses, own_probs, 0.0)
     upto = (places[:, None] <= places[None, :]).astype(jnp.bfloat16)
     slot = jnp.dot(chooses.astype(jnp.bfloat16), upto, preferred_element_type=jnp.float32) - 1.0
@@ -274,13 +696,15 @@
     grad_ffn_in = put_rows(
         grad_rows_in, [grad_shared_gate_pre, grad_shared_up_pre], [part_gate, part_up]
     )
-    grad_ffn_sum = lax.psum_scatter(
-        jnp.concatenate([grad_ffn_in, pair_columns.astype(jnp.bfloat16)], axis=1),
-        "dp",
-        scatter_dimension=0,
-        tiled=True,
-    )
-    grad_ffn_sum = lax.psum(grad_ffn_sum.astype(jnp.float32), "tensor")
+    (grad_ffn_sum,) = sum_home(
+        [
+            jnp.concatenate([grad_ffn_in, pair_columns.astype(jnp.bfloat16)], axis=1).reshape(
+                devices, rows_here, features + 128
+            )
+        ],
+        3,
+        True,
+    )
     dense_grad = (
         grad_ffn_sum[:, features : features + experts]
         + grad_ffn_sum[:, features + experts : features + 2 * experts]
@@ -289,7 +713,7 @@
         dense_grad - jnp.sum(router_probs * dense_grad, axis=-1, keepdims=True)
     )
     grad_router_in = contract_last(grad_logits, router, highest)
-    grad_router_part = contract_first(ffn_normed, grad_logits, highest) / lax.axis_size("tensor")
+    grad_router_part = contract_first(ffn_normed, grad_logits, highest)
     grad_ffn_total = grad_ffn_sum[:, :features] + grad_router_in
     grad_g_ffn = jnp.sum(grad_ffn_total * ffn_unit, axis=0)
     grad_hidden = grad_top + normalize_back(grad_ffn_total, ffn_unit, ffn_factor, g_ffn)
@@ -329,7 +753,6 @@
     )
     grad_query = grad_query.reshape(rows_here, heads_local * QK).astype(jnp.bfloat16)
     grad_w_query = contract_first(normed_bf, grad_query)
-    grad_in_query = contract_last(grad_query, w_query)
     grad_key_value = (
         jnp.concatenate([grad_key_nope, grad_value], axis=-1)
         .reshape(rows_here, heads_local * (PLAIN_HEAD_SIZE + VALUE_HEAD_SIZE))
@@ -337,17 +760,16 @@
     )
     grad_w_kv_up = contract_first(latent_bf, grad_key_value)
     grad_latent_normed = contract_last(grad_key_value, key_value_up_weight)
-    grad_g_kv_part = jnp.sum(grad_latent_normed * latent_unit_scale, axis=0)
+    grad_latent_part = jnp.concatenate(
+        [grad_latent_normed, apply_rotation(grad_key_rot, -token_position)], axis=1
+    ).astype(jnp.bfloat16)
+    grad_in_summed, grad_latent_sum = product_sum(grad_query, w_query, [grad_latent_part], 4)
+    grad_latent_normed = grad_latent_sum[:, :LATENT_RANK]
+    grad_g_kv = jnp.sum(grad_latent_normed * latent_unit_scale, axis=0)
     grad_latent = normalize_back(
         grad_latent_normed, latent_unit_scale, latent_norm_factor, latent_norm_gain
     )
-    grad_down_part = jnp.concatenate(
-        [grad_latent, apply_rotation(grad_key_rot, -token_position)], axis=1
-    )
-    grad_in_summed, grad_down = (
-        lax.psum(grad_in_query.astype(jnp.bfloat16), "tensor").astype(jnp.float32),
-        lax.psum(grad_down_part.astype(jnp.bfloat16), "tensor").astype(jnp.float32),
-    )
+    grad_down = jnp.concatenate([grad_latent, grad_latent_sum[:, LATENT_RANK:]], axis=1)
     grad_down_bf = grad_down.astype(jnp.bfloat16)
     share = grad_down.shape[1] // lax.axis_size("tensor")
     grad_columns = lax.dynamic_slice_in_dim(
@@ -357,41 +779,43 @@
     grad_attn_in = grad_in_summed + contract_last(grad_down_bf, key_value_down_weight)
     grad_g_attn = jnp.sum(grad_attn_in * attn_unit, axis=0)
     grad_tokens = grad_hidden + normalize_back(grad_attn_in, attn_unit, attn_factor, g_attn)
-    summed = (
-        lax.psum_scatter(
-            grad_w_query.astype(jnp.bfloat16), "dp", scatter_dimension=0, tiled=True
-        ).astype(jnp.float32),
-        lax.psum_scatter(
-            grad_w_kv_down.astype(jnp.bfloat16), "dp", scatter_dimension=0, tiled=True
-        ).astype(jnp.float32),
-        lax.psum_scatter(
-            grad_w_kv_up.astype(jnp.bfloat16), "dp", scatter_dimension=0, tiled=True
-        ).astype(jnp.float32),
-        lax.psum_scatter(
-            grad_w_out.astype(jnp.bfloat16), "dp", scatter_dimension=0, tiled=True
-        ).astype(jnp.float32),
-        lax.psum_scatter(
-            grad_g_attn.astype(jnp.bfloat16), "dp", scatter_dimension=0, tiled=True
-        ).astype(jnp.float32),
-        lax.psum_scatter(
-            grad_g_ffn.astype(jnp.bfloat16), "dp", scatter_dimension=0, tiled=True
-        ).astype(jnp.float32),
-    )
-    everywhere = (
-        lax.psum_scatter(grad_router_part, ("dp", "tensor"), scatter_dimension=0, tiled=True),
-        lax.psum_scatter(grad_g_kv_part, ("dp", "tensor"), scatter_dimension=0, tiled=True),
+    vectors = jnp.concatenate(
+        [
+            grad_router_part,
+            grad_g_attn[:, None],
+            grad_g_ffn[:, None],
+            jnp.pad(
+                grad_g_kv.reshape(devices, -1), ((0, 0), (0, share_rows - LATENT_RANK // devices))
+            ).reshape(-1, 1),
+            jnp.zeros((features, 128 - experts - 3), jnp.float32),
+        ],
+        axis=1,
+    )
+    blocks = [
+        a.astype(jnp.bfloat16).reshape(devices, a.shape[0] // devices, a.shape[1])
+        for a in (grad_w_query, grad_w_out, grad_w_kv_up, grad_w_kv_down)
+    ]
+    grad_w_query, grad_w_out, grad_w_kv_up, grad_w_kv_down, vectors = sum_home(
+        blocks + [vectors.reshape(devices, share_rows, 128)], 5
+    )
+    rank, ranks = lax.axis_index("tensor"), lax.axis_size("tensor")
+    router_rows = share_rows // ranks
+    grad_router = lax.dynamic_slice_in_dim(vectors[:, :experts], rank * router_rows, router_rows, 0)
+    latent_rows = LATENT_RANK // devices // ranks
+    grad_g_kv = lax.dynamic_slice_in_dim(
+        vectors[:, experts + 2], rank * latent_rows, latent_rows, 0
     )
     return (
         output,
         grad_tokens,
-        summed[4],
-        summed[0],
-        summed[1],
-        everywhere[1],
-        summed[2],
-        summed[3],
-        summed[5],
-        everywhere[0],
+        vectors[:, experts],
+        grad_w_query,
+        grad_w_kv_down,
+        grad_g_kv,
+        grad_w_kv_up,
+        grad_w_out,
+        vectors[:, experts + 1],
+        grad_router,
         grad_shared_gate,
         grad_shared_up,
         grad_shared_down,

time: 1350 us -> 961 us (0.71)
  waiting for transfers between devices: 712 us -> 20.3 us
  Pallas kernels: 0 us -> 472 us
  blocking collectives: 188 us -> 0 us
  local copies, waits for them, and re-layouts: 48.5 us -> 98.6 us
  matrix products: 295 us -> 272 us
    pallas_call x0 -> x5, Pallas kernels: none -> 472 us  [the longest x2 253 us: scatter_sums(): pl.pallas_call(functools.partial(scatter_kernel, x_size, parts, pair), ou...]
    reduce_scatter x4 -> x0, waiting for transfers between devices: 326 us -> none  [the longest x1 148 us: shards(): lax.psum_scatter(jnp.concatenate([grad_ffn_in, pair_columns.astype(jnp.bf...]
    all_gather x1 -> x0, waiting for transfers between devices: 104 us -> none  [shards(): everyone_ffn = lax.all_gather(ffn_bf, 'dp', tiled=True)]
    unnamed x13 -> x3, waiting for transfers between devices: 74.6 us -> 0.71 us
    reduce_scatter x1, waiting for transfers between devices: 71.8 us -> 0.02 us  [shards(): lax.psum_scatter(ffn_part, 'dp', scatter_dimension=0, tiled=True)]
    unnamed x2 -> x0, blocking collectives: 70.1 us -> none
    all_gather x2 -> x0, blocking collectives: 61.4 us -> none  [the longest x1 39 us: shards(): everyone_probs = lax.all_gather(router_probs, 'dp', tiled=True)]
    psum x1 -> x0, blocking collectives: 56.6 us -> none  [shards(): grad_ffn_sum = lax.psum(grad_ffn_sum.astype(jnp.float32), 'tensor')]
  transfers between devices with their start and end apart: 12 -> 4, of which waited for: 11 -> 1; matrix products, arithmetic and copies ran while one was open for 17% -> 29% of each run, Pallas kernels for 0% -> 36%
where the time goes in v2:
time: 961 us; the launch traced here: 950 us
  Pallas kernels  472 us (49%)
  matrix products  272 us (28%)
  local copies, waits for them, and re-layouts  98.6 us (10%)
  other arithmetic  68 us (7%)
  waiting for transfers between devices  20.3 us (2%)
  between operations  15.2 us (2%)
    pallas_call x2, Pallas kernels, scatter_sums(): pl.pallas_call(functools.partial(scatter_kernel, x_size, parts, pair), ou...  253 us
    pallas_call x1, Pallas kernels, gather_rows(): pl.pallas_call(functools.partial(gather_kernel, z_size, x_size, count), o...  151 us
    pallas_call x2, Pallas kernels, pair_product(): pl.pallas_call(functools.partial(pair_kernel, chunks, len(extras)), out_s...  67.6 us
    dot_general x11, matrix products, contract_first(): lax.dot_general(left, right, (((0,), (0,)), ((), ())), precision=precisio...  66.8 us
    dot_general x6, matrix products, contract_last(): lax.dot_general(left, right, (((1,), (1,)), ((), ())), precision=precisio...  46.1 us
    dot_general x2, matrix products, put_rows(): jnp.einsum('jtk,jkc->jtc', left, right, preferred_element_type=jnp.float32)  30.3 us
    unnamed x204, local copies, waits for them, and re-layouts  24.4 us
    dot_general x2, matrix products, pick_rows(): jnp.einsum('jst,jtc->jsc', pick, blocks, preferred_element_type=jnp.float32)  22.9 us
  transfers between devices with their start and end apart: 4, of which 1 were waited for; matrix products, arithmetic and copies ran while one was open for 29% of the time, Pallas kernels for 36%

profile of v2, /device:TPU:0, one launch (start us, length us, event | category | flops | bytes accessed | tf_op | source)
XLA Modules:
  0.0 950.3 jit_solution(1688271346406070042)
XLA Ops:
  25.7 5.9 fusion.167
  37.0 30.8 %pair_product.2 = f32[256,2048]{1,0:T(8,128)} custom-call(bf16[256,1024]{1,0:T(8,128)(2,1)} %copy.238.left, bf16[2048,1024]{1,0:T(8,128)(2,1)} %right.2), custom_call_target="tpu_custom_call" | custom-call | tf_op jit(solution)/shard_map/pair_product/pallas_call | solution.py:454
  85.6 150.7 %gather_rows.1 = (bf16[16,256,2048]{2,1,0:T(8,128)(2,1)}, f32[16,256,128]{2,1,0:T(8,128)}) custom-call(bf16[256,2048]{1,0:T(8,128)(2,1)} %multiply_convert_fusion.5.refs_0_, f32[256,128]{1,0:T(8,128)} %pad_select_fusion.refs_1_), custom_call_target="tpu_custom_call" | custom-call | tf_op jit(solution)/shard_map/gather_rows/pallas_call | solution.py:232
  240.6 12.5 %fusion.132 = f32[4096,88]{0,1:T(8,128)} fusion(bf16[4096,2048]{1,0:T(8,128)(2,1)} %bitcast.174, bf16[2048,1408]{1,0:T(8,128)(2,1)} %param.31, s32[]{:T(128)S(6)} %select_n.60), kind=kOutput, calls=%fused_computation.171 | convolution fusion | flops 1476395008 | bytes 18743300 | tf_op jit(solution)/shard_map/dot_general | solution.py:656
  253.1 11.6 %convolution_convert_fusion.2 = bf16[16,128,2048]{2,1,0:T(8,128)(2,1)} fusion(bf16[16,256,2048]{2,1,0:T(8,128)(2,1)} %get-tuple-element.26, f32[16,256]{1,0:T(8,128)S(1)} %convolution_add_fusion.2, pred[16,256]{1,0:T(8,128)(4,1)S(1)} %get-tuple-element.109), kind=kOutput, calls=%fused_computation.29 | convolution fusion | flops 2152726528 | bytes 25186304 | tf_op jit(solution)/shard_map/jst,jtc->jsc/dot_general | solution.py:606
  264.7 9.4 fusion.34
  276.6 9.1 multiply_convert_fusion.3
  285.8 11.3 %convolution_convert_fusion.1 = bf16[16,128,2048]{2,1,0:T(8,128)(2,1)} fusion(bf16[16,256,2048]{2,1,0:T(8,128)(2,1)} %bitcast.173, f32[16,256]{1,0:T(8,128)S(1)} %convolution_add_fusion.2, pred[16,256]{1,0:T(8,128)(4,1)S(1)} %get-tuple-element.109), kind=kOutput, calls=%fused_computation.28 | convolution fusion | flops 2152726528 | bytes 25186304 | tf_op jit(solution)/shard_map/jst,jtc->jsc/dot_general | solution.py:606
  297.1 12.8 %convolution_bitcast_fusion = f32[4096,88]{0,1:T(8,128)} fusion(bf16[4096,2048]{1,0:T(8,128)(2,1)} %all-gather.2.cloned.1.call-done, bf16[2048,1408]{1,0:T(8,128)(2,1)} %param.32, s32[]{:T(128)S(6)} %select_n.60), kind=kOutput, calls=%fused_computation.30 | convolution fusion | flops 1476395008 | bytes 18743300 | tf_op jit(solution)/shard_map/dot_general | solution.py:659
  309.9 13.8 %multiply_convert_fusion.7 = (bf16[4096,88]{0,1:T(8,128)(2,1)}, bf16[4096,88]{0,1:T(8,128)(2,1)}, bf16[4096,88]{0,1:T(8,128)(2,1)}) fusion(f32[4096,88]{0,1:T(8,128)} %convolution_bitcast_fusion, f32[4096,88]{0,1:T(8,128)} %fusion.132, bf16[4096,2048]{1,0:T(8,128)(2,1)} %bitcast.175, bf16[2048,1408]{1,0:T(8,128)(2,1)} %param.30, s32[]{:T(128)S(6)} %select_n.60), kind=kOutput, calls=%fused_computation.111 | convolution fusion | flops 1481801728 | bytes 22347780 | tf_op jit(solution)/shard_map/dot_general | solution.py:655
  324.9 14.1 %fusion.8 = (f32[2048]{0:T(1024)S(1)}, f32[2048,2048]{1,0:T(8,128)}) fusion(bf16[16,128,2048]{2,1,0:T(8,128)(2,1)} %convolution_convert_fusion.1, bf16[2048,704]{0,1:T(8,128)(2,1)} %get-tuple-element.145, bf16[1,2048,704]{1,2,0:T(8,128)(2,1)S(1)} %copy-done), kind=kOutput, calls=%fused_computation.12 | convolution fusion | flops 5918160896 | bytes 30941184 | tf_op jit(solution)/shard_map/dot_general | solution.py:56
  340.1 11.2 %fusion.9 = (bf16[2048,2048]{1,0:T(8,128)(2,1)}, bf16[2048,2048]{1,0:T(8,128)(2,1)S(1)}) fusion(bf16[16,128,2048]{2,1,0:T(8,128)(2,1)S(1)} %bitcast.180, f32[2048]{0:T(1024)S(1)} %bitcast.217, f32[2048,2048]{1,0:T(8,128)} %get-tuple-element.148), kind=kLoop, calls=%fused_computation.13 | loop fusion | flops 20971520 | bytes 41951232 | tf_op jit(solution)/shard_map/convert_element_type | solution.py:633
  354.6 12.5 %fusion.14 = bf16[16,256,2048]{2,1,0:T(8,128)(2,1)} fusion(bf16[16,88,2048]{2,1,0:T(8,128)(2,1)} %broadcast_in_dim.118, bf16[16,128,2048]{2,1,0:T(8,128)(2,1)S(1)} %bitcast.191, bf16[16,256,88]{1,2,0:T(8,128)(2,1)S(1)} %bitcast.216, bf16[16,256,128]{1,2,0:T(8,128)(2,1)S(1)} %copy-done.42), kind=kOutput, calls=%fused_computation.20 | convolution fusion | flops 3664117760 | bytes 32702464 | tf_op jit(solution)/shard_map/jtk,jkc->jtc/dot_general | solution.py:626
  367.1 22.5 %copy.215 = bf16[2048,4096]{1,0:T(8,128)(2,1)} copy(bf16[2048,4096]{0,1:T(8,128)(2,1)} %bitcast.176) | data formatting | bytes 33554432 | tf_op jit(solution)/shard_map/dot_general | solution.py:66
  393.8 9.0 fusion.98
  405.6 5.2 convolution_convert_fusion.11
  410.8 5.2 convolution_convert_fusion.12
  426.5 8.1 fusion.7
  434.5 13.2 %multiply_convert_fusion.1 = (bf16[2048,704]{0,1:T(8,128)(2,1)S(1)}, bf16[2048,704]{0,1:T(8,128)(2,1)S(1)}) fusion(f32[2048,704]{0,1:T(8,128)} %copy-done.89, f32[2048,704]{0,1:T(8,128)} %get-tuple-element.146, bf16[2048,2048]{1,0:T(8,128)(2,1)} %bitcast.188, bf16[1,2048,704]{1,2,0:T(8,128)(2,1)S(1)} %copy-done), kind=kOutput, calls=%fused_computation.23 | convolution fusion | flops 5924323328 | bytes 28573696 | tf_op jit(solution)/shard_map/dot_general | solution.py:642
  447.8 10.4 %fusion.32 = f32[2048,2048]{1,0:T(8,128)} fusion(bf16[2048,704]{0,1:T(8,128)(2,1)S(1)} %get-tuple-element.113, bf16[1,2048,704]{1,2,0:T(8,128)(2,1)S(1)} %copy-done.85), kind=kOutput, calls=%fused_computation.50 | convolution fusion | flops 5905580032 | bytes 22544384 | tf_op jit(solution)/shard_map/dot_general | solution.py:56
  458.3 12.9 %add_convert_fusion = bf16[2048,2048]{1,0:T(8,128)(2,1)} fusion(f32[2048,2048]{1,0:T(8,128)} %fusion.32, bf16[2048,704]{0,1:T(8,128)(2,1)S(1)} %get-tuple-element.112, bf16[1,2048,704]{1,2,0:T(8,128)(2,1)S(1)} %copy-done.87), kind=kOutput, calls=%fused_computation.14 | convolution fusion | flops 5913968640 | bytes 30932992 | tf_op jit(solution)/shard_map/dot_general | solution.py:56
  477.7 17.8 %fusion.17 = bf16[16,256,2048]{2,1,0:T(8,128)(2,1)} fusion(bf16[16,88,2048]{2,1,0:T(8,128)(2,1)} %broadcast_in_dim.120, bf16[16,88,2048]{2,1,0:T(8,128)(2,1)} %broadcast_in_dim.119, bf16[16,128,2048]{2,1,0:T(8,128)(2,1)} %bitcast.222, bf16[16,256,88]{1,2,0:T(8,128)(2,1)S(1)} %copy-done.45, bf16[16,256,88]{1,2,0:T(8,128)(2,1)} %get-tuple-element.156, ...), kind=kOutput, calls=%fused_computation.21 | convolution fusion | flops 5175902208 | bytes 39190528 | tf_op jit(solution)/shard_map/jtk,jkc->jtc/dot_general | solution.py:626
  495.6 14.5 %pad_maximum_fusion.refs_0_ = bf16[16,256,2176]{2,1,0:T(8,128)(2,1)} fusion(bf16[16,256,128]{2,1,0:T(8,128)(2,1)S(1)} %copy-done.16, bf16[16,256,2048]{2,1,0:T(8,128)(2,1)} %fusion.17), kind=kLoop, calls=%fused_computation.7 | loop fusion | flops 35651584 | bytes 35651584 | tf_op jit(solution)/shard_map/concatenate | solution.py:701
  510.1 164.2 %scatter_sums.2 = f32[256,2176]{1,0:T(8,128)} custom-call(bf16[16,256,2176]{2,1,0:T(8,128)(2,1)} %pad_maximum_fusion.refs_0_), custom_call_target="tpu_custom_call" | custom-call | tf_op jit(solution)/shard_map/scatter_sums/pallas_call | solution.py:387
  675.6 11.4 %convolution_bitcast_fusion.2 = f32[1,2048,704]{1,2,0:T(8,128)} fusion(bf16[2048,704]{0,1:T(8,128)(2,1)} %copy-done.92, bf16[2048,2048]{1,0:T(8,128)(2,1)} %bitcast.184), kind=kOutput, calls=%fused_computation.33 | convolution fusion | flops 5905580032 | bytes 17039360 | tf_op jit(solution)/shard_map/dot_general | solution.py:66
  686.9 10.2 %convolution_bitcast_fusion.3 = f32[1,2048,704]{1,2,0:T(8,128)} fusion(bf16[2048,704]{0,1:T(8,128)(2,1)S(1)} %copy-done.91, bf16[2048,2048]{1,0:T(8,128)(2,1)} %bitcast.185), kind=kOutput, calls=%fused_computation.34 | convolution fusion | flops 5905580032 | bytes 17039360 | tf_op jit(solution)/shard_map/dot_general | solution.py:66
  697.2 8.3 convolution_bitcast_fusion.1
  705.7 5.3 multiply_reduce_fusion
  712.4 5.6 fusion.59
  726.0 19.6 %all-reduce.4.cloned.1.call-done = bf16[256,2048]{1,0:T(8,128)(2,1)} async-done(((bf16[256,2048]{1,0:T(8,128)(2,1)}), bf16[256,2048]{1,0:T(8,128)(2,1)}) %all-reduce.4.cloned.1.call-update) | async-done | bytes 1048592 | tf_op jit(solution)/shard_map/psum | solution.py:684
  777.2 36.8 %pair_product.3 = (f32[256,2048]{1,0:T(8,128)}, f32[256,576]{1,0:T(8,128)}) custom-call(bf16[256,1536]{1,0:T(8,128)(2,1)} %copy.209.left, bf16[2048,1536]{1,0:T(8,128)(2,1)} %right.3, bf16[256,576]{1,0:T(8,128)(2,1)} %pad_maximum_fusion.6.refs_0_), custom_call_target="tpu_custom_call" | custom-call | tf_op jit(solution)/shard_map/pair_product/pallas_call | solution.py:454
  842.0 89.2 %scatter_sums.3 = (f32[128,1536]{1,0:T(8,128)}, f32[128,1024]{1,0:T(8,128)}, f32[32,2048]{1,0:T(8,128)}, f32[128,288]{1,0:T(8,128)}, f32[128,128]{1,0:T(8,128)}) custom-call(bf16[16,128,1536]{2,1,0:T(8,128)(2,1)} %bitcast.181, bf16[16,128,1024]{2,1,0:T(8,128)(2,1)} %bitcast.182, bf16[16,32,2048]{2,1,0:T(8,128)(2,1)} %bitcast.192, ...), custom_call_target="tpu_custom_call" | custom-call | tf_op jit(solution)/shard_map/scatter_sums/pallas_call | solution.py:387
  (313 shorter events, 160.0 us)
Async XLA Ops:
  7.2 317.7 %copy-start = (bf16[1,2048,704]{1,2,0:T(8,128)(2,1)S(1)}, bf16[1,2048,704]{1,2,0:T(8,128)(2,1)}, u32[]{:S(2)}) copy-start(bf16[1,2048,704]{1,2,0:T(8,128)(2,1)} %param.35) | copy-start | bytes 8650756
  7.2 278.6 %all-gather.2.cloned.1.call-start = ((), (), s32[]{:S(2)}) async-start(), calls=%async_computation.4 | async-start | bytes 17825792 | tf_op jit(solution)/shard_map/all_gather | solution.py:587
  7.9 697.6 %reduce-scatter.2.cloned.1.call-start = ((), (), s32[]{:S(2)}) async-start(), calls=%async_computation.2 | async-start | bytes 17825792 | tf_op jit(solution)/shard_map/reduce_scatter | solution.py:683
  11.3 14.4 %copy-start.65 = (f32[256]{0:T(256)}, f32[256]{0:T(256)S(1)}, u32[]{:S(2)}) copy-start(f32[256]{0:T(256)S(1)} %add_rsqrt_fusion.2) | copy-start | bytes 3076
  37.0 30.8 %copy-start.5 = (bf16[256,2048]{1,0:T(8,128)(2,1)S(1)}, bf16[256,2048]{1,0:T(8,128)(2,1)}, u32[]{:S(2)}) copy-start(bf16[256,2048]{1,0:T(8,128)(2,1)} %param.18) | copy-start | bytes 3145732
  73.6 12.0 %copy-start.30 = (f32[256,16]{1,0:T(8,128)}, f32[256,16]{1,0:T(8,128)S(1)}, u32[]{:S(2)}) copy-start(f32[256,16]{1,0:T(8,128)S(1)} %copy.187) | copy-start | bytes 49156
  253.1 11.6 %copy-start.84 = (bf16[1,2048,704]{1,2,0:T(8,128)(2,1)S(1)}, bf16[1,2048,704]{1,2,0:T(8,128)(2,1)}, u32[]{:S(2)}) copy-start(bf16[1,2048,704]{1,2,0:T(8,128)(2,1)} %param.33) | copy-start | bytes 8650756
  264.7 11.9 %copy-start.11 = (bf16[16,128,2048]{2,1,0:T(8,128)(2,1)S(1)}, bf16[16,128,2048]{2,1,0:T(8,128)(2,1)}, u32[]{:S(2)}) copy-start(bf16[16,128,2048]{2,1,0:T(8,128)(2,1)} %convolution_convert_fusion.2) | copy-start | bytes 25165828
  264.7 11.9 %copy-start.86 = (bf16[1,2048,704]{1,2,0:T(8,128)(2,1)S(1)}, bf16[1,2048,704]{1,2,0:T(8,128)(2,1)}, u32[]{:S(2)}) copy-start(bf16[1,2048,704]{1,2,0:T(8,128)(2,1)} %param.34) | copy-start | bytes 8650756
  324.9 15.2 %slice-start = ((s8[8388608]{0:T(1024)(128)(4,1)}), s8[4194304]{0:T(1024)(128)(4,1)S(1)}, s32[]{:S(2)}) async-start(s8[8388608]{0:T(1024)(128)(4,1)} %bitcast.179), calls=%async_computation.5 | async-start | bytes 8388608
  324.9 15.2 %slice-start.1 = ((s8[8388608]{0:T(1024)(128)(4,1)}), s8[4194304]{0:T(1024)(128)(4,1)S(1)}, s32[]{:S(2)}) async-start(s8[8388608]{0:T(1024)(128)(4,1)} %bitcast.179), calls=%async_computation.6 | async-start | bytes 8388608
  340.1 11.2 %copy-start.41 = (bf16[88,2048]{1,0:T(8,128)(2,1)S(1)}, bf16[88,2048]{1,0:T(8,128)(2,1)}, u32[]{:S(2)}) copy-start(bf16[88,2048]{1,0:T(8,128)(2,1)} %copy.189) | copy-start | bytes 1081348
  393.8 11.6 %copy-start.2 = (bf16[2048,4096]{1,0:T(8,128)(2,1)S(1)}, bf16[2048,4096]{1,0:T(8,128)(2,1)}, u32[]{:S(2)}) copy-start(bf16[2048,4096]{1,0:T(8,128)(2,1)} %copy.215) | copy-start | bytes 50331652
  393.8 11.7 %copy-start.23 = (bf16[4096,88]{0,1:T(8,128)(2,1)S(1)}, bf16[4096,88]{0,1:T(8,128)(2,1)}, u32[]{:S(2)}) copy-start(bf16[4096,88]{0,1:T(8,128)(2,1)} %get-tuple-element.115) | copy-start | bytes 2162692
  417.1 300.8 %all-to-all-start = ((bf16[16,128,264]{1,2,0:T(8,128)(2,1)}), bf16[16,128,264]{1,2,0:T(8,128)(2,1)}, u32[]{:S(2)}, u32[]{:S(2)}) async-start(bf16[16,128,264]{1,2,0:T(8,128)(2,1)} %pad_maximum_fusion.1), calls=%async_computation.1 | async-start | bytes 2162688 | tf_op jit(solution)/shard_map/all_to_all | solution.py:671
  421.6 323.9 %all-reduce.4.cloned.1.call-start = ((), (), s32[]{:S(2)}) async-start(), calls=%async_computation.3 | async-start | bytes 2097152 | tf_op jit(solution)/shard_map/psum | solution.py:684
  434.5 13.3 %copy-start.85 = (bf16[1,2048,704]{1,2,0:T(8,128)(2,1)S(1)}, bf16[1,2048,704]{1,2,0:T(8,128)(2,1)}, u32[]{:S(2)}) copy-start(bf16[1,2048,704]{1,2,0:T(8,128)(2,1)} %param.33) | copy-start | bytes 8650756
  447.8 10.5 %copy-start.90 = (bf16[2048,704]{0,1:T(8,128)(2,1)}, bf16[2048,704]{0,1:T(8,128)(2,1)S(1)}, u32[]{:S(2)}) copy-start(bf16[2048,704]{0,1:T(8,128)(2,1)S(1)} %get-tuple-element.113) | copy-start | bytes 8650756
  447.8 10.5 %copy-start.92 = (bf16[2048,704]{0,1:T(8,128)(2,1)}, bf16[2048,704]{0,1:T(8,128)(2,1)S(1)}, u32[]{:S(2)}) copy-start(bf16[2048,704]{0,1:T(8,128)(2,1)S(1)} %get-tuple-element.112) | copy-start | bytes 8650756
  447.8 10.4 %copy-start.87 = (bf16[1,2048,704]{1,2,0:T(8,128)(2,1)S(1)}, bf16[1,2048,704]{1,2,0:T(8,128)(2,1)}, u32[]{:S(2)}) copy-start(bf16[1,2048,704]{1,2,0:T(8,128)(2,1)} %param.34) | copy-start | bytes 8650756
  458.3 12.9 %copy-start.39 = (bf16[88,2048]{1,0:T(8,128)(2,1)S(1)}, bf16[88,2048]{1,0:T(8,128)(2,1)}, u32[]{:S(2)}) copy-start(bf16[88,2048]{1,0:T(8,128)(2,1)} %copy.193) | copy-start | bytes 1081348
  477.7 17.8 %copy-start.16 = (bf16[16,256,128]{2,1,0:T(8,128)(2,1)S(1)}, bf16[16,256,128]{2,1,0:T(8,128)(2,1)}, u32[]{:S(2)}) copy-start(bf16[16,256,128]{2,1,0:T(8,128)(2,1)} %select_convert_fusion) | copy-start | bytes 3145732
  510.0 164.2 %copy-start.31 = (f32[256,16]{1,0:T(8,128)S(1)}, f32[256,16]{1,0:T(8,128)}, u32[]{:S(2)}) copy-start(f32[256,16]{1,0:T(8,128)} %copy-done.30) | copy-start | bytes 49156
  510.0 164.2 %copy-start.76 = (f32[256]{0:T(256)S(1)}, f32[256]{0:T(256)}, u32[]{:S(2)}) copy-start(f32[256]{0:T(256)} %get-tuple-element.143) | copy-start | bytes 3076
  510.1 164.2 %copy-start.78 = (f32[256]{0:T(256)S(1)}, f32[256]{0:T(256)}, u32[]{:S(2)}) copy-start(f32[256]{0:T(256)} %copy-done.77) | copy-start | bytes 3076
  675.5 11.4 %copy-start.91 = (bf16[2048,704]{0,1:T(8,128)(2,1)S(1)}, bf16[2048,704]{0,1:T(8,128)(2,1)}, u32[]{:S(2)}) copy-start(bf16[2048,704]{0,1:T(8,128)(2,1)} %copy-done.90) | copy-start | bytes 8650756
  675.5 21.6 %slice-start.2 = ((s8[8388608]{0:T(1024)(128)(4,1)}), s8[4194304]{0:T(1024)(128)(4,1)S(1)}, s32[]{:S(2)}) async-start(s8[8388608]{0:T(1024)(128)(4,1)} %bitcast.189), calls=%async_computation.7 | async-start | bytes 8388608
  777.1 36.9 %copy-start.13 = (f32[256,576]{1,0:T(8,128)S(1)}, f32[256,576]{1,0:T(8,128)}, u32[]{:S(2)}) copy-start(f32[256,576]{1,0:T(8,128)} %copy-done.12) | copy-start | bytes 1769476
  777.1 36.9 %copy-start.70 = (f32[512]{0:T(512)S(1)}, f32[512]{0:T(512)}, u32[]{:S(2)}) copy-start(f32[512]{0:T(512)} %param.25) | copy-start | bytes 6148
  777.1 36.9 %copy-start.75 = (f32[256]{0:T(256)S(1)}, f32[256]{0:T(256)}, u32[]{:S(2)}) copy-start(f32[256]{0:T(256)} %copy-done.74) | copy-start | bytes 3076
  777.1 39.1 %copy-start.8 = (f32[256,2048]{1,0:T(8,128)S(1)}, f32[256,2048]{1,0:T(8,128)}, u32[]{:S(2)}) copy-start(f32[256,2048]{1,0:T(8,128)} %copy-done.7) | copy-start | bytes 6291460
  777.1 39.1 %copy-start.27 = (bf16[8,128,256]{2,1,0:T(8,128)(2,1)S(1)}, bf16[8,128,256]{2,1,0:T(8,128)(2,1)}, u32[]{:S(2)}) copy-start(bf16[8,128,256]{2,1,0:T(8,128)(2,1)} %copy-done.26) | copy-start | bytes 1572868
  (69 other events, 269.9 us)
Sparse Core Ops, SparseCore 0:
  10.2 161.6 all-gather.1
  367.2 223.2 reduce-scatter.1
  705.7 39.7 all-reduce.3

commit v3 on v2

--- a/solution.py
+++ b/solution.py
@@ -131,118 +131,6 @@
             device_id_type=pl.DeviceIdType.MESH,
         )
     pl.semaphore_wait(barrier, 3 + inner + (1 if pair else 0))
-
-
-def gather_kernel(z_size, x_size, count, *refs):
-    ins, outs = refs[:count], refs[count : 2 * count]
-    own_sem, up_s, up_r, dn_s, dn_r, x_s, x_r, c_s, c_r = refs[2 * count :]
-    z, x, core = place_of(x_size)
-    greet(z, x, core, z_size, x_size)
-    at = functools.partial(index_of, x_size=x_size)
-    keep = [
-        pltpu.make_async_copy(ins[a], outs[a].at[at(z, x, core)], own_sem.at[a])
-        for a in range(count)
-    ]
-    for copy in keep:
-        copy.start()
-
-    def up(a, d):
-        block = outs[a].at[at(z - d, x, core)]
-        src = ins[a] if d == 0 else block
-        return remote(src, block, up_s.at[a, d], up_r.at[a, d], at(z + 1, x, core))
-
-    def down(a, d):
-        block = outs[a].at[at(z + d, x, core)]
-        src = ins[a] if d == 0 else block
-        return remote(src, block, dn_s.at[a, d], dn_r.at[a, d], at(z - 1, x, core))
-
-    def across(a, w, own=False):
-        block = outs[a].at[at(w, x, core)]
-        return remote(ins[a] if own else block, block, x_s.at[a, w], x_r.at[a, w], at(z, 1 - x, core))
-
-    def beside(a, w, v, own=False):
-        block = outs[a].at[at(w, v, core)]
-        return remote(
-            ins[a] if own else block, block, c_s.at[a, w, v], c_r.at[a, w, v], at(z, x, 1 - core)
-        )
-
-    def each(do):
-        for a in range(count):
-            do(a)
-
-    def from_across(w):
-        def do(a):
-            across(a, w).wait_recv()
-            beside(a, w, 1 - x).start()
-
-        each(do)
-
-    def when_up(d, do):
-        pl.when(z >= d)(lambda: each(do))
-
-    def when_down(d, do):
-        pl.when(z + d < z_size)(lambda: each(do))
-
-    def first(a):
-        across(a, z, True).start()
-        pl.when(z < z_size - 1)(lambda: up(a, 0).start())
-        pl.when(z > 0)(lambda: down(a, 0).start())
-        beside(a, z, x, True).start()
-
-    each(first)
-    for d in range(1, z_size):
-
-        def passed_up(a):
-            up(a, d - 1).wait_recv()
-            pl.when(z < z_size - 1)(lambda: up(a, d).start())
-            across(a, z - d).start()
-            beside(a, z - d, x).start()
-
-        def passed_down(a):
-            down(a, d - 1).wait_recv()
-            pl.when(z > 0)(lambda: down(a, d).start())
-            across(a, z + d).start()
-            beside(a, z + d, x).start()
-
-        when_up(d, passed_up)
-        when_down(d, passed_down)
-        if d == 1:
-            from_across(z)
-        else:
-            pl.when(z >= d - 1)(lambda: from_across(z - (d - 1)))
-            pl.when(z + d - 1 < z_size)(lambda: from_across(z + (d - 1)))
-    pl.when(z >= z_size - 1)(lambda: from_across(z - (z_size - 1)))
-    pl.when(z < 1)(lambda: from_across(z + (z_size - 1)))
-    for a in range(count):
-        for w in range(z_size):
-            for v in range(x_size):
-                beside(a, w, v).wait()
-            across(a, w).wait_send()
-    for d in range(z_size):
-        pl.when((z >= d) & (z < z_size - 1))(lambda: each(lambda a: up(a, d).wait_send()))
-        pl.when((z + d < z_size) & (z > 0))(lambda: each(lambda a: down(a, d).wait_send()))
-    for copy in keep:
-        copy.wait()
-
-
-def gather_rows(arrays, z_size, x_size, collective_id):
-    count = len(arrays)
-    n = 2 * z_size * x_size
-    dma = pltpu.SemaphoreType.DMA
-    outs = pl.pallas_call(
-        functools.partial(gather_kernel, z_size, x_size, count),
-        out_shape=[jax.ShapeDtypeStruct((n,) + a.shape, a.dtype) for a in arrays],
-        in_specs=[pl.BlockSpec(memory_space=pl.ANY)] * count,
-        out_specs=[pl.BlockSpec(memory_space=pl.ANY)] * count,
-        scratch_shapes=[dma((count,))]
-        + [dma((count, z_size))] * 6
-        + [dma((count, z_size, x_size))] * 2,
-        compiler_params=pltpu.CompilerParams(
-            collective_id=collective_id, has_side_effects=True, vmem_limit_bytes=VMEM_LIMIT
-        ),
-        name="gather_rows",
-    )(*arrays)
-    return outs
 
 
 def add_into(dst, *srcs):
@@ -468,14 +356,399 @@
     )(left, right, *extras)
 
 
+def nn(left, right):
+    return lax.dot_general(
+        left, right, (((1,), (0,)), ((), ())), preferred_element_type=jnp.float32
+    )
+
+
+def is_at(j, where):
+    low = (3 - j) // 3
+    high = j // 3
+    return (low, (4 - j) // 3 - low, (j + 1) // 3 - high, high)[where]
+
+
+def ffn_kernel(
+    x_size,
+    own_ffn,
+    own_gates,
+    grad_all,
+    gate_t,
+    up_t,
+    down_t,
+    shared_in,
+    shared_out,
+    out_part,
+    dx_part,
+    rows_all,
+    dy_all,
+    he_all,
+    dge_all,
+    due_all,
+    shared_grads,
+    blk,
+    gts,
+    gate_v,
+    up_v,
+    down_v,
+    s_in,
+    s_out,
+    g_buf,
+    rows_b,
+    grow_b,
+    dy_b,
+    he_b,
+    dge_b,
+    due_b,
+    out_r,
+    dx_r,
+    out_l,
+    dx_l,
+    out_st,
+    dx_st,
+    acc,
+    gate_col,
+    dgate_acc,
+    own_sem,
+    up_s,
+    up_r,
+    dn_s,
+    dn_r,
+    x_s,
+    x_r,
+    c_s,
+    c_r,
+    w_sem,
+    g_sem,
+    st_sem,
+):
+    z_size, bf16, f32 = 4, jnp.bfloat16, jnp.float32
+    hidden = gate_t.shape[0]
+    rows_here, features = own_ffn.shape
+    slots = rows_b.shape[0] // 2
+    wide = 512
+    z, x, core = place_of(x_size)
+    own = lax.axis_index("dp")
+    at = functools.partial(index_of, x_size=x_size)
+    ins, outs = (own_ffn, own_gates), (blk, gts)
+    half = z // 2
+    order = [z, 1 - z + 4 * half, 2 - half, 3 - 3 * half]
+
+    def place(j):
+        return sum(is_at(j, i) * order[i] for i in range(4))
+
+    weights = [
+        pltpu.make_async_copy(gate_t, gate_v.at[pl.ds(0, hidden)], w_sem.at[0]),
+        pltpu.make_async_copy(up_t, up_v.at[pl.ds(0, hidden)], w_sem.at[1]),
+        pltpu.make_async_copy(down_t, down_v.at[pl.ds(0, hidden)], w_sem.at[2]),
+        pltpu.make_async_copy(shared_in, s_in, w_sem.at[3]),
+        pltpu.make_async_copy(shared_out, s_out, w_sem.at[4]),
+    ]
+    keep = [
+        pltpu.make_async_copy(ins[a], outs[a].at[at(z, x, core)], own_sem.at[a]) for a in range(2)
+    ]
+
+    def grad_copy(k):
+        w, v = place(k // 2), x + (k % 2) * (1 - 2 * x)
+        return pltpu.make_async_copy(
+            grad_all.at[pl.ds(2 * (w * x_size + v), 2)], g_buf.at[k % 2], g_sem.at[k % 2]
+        )
+
+    for copy in keep + weights:
+        copy.start()
+    grad_copy(0).start()
+    greet(z, x, core, z_size, x_size)
+
+    def up(a, d):
+        block = outs[a].at[at(z - d, x, core)]
+        src = ins[a] if d == 0 else block
+        return remote(src, block, up_s.at[a, d], up_r.at[a, d], at(z + 1, x, core))
+
+    def down(a, d):
+        block = outs[a].at[at(z + d, x, core)]
+        src = ins[a] if d == 0 else block
+        return remote(src, block, dn_s.at[a, d], dn_r.at[a, d], at(z - 1, x, core))
+
+    def across(a, w, first=False):
+        block = outs[a].at[at(w, x, core)]
+        src = ins[a] if first else block
+        return remote(src, block, x_s.at[a, w], x_r.at[a, w], at(z, 1 - x, core))
+
+    def beside(a, w, v, first=False):
+        block = outs[a].at[at(w, v, core)]
+        src = ins[a] if first else block
+        return remote(src, block, c_s.at[a, w, v], c_r.at[a, w, v], at(z, x, 1 - core))
+
+    for a in (1, 0):
+        beside(a, z, x, True).start()
+        across(a, z, True).start()
+        pl.when(z < z_size - 1)(lambda: up(a, 0).start())
+        pl.when(z > 0)(lambda: down(a, 0).start())
+
+    def pass_on(d):
+        for a in (1, 0):
+
+            @pl.when(z >= d)
+            def _():
+                up(a, d - 1).wait_recv()
+                pl.when(z < z_size - 1)(lambda: up(a, d).start())
+                across(a, z - d).start()
+                beside(a, z - d, x).start()
+
+            @pl.when(z + d < z_size)
+            def _():
+                down(a, d - 1).wait_recv()
+                pl.when(z > 0)(lambda: down(a, d).start())
+                across(a, z + d).start()
+                beside(a, z + d, x).start()
+
+    def from_across(w):
+        for a in (1, 0):
+            across(a, w).wait_recv()
+            beside(a, w, 1 - x).start()
+
+    gate_v[pl.ds(hidden, gate_v.shape[0] - hidden), :] = jnp.zeros(
+        (gate_v.shape[0] - hidden, features), bf16
+    )
+    up_v[pl.ds(hidden, up_v.shape[0] - hidden), :] = jnp.zeros(
+        (up_v.shape[0] - hidden, features), bf16
+    )
+    down_v[pl.ds(hidden, down_v.shape[0] - hidden), :] = jnp.zeros(
+        (down_v.shape[0] - hidden, features), bf16
+    )
+    acc[...] = jnp.zeros(acc.shape, f32)
+    for copy in weights:
+        copy.wait()
+    for a in range(2):
+        out_r[a, pl.ds(slots, 128), :] = s_out[...]
+        dx_r[a, pl.ds(slots, 256), :] = s_in[...]
+    for copy in keep:
+        copy.wait()
+    lane = lax.broadcasted_iota(jnp.int32, (rows_here, 128), 1)
+    earlier = lax.broadcasted_iota(jnp.int32, (rows_here, rows_here), 1)
+    later = lax.broadcasted_iota(jnp.int32, (rows_here, rows_here), 0)
+    upto = (earlier <= later).astype(bf16)
+    slot_lane = lax.broadcasted_iota(jnp.int32, (rows_here, slots), 1).astype(f32)
+
+    def staged(pair):
+        return [
+            pltpu.make_async_copy(src, dst.at[pair], st_sem.at[i])
+            for i, (src, dst) in enumerate(
+                [
+                    (rows_b, rows_all),
+                    (dy_b, dy_all),
+                    (he_b, he_all),
+                    (dge_b, dge_all),
+                    (due_b, due_all),
+                    (out_st, out_part),
+                    (dx_st, dx_part),
+                ]
+            )
+        ]
+
+    def body(k, _):
+        w, v = place(k // 2), x + (k % 2) * (1 - 2 * x)
+        pair = w * x_size + v
+        block = 2 * pair
+        here = k % 2
+        for r in range(1, 5):
+
+            @pl.when(k == 2 * r - 1)
+            def _():
+                if r < 4:
+                    pass_on(r)
+                from_across(order[r - 1])
+
+        grad_copy(k).wait()
+        pl.when(k < 7)(lambda: grad_copy(k + 1).start())
+        for a in (1, 0):
+            beside(a, w, v).wait_recv()
+
+        @pl.when(k > 0)
+        def _():
+            for copy in staged(pair):
+                copy.wait()
+
+        for a in range(2):
+            gates = gts[block + a]
+            count = nn(upto, (gates >= 0.0).astype(bf16))
+            gate = jnp.sum(jnp.where(lane == own, gates, 0.0), axis=1, keepdims=True)
+            slot = jnp.sum(jnp.where(lane == own, count, 0.0), axis=1, keepdims=True) - 1.0
+            pick = ((slot_lane == slot) & (gate >= 0.0)).astype(f32).astype(bf16)
+            out_l[a, :, pl.ds(0, slots)] = pick
+            dx_l[a, :, pl.ds(0, slots)] = pick
+            high = gate.astype(bf16).astype(f32)
+            middle = (gate - high).astype(bf16).astype(f32)
+            low = gate - high - middle
+            parts = jnp.where(
+                lane == 0, high, jnp.where(lane == 1, middle, jnp.where(lane == 2, low, 0.0))
+            ).astype(bf16)
+            picked = jnp.sum(contract_first(pick, parts), axis=1, keepdims=True)
+            gate_col[pl.ds(a * slots, slots), :] = jnp.broadcast_to(picked, (slots, 128))
+
+        def pick_rows(n, _):
+            cols = pl.ds(pl.multiple_of(n * wide, wide), wide)
+            for a in range(2):
+                mine = pl.ds(a * slots, slots)
+                pick = out_l[a, :, pl.ds(0, slots)]
+                rows_b[mine, cols] = contract_first(pick, blk[block + a, :, cols]).astype(bf16)
+                grows = contract_first(pick, g_buf[here, a, :, cols])
+                grow_b[mine, cols] = grows.astype(bf16)
+                dy_b[mine, cols] = (gate_col[mine, pl.ds(0, 1)] * grows).astype(bf16)
+            return 0
+
+        lax.fori_loop(0, features // wide, pick_rows, 0)
+
+        for a in range(2):
+            pre = contract_last(blk[block + a], s_in[...])
+            grad_hidden = contract_last(g_buf[here, a], s_out[...])
+            act, slope = swish_parts(pre[:, :128])
+            up_pre = pre[:, 128:]
+            out_l[a, :, pl.ds(slots, 128)] = (act * up_pre).astype(bf16)
+            dx_l[a, :, pl.ds(slots, 128)] = (grad_hidden * up_pre * slope).astype(bf16)
+            dx_l[a, :, pl.ds(slots + 128, 128)] = (grad_hidden * act).astype(bf16)
+
+        def shared_weights(n, _):
+            cols = pl.ds(pl.multiple_of(n * wide, wide), wide)
+            for a in range(2):
+                acc[pl.ds(0, 256), cols] += contract_first(
+                    dx_l[a, :, pl.ds(slots, 256)], blk[block + a, :, cols]
+                )
+                acc[pl.ds(256, 128), cols] += contract_first(
+                    out_l[a, :, pl.ds(slots, 128)], g_buf[here, a, :, cols]
+                )
+            return 0
+
+        lax.fori_loop(0, features // wide, shared_weights, 0)
+
+        def hidden_units(n, _):
+            units = pl.ds(pl.multiple_of(n * 256, 256), 256)
+            gate_pre = contract_last(rows_b[...], gate_v[units, :])
+            up_pre = contract_last(rows_b[...], up_v[units, :])
+            grad_hidden = contract_last(dy_b[...], down_v[units, :])
+            act, slope = swish_parts(gate_pre)
+            he_b[:, units] = (act * up_pre).astype(bf16)
+            dge_b[:, units] = (grad_hidden * up_pre * slope).astype(bf16)
+            due_b[:, units] = (grad_hidden * act).astype(bf16)
+            return 0
+
+        lax.fori_loop(0, gate_v.shape[0] // 256, hidden_units, 0)
+        dgate_acc[...] = jnp.zeros(dgate_acc.shape, f32)
+
+        def back(n, _):
+            cols = pl.ds(pl.multiple_of(n * wide, wide), wide)
+            result = nn(he_b[...], down_v[:, cols])
+            product = grow_b[:, cols].astype(f32) * result
+            for i in range(wide // 128):
+                dgate_acc[...] += product[:, i * 128 : (i + 1) * 128]
+            result = (gate_col[:, pl.ds(0, 1)] * result).astype(bf16)
+            grad_in = (nn(dge_b[...], gate_v[:, cols]) + nn(due_b[...], up_v[:, cols])).astype(bf16)
+            for a in range(2):
+                mine = slice(a * slots, (a + 1) * slots)
+                out_r[a, pl.ds(0, slots), cols] = result[mine]
+                dx_r[a, pl.ds(0, slots), cols] = grad_in[mine]
+                out_st[a, :, cols] = nn(out_l[a], out_r[a, :, cols]).astype(bf16)
+                dx_st[a, :, cols] = nn(dx_l[a], dx_r[a, :, cols]).astype(bf16)
+            return 0
+
+        lax.fori_loop(0, features // wide, back, 0)
+        dgate = jnp.sum(dgate_acc[...], axis=1, keepdims=True)
+        high = dgate.astype(bf16).astype(f32)
+        spread = lax.broadcasted_iota(jnp.int32, (2 * slots, 128), 1)
+        spread = jnp.where(
+            spread == own, high, jnp.where(spread == own + 16, dgate - high, 0.0)
+        ).astype(bf16)
+        for a in range(2):
+            dx_st[a, :, pl.ds(features, 128)] = nn(
+                out_l[a, :, pl.ds(0, slots)], spread[a * slots : (a + 1) * slots]
+            ).astype(bf16)
+        for copy in staged(pair):
+            copy.start()
+        return 0
+
+    lax.fori_loop(0, 8, body, 0)
+    for copy in staged(0):
+        copy.wait()
+    shared_grads[...] = acc[...].astype(bf16)
+    for a in range(2):
+        for w in range(z_size):
+            for v in range(x_size):
+                beside(a, w, v).wait_send()
+            across(a, w).wait_send()
+    for d in range(z_size):
+        for a in range(2):
+            pl.when((z >= d) & (z < z_size - 1))(lambda: up(a, d).wait_send())
+            pl.when((z + d < z_size) & (z > 0))(lambda: down(a, d).wait_send())
+
+
+def ffn_tuned(own_ffn, own_gates, grad_all, gate_t, up_t, down_t, shared_in, shared_out, slots):
+    rows, features = own_ffn.shape
+    hidden = gate_t.shape[0]
+    padded = -(-hidden // 256) * 256
+    bf16, f32, dma = jnp.bfloat16, jnp.float32, pltpu.SemaphoreType.DMA
+    anywhere = pl.BlockSpec(memory_space=pl.ANY)
+    shape = jax.ShapeDtypeStruct
+    return pl.pallas_call(
+        functools.partial(ffn_kernel, 2),
+        out_shape=[
+            shape((8, 2, rows, features), bf16),
+            shape((8, 2, rows, features + 128), bf16),
+            shape((8, 2 * slots, features), bf16),
+            shape((8, 2 * slots, features), bf16),
+            shape((8, 2 * slots, padded), bf16),
+            shape((8, 2 * slots, padded), bf16),
+            shape((8, 2 * slots, padded), bf16),
+            shape((384, features), bf16),
+        ],
+        in_specs=[anywhere] * 8,
+        out_specs=[anywhere] * 7 + [pl.BlockSpec(memory_space=pltpu.VMEM)],
+        scratch_shapes=[
+            pltpu.VMEM((16, rows, features), bf16),
+            pltpu.VMEM((16, rows, 128), f32),
+            pltpu.VMEM((padded, features), bf16),
+            pltpu.VMEM((padded, features), bf16),
+            pltpu.VMEM((padded, features), bf16),
+            pltpu.VMEM((256, features), bf16),
+            pltpu.VMEM((128, features), bf16),
+            pltpu.VMEM((2, 2, rows, features), bf16),
+            pltpu.VMEM((2 * slots, features), bf16),
+            pltpu.VMEM((2 * slots, features), bf16),
+            pltpu.VMEM((2 * slots, features), bf16),
+            pltpu.VMEM((2 * slots, padded), bf16),
+            pltpu.VMEM((2 * slots, padded), bf16),
+            pltpu.VMEM((2 * slots, padded), bf16),
+            pltpu.VMEM((2, slots + 128, features), bf16),
+            pltpu.VMEM((2, slots + 256, features), bf16),
+            pltpu.VMEM((2, rows, slots + 128), bf16),
+            pltpu.VMEM((2, rows, slots + 256), bf16),
+            pltpu.VMEM((2, rows, features), bf16),
+            pltpu.VMEM((2, rows, features + 128), bf16),
+            pltpu.VMEM((384, features), f32),
+            pltpu.VMEM((2 * slots, 128), f32),
+            pltpu.VMEM((2 * slots, 128), f32),
+            dma((2,)),
+        ]
+        + [dma((2, 4))] * 6
+        + [dma((2, 4, 2))] * 2
+        + [dma((5,)), dma((2,)), dma((7,))],
+        compiler_params=pltpu.CompilerParams(
+            collective_id=1, has_side_effects=True, vmem_limit_bytes=VMEM_LIMIT
+        ),
+        name="ffn",
+    )(
+        own_ffn,
+        own_gates,
+        grad_all.reshape(16, rows, features),
+        gate_t,
+        up_t,
+        down_t,
+        shared_in,
+        shared_out,
+    )
+
+
 def tuned():
     return lax.axis_size("dp") == 16 and lax.axis_size("tensor") == 2
-
-
-def gather_all(arrays):
-    if tuned():
-        return gather_rows(arrays, 4, 2, 1)
-    return [lax.all_gather(a, "dp") for a in arrays]
 
 
 def sum_home(arrays, collective_id, pair=False):
@@ -492,6 +765,138 @@
         return pair_product(left, right, extras, collective_id)
     product = contract_last(left, right).astype(jnp.bfloat16)
     return [lax.psum(a, "tensor").astype(jnp.float32) for a in [product] + extras]
+
+
+def ffn_with_kernel(own_ffn, gates, everyone_grad, weights, shared, capacity, experts):
+    part = shared[0].shape[1]
+    hidden, features = weights[0].shape[1], own_ffn.shape[1]
+    gate_t, up_t, down_t = (jnp.pad(w.T, ((0, 128 - part), (0, 0))) for w in shared)
+    out_part, grad_part, rows, dy, he, dge, due, shared_grads = ffn_tuned(
+        own_ffn,
+        gates,
+        everyone_grad,
+        *(w.T for w in weights),
+        jnp.concatenate([gate_t, up_t], axis=0),
+        down_t,
+        capacity,
+    )
+    rows, dy = rows.reshape(-1, features), dy.reshape(-1, features)
+    he, dge, due = (a.reshape(-1, a.shape[2])[:, :hidden] for a in (he, dge, due))
+    devices, rows_here = everyone_grad.shape[:2]
+    return (
+        out_part.reshape(devices, rows_here, -1),
+        grad_part.reshape(devices, rows_here, -1),
+        contract_first(rows, dge)[None],
+        contract_first(rows, due)[None],
+        contract_first(dy, he)[None],
+        shared_grads.reshape(3, 128, features)[:, :part].reshape(3 * part, features),
+    )
+
+
+def ffn_plain(own_ffn, gates, everyone_grad, weights, shared, capacity, experts):
+    own, devices = lax.axis_index("dp"), lax.axis_size("dp")
+    rows_here, features = own_ffn.shape
+    places = jnp.arange(rows_here, dtype=jnp.int32)
+    expert_gate, expert_up, expert_down = weights
+    part_gate, part_up, part_down = shared
+    everyone_ffn = lax.all_gather(own_ffn, "dp", tiled=True)
+    everyone_gates = lax.all_gather(gates, "dp")
+    everyone_grad = everyone_grad.reshape(devices * rows_here, features)
+    own_probs = lax.dynamic_slice_in_dim(everyone_gates, own, 1, 2).reshape(devices, rows_here)
+    chooses = own_probs >= 0.0
+    own_gates = jnp.where(chooses, own_probs, 0.0)
+    upto = (places[:, None] <= places[None, :]).astype(jnp.bfloat16)
+    slot = jnp.dot(chooses.astype(jnp.bfloat16), upto, preferred_element_type=jnp.float32) - 1.0
+    slots = jnp.arange(capacity, dtype=jnp.float32)
+    picked = chooses[:, None, :] & (slot[:, None, :] == slots[None, :, None])
+    pick = picked.astype(jnp.bfloat16)
+    slot_gates = jnp.sum(jnp.where(picked, own_gates[:, None, :], 0.0), axis=2).reshape(-1, 1)
+
+    def pick_rows(values):
+        blocks = values.reshape(devices, rows_here, features)
+        return jnp.einsum(
+            "jst,jtc->jsc", pick, blocks, preferred_element_type=jnp.float32
+        ).astype(jnp.bfloat16).reshape(devices * capacity, features)
+
+    def put_rows(values, hidden_parts, weights):
+        blocks = values.astype(jnp.bfloat16).reshape(devices, capacity, features)
+        left = jnp.concatenate(
+            [pick.transpose(0, 2, 1)]
+            + [h.reshape(devices, rows_here, h.shape[1]) for h in hidden_parts],
+            axis=2,
+        )
+        right = jnp.concatenate(
+            [blocks]
+            + [
+                jnp.broadcast_to(w.T[None], (devices, w.shape[1], features))
+                for w in weights
+            ],
+            axis=1,
+        )
+        return (
+            jnp.einsum("jtk,jkc->jtc", left, right, preferred_element_type=jnp.float32)
+            .astype(jnp.bfloat16)
+            .reshape(devices * rows_here, features)
+        )
+
+    expert_rows = pick_rows(everyone_ffn)
+    grad_picked = pick_rows(everyone_grad)
+    grad_rows = (slot_gates * grad_picked.astype(jnp.float32)).astype(jnp.bfloat16)
+
+    gate_pre = jnp.dot(expert_rows, expert_gate, preferred_element_type=jnp.float32)
+    up_pre = jnp.dot(expert_rows, expert_up, preferred_element_type=jnp.float32)
+    gate_act, gate_slope = swish_parts(gate_pre)
+    expert_hidden = (gate_act * up_pre).astype(jnp.bfloat16)
+    expert_result = contract_last(expert_hidden, expert_down)
+    slot_grads = jnp.sum(grad_picked.astype(jnp.float32) * expert_result, axis=1)
+    grad_expert_down = contract_first(grad_rows, expert_hidden)[None]
+    grad_expert_hidden = jnp.dot(grad_rows, expert_down, preferred_element_type=jnp.float32)
+    grad_gate_pre = (grad_expert_hidden * up_pre * gate_slope).astype(jnp.bfloat16)
+    grad_up_pre = (grad_expert_hidden * gate_act).astype(jnp.bfloat16)
+    grad_expert_gate = contract_first(expert_rows, grad_gate_pre)[None]
+    grad_expert_up = contract_first(expert_rows, grad_up_pre)[None]
+    grad_rows_in = contract_last(grad_gate_pre, expert_gate) + contract_last(
+        grad_up_pre, expert_up
+    )
+
+    shared_pre_gate = jnp.dot(everyone_ffn, part_gate, preferred_element_type=jnp.float32)
+    shared_pre_up = jnp.dot(everyone_ffn, part_up, preferred_element_type=jnp.float32)
+    shared_act, shared_slope = swish_parts(shared_pre_gate)
+    shared_hidden = (shared_act * shared_pre_up).astype(jnp.bfloat16)
+    grad_shared_hidden = jnp.dot(everyone_grad, part_down, preferred_element_type=jnp.float32)
+    grad_shared_gate_pre = (grad_shared_hidden * shared_pre_up * shared_slope).astype(jnp.bfloat16)
+    grad_shared_up_pre = (grad_shared_hidden * shared_act).astype(jnp.bfloat16)
+    shared_grads = jnp.concatenate(
+        [
+            contract_first(grad_shared_gate_pre, everyone_ffn),
+            contract_first(grad_shared_up_pre, everyone_ffn),
+            contract_first(shared_hidden, everyone_grad),
+        ],
+        axis=0,
+    ).astype(jnp.bfloat16)
+    ffn_part = put_rows(slot_gates * expert_result, [shared_hidden], [part_down])
+    pair_grads = jnp.sum(
+        jnp.where(picked, slot_grads.reshape(devices, capacity, 1), 0.0), axis=1
+    ).reshape(devices * rows_here, 1)
+    pair_high = pair_grads.astype(jnp.bfloat16).astype(jnp.float32)
+    column = jnp.arange(128, dtype=jnp.int32)[None, :]
+    pair_columns = jnp.where(
+        column == own,
+        pair_high,
+        jnp.where(column == own + experts, pair_grads - pair_high, 0.0),
+    )
+    grad_ffn_in = put_rows(
+        grad_rows_in, [grad_shared_gate_pre, grad_shared_up_pre], [part_gate, part_up]
+    )
+    grad_part = jnp.concatenate([grad_ffn_in, pair_columns.astype(jnp.bfloat16)], axis=1)
+    return (
+        ffn_part.reshape(devices, rows_here, -1),
+        grad_part.reshape(devices, rows_here, -1),
+        grad_expert_gate,
+        grad_expert_up,
+        grad_expert_down,
+        shared_grads,
+    )
 
 
 def shards(
@@ -584,92 +989,37 @@
     router_probs = jax.nn.softmax(jnp.dot(ffn_normed, router, precision=highest), axis=-1)
     own = lax.axis_index("dp")
 
-    everyone_grad = lax.all_gather(grad_out, "dp", tiled=True)
     named = jnp.any(routes[:, :, None] == jnp.arange(128, dtype=jnp.int32)[None, None, :], axis=1)
-    dense_gates = jnp.where(
-        named, jnp.pad(router_probs, ((0, 0), (0, 128 - experts))), -1.0
-    )
-    everyone_ffn, everyone_gates = gather_all([ffn_bf, dense_gates])
-    everyone_ffn = everyone_ffn.reshape(devices * rows_here, features)
-    own_probs = lax.dynamic_slice_in_dim(everyone_gates, own, 1, 2).reshape(devices, rows_here)
-    chooses = own_probs >= 0.0
-    own_gates = jnp.where(chooses, own_probs, 0.0)
-    upto = (places[:, None] <= places[None, :]).astype(jnp.bfloat16)
-    slot = jnp.dot(chooses.astype(jnp.bfloat16), upto, preferred_element_type=jnp.float32) - 1.0
-    slots = jnp.arange(capacity, dtype=jnp.float32)
-    picked = chooses[:, None, :] & (slot[:, None, :] == slots[None, :, None])
-    pick = picked.astype(jnp.bfloat16)
-    slot_gates = jnp.sum(jnp.where(picked, own_gates[:, None, :], 0.0), axis=2).reshape(-1, 1)
-
-    def pick_rows(values):
-        blocks = values.reshape(devices, rows_here, features)
-        return jnp.einsum(
-            "jst,jtc->jsc", pick, blocks, preferred_element_type=jnp.float32
-        ).astype(jnp.bfloat16).reshape(devices * capacity, features)
-
-    def put_rows(values, hidden_parts, weights):
-        blocks = values.astype(jnp.bfloat16).reshape(devices, capacity, features)
-        left = jnp.concatenate(
-            [pick.transpose(0, 2, 1)]
-            + [h.reshape(devices, rows_here, h.shape[1]) for h in hidden_parts],
-            axis=2,
-        )
-        right = jnp.concatenate(
-            [blocks]
-            + [
-                jnp.broadcast_to(w.T[None], (devices, w.shape[1], features))
-                for w in weights
-            ],
-            axis=1,
-        )
-        return (
-            jnp.einsum("jtk,jkc->jtc", left, right, preferred_element_type=jnp.float32)
-            .astype(jnp.bfloat16)
-            .reshape(devices * rows_here, features)
-        )
-
-    expert_rows = pick_rows(everyone_ffn)
-    grad_picked = pick_rows(everyone_grad)
-    grad_rows = (slot_gates * grad_picked.astype(jnp.float32)).astype(jnp.bfloat16)
-
-    gate_pre = jnp.dot(expert_rows, expert_gate[0], preferred_element_type=jnp.float32)
-    up_pre = jnp.dot(expert_rows, expert_up[0], preferred_element_type=jnp.float32)
-    gate_act, gate_slope = swish_parts(gate_pre)
-    expert_hidden = (gate_act * up_pre).astype(jnp.bfloat16)
-    expert_result = contract_last(expert_hidden, expert_down[0])
-    slot_grads = jnp.sum(grad_picked.astype(jnp.float32) * expert_result, axis=1)
-    grad_expert_down = contract_first(grad_rows, expert_hidden)[None]
-    grad_expert_hidden = jnp.dot(grad_rows, expert_down[0], preferred_element_type=jnp.float32)
-    grad_gate_pre = (grad_expert_hidden * up_pre * gate_slope).astype(jnp.bfloat16)
-    grad_up_pre = (grad_expert_hidden * gate_act).astype(jnp.bfloat16)
-    grad_expert_gate = contract_first(expert_rows, grad_gate_pre)[None]
-    grad_expert_up = contract_first(expert_rows, grad_up_pre)[None]
-    grad_rows_in = contract_last(grad_gate_pre, expert_gate[0]) + contract_last(
-        grad_up_pre, expert_up[0]
-    )
-
+    dense_gates = jnp.where(named, jnp.pad(router_probs, ((0, 0), (0, 128 - experts))), -1.0)
+    everyone_grad = lax.all_gather(grad_out, "dp")
     part = shared_gate.shape[1] // devices
-    part_gate = lax.dynamic_slice_in_dim(shared_gate, own * part, part, 1)
-    part_up = lax.dynamic_slice_in_dim(shared_up, own * part, part, 1)
-    part_down = lax.dynamic_slice_in_dim(shared_down, own * part, part, 1)
-    shared_pre_gate = jnp.dot(everyone_ffn, part_gate, preferred_element_type=jnp.float32)
-    shared_pre_up = jnp.dot(everyone_ffn, part_up, preferred_element_type=jnp.float32)
-    shared_act, shared_slope = swish_parts(shared_pre_gate)
-    shared_hidden = (shared_act * shared_pre_up).astype(jnp.bfloat16)
-    grad_shared_hidden = jnp.dot(everyone_grad, part_down, preferred_element_type=jnp.float32)
-    grad_shared_gate_pre = (grad_shared_hidden * shared_pre_up * shared_slope).astype(jnp.bfloat16)
-    grad_shared_up_pre = (grad_shared_hidden * shared_act).astype(jnp.bfloat16)
-    shared_grads = jnp.concatenate(
-        [
-            contract_first(everyone_ffn, grad_shared_gate_pre),
-            contract_first(everyone_ffn, grad_shared_up_pre),
-            contract_first(everyone_grad, shared_hidden),
-        ],
-        axis=1,
-    ).astype(jnp.bfloat16)
+    shared_parts = [
+        lax.dynamic_slice_in_dim(w, own * part, part, 1)
+        for w in (shared_gate, shared_up, shared_down)
+    ]
+    feed_forward = ffn_with_kernel if tuned() else ffn_plain
+    (
+        ffn_part,
+        grad_ffn_part,
+        grad_expert_gate,
+        grad_expert_up,
+        grad_expert_down,
+        shared_grads,
+    ) = feed_forward(
+        ffn_bf,
+        dense_gates,
+        everyone_grad,
+        [w[0] for w in (expert_gate, expert_up, expert_down)],
+        shared_parts,
+        capacity,
+        experts,
+    )
     share_rows = features // devices
     shared_grads = lax.all_to_all(
-        shared_grads.reshape(devices, share_rows, 3 * part), "dp", split_axis=0, concat_axis=0
+        shared_grads.reshape(3 * part, devices, share_rows).transpose(1, 2, 0),
+        "dp",
+        split_axis=0,
+        concat_axis=0,
     ).astype(jnp.float32)
     grad_shared_gate, grad_shared_up, grad_shared_down = (
         shared_grads[:, :, i * part : (i + 1) * part]
@@ -679,32 +1029,12 @@
     )
 
     grad_top = grad_out.astype(jnp.float32)
-    ffn_part = put_rows(slot_gates * expert_result, [shared_hidden], [part_down])
-    ffn_total = lax.psum_scatter(ffn_part, "dp", scatter_dimension=0, tiled=True)
+    ffn_total = lax.psum_scatter(
+        ffn_part.reshape(devices * rows_here, features), "dp", scatter_dimension=0, tiled=True
+    )
     ffn_total = lax.psum(ffn_total, "tensor").astype(jnp.float32)
     output = (hidden + ffn_total).astype(jnp.bfloat16)
-    pair_grads = jnp.sum(
-        jnp.where(picked, slot_grads.reshape(devices, capacity, 1), 0.0), axis=1
-    ).reshape(devices * rows_here, 1)
-    pair_high = pair_grads.astype(jnp.bfloat16).astype(jnp.float32)
-    column = jnp.arange(128, dtype=jnp.int32)[None, :]
-    pair_columns = jnp.where(
-        column == own,
-        pair_high,
-        jnp.where(column == own + experts, pair_grads - pair_high, 0.0),
-    )
-    grad_ffn_in = put_rows(
-        grad_rows_in, [grad_shared_gate_pre, grad_shared_up_pre], [part_gate, part_up]
-    )
-    (grad_ffn_sum,) = sum_home(
-        [
-            jnp.concatenate([grad_ffn_in, pair_columns.astype(jnp.bfloat16)], axis=1).reshape(
-                devices, rows_here, features + 128
-            )
-        ],
-        3,
-        True,
-    )
+    (grad_ffn_sum,) = sum_home([grad_ffn_part], 3, True)
     dense_grad = (
         grad_ffn_sum[:, features : features + experts]
         + grad_ffn_sum[:, features + experts : features + 2 * experts]

time: 961 us -> 842 us (0.88)
  matrix products: 272 us -> 105 us
  waiting for transfers between devices: 20.3 us -> 89 us
  other arithmetic: 68 us -> 38.1 us
  local copies, waits for them, and re-layouts: 98.6 us -> 69 us
  Pallas kernels: 472 us -> 496 us
  starting transfers between devices: 4.6 us -> 18.1 us
    dot_general x11 -> x0, matrix products: 124 us -> none  [the longest x2 30.3 us: put_rows(): jnp.einsum('jtk,jkc->jtc', left, right, preferred_element_type=jnp.float32)]
    all_gather x1, waiting for transfers between devices: 0.02 us -> 44.4 us  [shards(): everyone_grad = lax.all_gather(grad_out, 'dp')]
    dot_general x6 -> x3, matrix products: 46.1 us -> 10.7 us  [contract_last(): lax.dot_general(left, right, (((1,), (1,)), ((), ())), precision=precisio...]
    reduce_scatter x1, waiting for transfers between devices: 0.02 us -> 28.9 us  [shards(): lax.psum_scatter(ffn_part.reshape(devices * rows_here, features), 'dp', s...]
    pallas_call x2, Pallas kernels: 253 us -> 279 us  [scatter_sums(): pl.pallas_call(functools.partial(scatter_kernel, x_size, parts, pair), ou...]
    convert_element_type x5 -> x0, other arithmetic: 22.8 us -> none  [the longest x2 19.3 us: shards(): (slot_gates * grad_picked.astype(jnp.float32)).astype(jnp.bfloat16)]
    dot_general x1 -> x0, local copies, waits for them, and re-layouts: 22.5 us -> none  [contract_first(): lax.dot_general(left, right, (((0,), (0,)), ((), ())), precision=precisio...]
    dot_general x11 -> x8, matrix products: 66.8 us -> 51.8 us  [contract_first(): lax.dot_general(left, right, (((0,), (0,)), ((), ())), precision=precisio...]
  transfers between devices with their start and end apart: 4 -> 4, of which waited for: 1 -> 3; matrix products, arithmetic and copies ran while one was open for 29% -> 14% of each run, Pallas kernels for 36% -> 26%
where the time goes in v3:
time: 842 us; the launch traced here: 831 us
  Pallas kernels  496 us (59%)
  matrix products  105 us (12%)
  waiting for transfers between devices  89 us (11%)
  local copies, waits for them, and re-layouts  69 us (8%)
  other arithmetic  38.1 us (5%)
  starting transfers between devices  18.1 us (2%)
  between operations  14.8 us (2%)
    pallas_call x2, Pallas kernels, scatter_sums(): pl.pallas_call(functools.partial(scatter_kernel, x_size, parts, pair), ou...  279 us
    pallas_call x1, Pallas kernels, ffn_tuned(): pl.pallas_call(functools.partial(ffn_kernel, 2), out_shape=[shape((8, 2,...  151 us
    pallas_call x2, Pallas kernels, pair_product(): pl.pallas_call(functools.partial(pair_kernel, chunks, len(extras)), out_s...  67.2 us
    dot_general x8, matrix products, contract_first(): lax.dot_general(left, right, (((0,), (0,)), ((), ())), precision=precisio...  51.8 us
    all_gather x1, waiting for transfers between devices, shards(): everyone_grad = lax.all_gather(grad_out, 'dp')  44.4 us
    reduce_scatter x1, waiting for transfers between devices, shards(): lax.psum_scatter(ffn_part.reshape(devices * rows_here, features), 'dp', s...  28.9 us
    unnamed x144, local copies, waits for them, and re-layouts  26.1 us
    all_to_all x1, starting transfers between devices, shards(): lax.all_to_all(shared_grads.reshape(3 * part, devices, share_rows).transp...  17.6 us
  transfers between devices with their start and end apart: 4, of which 3 were waited for; matrix products, arithmetic and copies ran while one was open for 14% of the time, Pallas kernels for 26%

profile of v3, /device:TPU:0, one launch (start us, length us, event | category | flops | bytes accessed | tf_op | source)
XLA Modules:
  0.0 831.0 jit_solution(109621437270121048)
XLA Ops:
  18.6 2.7 convolution_convert_fusion.4
  24.9 5.5 fusion.110
  37.4 30.5 %pair_product.2 = f32[256,2048]{1,0:T(8,128)} custom-call(bf16[256,1024]{1,0:T(8,128)(2,1)} %copy.309.left, bf16[2048,1024]{1,0:T(8,128)(2,1)} %right.2), custom_call_target="tpu_custom_call" | custom-call | tf_op jit(solution)/shard_map/pair_product/pallas_call | solution.py:342
  71.2 3.0 fusion.117
  75.1 3.2 constant_dynamic-slice_fusion
  95.4 44.4 %all-gather.3.cloned.1.call-done = bf16[4096,2048]{1,0:T(8,128)(2,1)} async-done(((bf16[256,2048]{1,0:T(8,128)(2,1)}), bf16[4096,2048]{1,0:T(8,128)(2,1)}) %all-gather.3.cloned.1.call-update) | async-done | bytes 16777232 | tf_op jit(solution)/shard_map/all_gather | solution.py:994
  139.8 150.5 %ffn.1 = (bf16[8,2,256,2048]{3,2,1,0:T(8,128)(2,1)}, bf16[8,2,256,2176]{3,2,1,0:T(8,128)(2,1)}, bf16[8,256,2048]{2,1,0:T(8,128)(2,1)}, bf16[8,256,2048]{2,1,0:T(...) custom-call(bf16[256,2048]{1,0:T(8,128)(2,1)} %multiply_convert_fusi, ...), custom_call_target="tpu_custom_call" | custom-call | tf_op jit(solution)/shard_map/ffn/pallas_call | solution.py:691
  291.7 189.7 %scatter_sums.2 = f32[256,2176]{1,0:T(8,128)} custom-call(bf16[16,256,2176]{2,1,0:T(8,128)(2,1)} %bitcast.112), custom_call_target="tpu_custom_call" | custom-call | tf_op jit(solution)/shard_map/scatter_sums/pallas_call | solution.py:275
  484.3 17.6 %all-to-all-start = ((bf16[16,128,264]{1,2,0:T(8,128)(2,1)}), bf16[16,128,264]{1,2,0:T(8,128)(2,1)}, u32[]{:S(2)}, u32[]{:S(2)}) async-start(bf16[16,128,264]{1,2,0:T(8,128)(2,1)} %copy.287), calls=%async_computation.1 | async-start | bytes 2162688 | tf_op jit(solution)/shard_map/all_to_all | solution.py:1018
  504.2 12.0 %convolution_bitcast_fusion.1 = f32[1,2048,704]{1,2,0:T(8,128)} fusion(bf16[2048,2048]{1,0:T(8,128)(2,1)} %bitcast.149, bf16[2048,768]{1,0:T(8,128)(2,1)} %bitcast.153), kind=kOutput, calls=%fused_computation.4 | convolution fusion | flops 5905580032 | bytes 17301504 | tf_op jit(solution)/shard_map/dot_general | solution.py:66
  516.3 10.5 %convolution_bitcast_fusion.2 = f32[1,2048,704]{1,2,0:T(8,128)} fusion(bf16[2048,2048]{1,0:T(8,128)(2,1)} %bitcast.150, bf16[2048,768]{1,0:T(8,128)(2,1)S(1)} %bitcast.152), kind=kOutput, calls=%fused_computation.5 | convolution fusion | flops 5905580032 | bytes 17301504 | tf_op jit(solution)/shard_map/dot_general | solution.py:66
  526.8 8.4 %convolution_bitcast_fusion = f32[1,2048,704]{1,2,0:T(8,128)} fusion(bf16[2048,2048]{1,0:T(8,128)(2,1)S(1)} %bitcast.148, bf16[2048,768]{1,0:T(8,128)(2,1)S(1)} %bitcast.151), kind=kOutput, calls=%fused_computation.3 | convolution fusion | flops 5905580032 | bytes 17301504 | tf_op jit(solution)/shard_map/dot_general | solution.py:66
  535.2 28.9 %reduce-scatter.2.cloned.1.call-done = bf16[256,2048]{1,0:T(8,128)(2,1)} async-done(((bf16[4096,2048]{1,0:T(8,128)(2,1)}), bf16[256,2048]{1,0:T(8,128)(2,1)}) %reduce-scatter.2.cloned.1.call-update) | async-done | bytes 1048592 | tf_op jit(solution)/shard_map/reduce_scatter | solution.py:1032
  564.1 6.7 multiply_reduce_fusion
  574.1 6.2 fusion.23
  580.3 2.6 fusion.114
  589.6 15.0 %all-reduce.7.cloned.1.call-done = bf16[256,2048]{1,0:T(8,128)(2,1)} async-done(((bf16[256,2048]{1,0:T(8,128)(2,1)}), bf16[256,2048]{1,0:T(8,128)(2,1)}) %all-reduce.7.cloned.1.call-update) | async-done | bytes 1048592 | tf_op jit(solution)/shard_map/psum | solution.py:1035
  604.6 4.7 multiply_add_fusion
  614.7 3.2 fusion.118
  619.2 5.6 fusion.52
  624.8 5.1 fusion.58
  629.9 5.7 fusion.55
  635.6 5.3 fusion.49
  655.1 36.7 %pair_product.3 = (f32[256,2048]{1,0:T(8,128)}, f32[256,576]{1,0:T(8,128)}) custom-call(bf16[256,1536]{1,0:T(8,128)(2,1)} %copy.281.left, bf16[2048,1536]{1,0:T(8,128)(2,1)} %right.3, bf16[256,576]{1,0:T(8,128)(2,1)} %pad_maximum_fusion.4.refs_0_), custom_call_target="tpu_custom_call" | custom-call | tf_op jit(solution)/shard_map/pair_product/pallas_call | solution.py:342
  694.0 5.1 convolution_convert_fusion.1
  701.3 4.6 convolution_convert_fusion
  706.2 2.6 fusion.13
  711.6 2.7 convolution_convert_fusion.3
  714.3 2.8 copy.282
  718.2 4.7 concatenate.51.refs_4_
  722.9 89.1 %scatter_sums.3 = (f32[128,1536]{1,0:T(8,128)}, f32[128,1024]{1,0:T(8,128)}, f32[32,2048]{1,0:T(8,128)}, f32[128,288]{1,0:T(8,128)}, f32[128,128]{1,0:T(8,128)}) custom-call(bf16[16,128,1536]{2,1,0:T(8,128)(2,1)} %bitcast.110, bf16[16,128,1024]{2,1,0:T(8,128)(2,1)} %bitcast.111, bf16[16,32,2048]{2,1,0:T(8,128)(2,1)} %bitcast.115, ...), custom_call_target="tpu_custom_call" | custom-call | tf_op jit(solution)/shard_map/scatter_sums/pallas_call | solution.py:275
  817.4 4.2 fusion.12
  (217 shorter events, 96.7 us)
Async XLA Ops:
  7.2 132.6 %all-gather.3.cloned.1.call-start = ((), (), s32[]{:S(2)}) async-start(), calls=%async_computation.4 | async-start | bytes 17825792 | tf_op jit(solution)/shard_map/all_gather | solution.py:994
  8.0 556.2 %reduce-scatter.2.cloned.1.call-start = ((), (), s32[]{:S(2)}) async-start(), calls=%async_computation.2 | async-start | bytes 17825792 | tf_op jit(solution)/shard_map/reduce_scatter | solution.py:1032
  11.4 13.5 %copy-start.43 = (f32[256]{0:T(256)}, f32[256]{0:T(256)S(1)}, u32[]{:S(2)}) copy-start(f32[256]{0:T(256)S(1)} %add_rsqrt_fusion.2) | copy-start | bytes 3076
  12.0 6.6 copy-start.48
  24.9 5.6 copy-start.40
  24.9 5.6 copy-start.41
  24.9 5.7 copy-start.32
  24.9 5.7 copy-start.34
  75.1 13.4 %copy-start.15 = (f32[256,16]{1,0:T(8,128)}, f32[256,16]{1,0:T(8,128)S(1)}, u32[]{:S(2)}) copy-start(f32[256,16]{1,0:T(8,128)S(1)} %copy.262) | copy-start | bytes 49156
  86.4 7.7 copy-start.2
  86.4 7.7 copy-start.46
  484.3 96.0 %all-to-all-start = ((bf16[16,128,264]{1,2,0:T(8,128)(2,1)}), bf16[16,128,264]{1,2,0:T(8,128)(2,1)}, u32[]{:S(2)}, u32[]{:S(2)}) async-start(bf16[16,128,264]{1,2,0:T(8,128)(2,1)} %copy.287), calls=%async_computation.1 | async-start | bytes 2162688 | tf_op jit(solution)/shard_map/all_to_all | solution.py:1018
  501.9 102.7 %all-reduce.7.cloned.1.call-start = ((), (), s32[]{:S(2)}) async-start(), calls=%async_computation.3 | async-start | bytes 2097152 | tf_op jit(solution)/shard_map/psum | solution.py:1035
  504.2 12.0 %copy-start.62 = (bf16[8,256,768]{2,1,0:T(8,128)(2,1)S(1)}, bf16[8,256,768]{2,1,0:T(8,128)(2,1)}, u32[]{:S(2)}) copy-start(bf16[8,256,768]{2,1,0:T(8,128)(2,1)} %get-tuple-element.42) | copy-start | bytes 9437188
  504.2 22.6 %slice-start = ((s8[8388608]{0:T(1024)(128)(4,1)}), s8[4194304]{0:T(1024)(128)(4,1)S(1)}, s32[]{:S(2)}) async-start(s8[8388608]{0:T(1024)(128)(4,1)} %bitcast.146), calls=%async_computation.5 | async-start | bytes 8388608
  516.2 10.5 %slice-start.1 = ((s8[8388608]{0:T(1024)(128)(4,1)}), s8[4194304]{0:T(1024)(128)(4,1)S(1)}, s32[]{:S(2)}) async-start(s8[8388608]{0:T(1024)(128)(4,1)} %bitcast.146), calls=%async_computation.6 | async-start | bytes 8388608
  516.2 10.5 %copy-start.61 = (bf16[8,256,768]{2,1,0:T(8,128)(2,1)S(1)}, bf16[8,256,768]{2,1,0:T(8,128)(2,1)}, u32[]{:S(2)}) copy-start(bf16[8,256,768]{2,1,0:T(8,128)(2,1)} %get-tuple-element.45) | copy-start | bytes 9437188
  582.9 21.7 %copy-start.47 = (f32[256]{0:T(256)S(1)}, f32[256]{0:T(256)}, u32[]{:S(2)}) copy-start(f32[256]{0:T(256)} %copy-done.45) | copy-start | bytes 3076
  582.9 21.7 %copy-start.58 = (f32[256]{0:T(256)S(1)}, f32[256]{0:T(256)}, u32[]{:S(2)}) copy-start(f32[256]{0:T(256)} %broadcast_multiply_fusion.2) | copy-start | bytes 3076
  604.6 6.0 copy-start.11
  612.6 5.3 copy-start.51
  619.2 5.6 copy-start.26
  629.9 5.7 copy-start.33
  629.9 5.7 copy-start.35
  647.8 5.5 copy-start.37
  647.8 5.5 copy-start.38
  655.1 36.7 %copy-start.8 = (f32[256,576]{1,0:T(8,128)S(1)}, f32[256,576]{1,0:T(8,128)}, u32[]{:S(2)}) copy-start(f32[256,576]{1,0:T(8,128)} %copy-done.7) | copy-start | bytes 1769476
  655.1 36.7 %copy-start.49 = (f32[512]{0:T(512)S(1)}, f32[512]{0:T(512)}, u32[]{:S(2)}) copy-start(f32[512]{0:T(512)} %param.25) | copy-start | bytes 6148
  655.1 36.7 %copy-start.53 = (f32[256]{0:T(256)S(1)}, f32[256]{0:T(256)}, u32[]{:S(2)}) copy-start(f32[256]{0:T(256)} %copy-done.52) | copy-start | bytes 3076
  694.0 12.2 %copy-start.30 = (bf16[256,64]{1,0:T(8,128)(2,1)}, bf16[256,64]{1,0:T(8,128)(2,1)S(1)}, u32[]{:S(2)}) copy-start(bf16[256,64]{1,0:T(8,128)(2,1)S(1)} %slice.201) | copy-start | bytes 98308
  694.0 5.1 copy-start.13
  817.4 5.1 copy-start.36
  (37 other events, 95.8 us)
Sparse Core Ops, SparseCore 0:
  10.2 129.5 all-gather.2
  290.5 273.5 reduce-scatter.1
  566.4 38.1 all-reduce.6

commit v4 on v3

--- a/solution.py
+++ b/solution.py
@@ -135,7 +135,7 @@
 
 def add_into(dst, *srcs):
     rows = dst.shape[0]
-    step = 32 if rows % 32 == 0 else 16
+    step = 32 if rows % 32 == 0 else 8
 
     def body(i, _):
         here = pl.ds(pl.multiple_of(i * step, step), step)
@@ -290,70 +290,6 @@
         ),
         name="scatter_sums",
     )(*arrays)
-
-
-def pair_kernel(chunks, extras, left, right, *refs):
-    ins, total, outs = refs[:extras], refs[extras], refs[extras + 1 : 2 * extras + 1]
-    sent, got, refs = refs[2 * extras + 1], refs[2 * extras + 2], refs[2 * extras + 3 :]
-    e_got, (s_sem, r_sem, es_sem, er_sem) = refs[:extras], refs[extras:]
-    width = total.shape[1] // chunks
-    other = {"tensor": 1 - lax.axis_index("tensor")}
-    barrier = pltpu.get_barrier_semaphore()
-    pl.semaphore_signal(barrier, inc=1, device_id=other, device_id_type=pl.DeviceIdType.MESH)
-    pl.semaphore_wait(barrier, 1)
-
-    def copy(src, dst, send_sem, recv_sem):
-        return pltpu.make_async_remote_copy(
-            src_ref=src,
-            dst_ref=dst,
-            send_sem=send_sem,
-            recv_sem=recv_sem,
-            device_id=other,
-            device_id_type=pl.DeviceIdType.MESH,
-        )
-
-    chunk = lambda i: copy(sent.at[i], got.at[i], s_sem.at[i], r_sem.at[i])
-    extra = lambda i: copy(ins[i], e_got[i], es_sem.at[i], er_sem.at[i])
-    for i in range(extras):
-        extra(i).start()
-    for i in range(chunks):
-        sent[i] = lax.dot_general(
-            left[...],
-            right[pl.ds(i * width, width), :],
-            (((1,), (1,)), ((), ())),
-            preferred_element_type=jnp.float32,
-        ).astype(jnp.bfloat16)
-        chunk(i).start()
-    for i in range(extras):
-        extra(i).wait()
-        outs[i][...] = ins[i][...].astype(jnp.float32) + e_got[i][...].astype(jnp.float32)
-    for i in range(chunks):
-        chunk(i).wait()
-        total[:, pl.ds(i * width, width)] = sent[i].astype(jnp.float32) + got[i].astype(
-            jnp.float32
-        )
-
-
-def pair_product(left, right, extras, collective_id, chunks=8):
-    rows, columns = left.shape[0], right.shape[0]
-    dma = pltpu.SemaphoreType.DMA
-    vmem = pl.BlockSpec(memory_space=pltpu.VMEM)
-    block = pltpu.VMEM((chunks, rows, columns // chunks), jnp.bfloat16)
-    return pl.pallas_call(
-        functools.partial(pair_kernel, chunks, len(extras)),
-        out_shape=[jax.ShapeDtypeStruct((rows, columns), jnp.float32)]
-        + [jax.ShapeDtypeStruct(e.shape, jnp.float32) for e in extras],
-        in_specs=[vmem] * (2 + len(extras)),
-        out_specs=[vmem] * (1 + len(extras)),
-        scratch_shapes=[block, block]
-        + [pltpu.VMEM(e.shape, e.dtype) for e in extras]
-        + [dma((chunks,))] * 2
-        + [dma((max(1, len(extras)),))] * 2,
-        compiler_params=pltpu.CompilerParams(
-            collective_id=collective_id, has_side_effects=True, vmem_limit_bytes=VMEM_LIMIT
-        ),
-        name="pair_product",
-    )(left, right, *extras)
 
 
 def nn(left, right):
@@ -409,6 +345,8 @@
     acc,
     gate_col,
     dgate_acc,
+    left_ffn,
+    left_grad,
     own_sem,
     up_s,
     up_r,
@@ -432,7 +370,7 @@
     at = functools.partial(index_of, x_size=x_size)
     ins, outs = (own_ffn, own_gates), (blk, gts)
     half = z // 2
-    order = [z, 1 - z + 4 * half, 2 - half, 3 - 3 * half]
+    order = [z, (1 - z) * (1 - 2 * half), 2 * (1 - half) + half * (7 - 2 * z), 3 - 3 * half]
 
     def place(j):
         return sum(is_at(j, i) * order[i] for i in range(4))
@@ -530,21 +468,29 @@
     upto = (earlier <= later).astype(bf16)
     slot_lane = lax.broadcasted_iota(jnp.int32, (rows_here, slots), 1).astype(f32)
 
-    def staged(pair):
+    def staged(pair, which):
+        pairs = [
+            (rows_b, rows_all),
+            (dy_b, dy_all),
+            (he_b, he_all),
+            (dge_b, dge_all),
+            (due_b, due_all),
+            (out_st, out_part),
+            (dx_st, dx_part),
+        ]
         return [
-            pltpu.make_async_copy(src, dst.at[pair], st_sem.at[i])
-            for i, (src, dst) in enumerate(
-                [
-                    (rows_b, rows_all),
-                    (dy_b, dy_all),
-                    (he_b, he_all),
-                    (dge_b, dge_all),
-                    (due_b, due_all),
-                    (out_st, out_part),
-                    (dx_st, dx_part),
-                ]
-            )
+            pltpu.make_async_copy(pairs[i][0], pairs[i][1].at[pair], st_sem.at[i]) for i in which
         ]
+
+    def start_staged(pair, which):
+        for copy in staged(pair, which):
+            copy.start()
+
+    def wait_staged(k, which):
+        @pl.when(k > 0)
+        def _():
+            for copy in staged(0, which):
+                copy.wait()
 
     def body(k, _):
         w, v = place(k // 2), x + (k % 2) * (1 - 2 * x)
@@ -563,11 +509,6 @@
         pl.when(k < 7)(lambda: grad_copy(k + 1).start())
         for a in (1, 0):
             beside(a, w, v).wait_recv()
-
-        @pl.when(k > 0)
-        def _():
-            for copy in staged(pair):
-                copy.wait()
 
         for a in range(2):
             gates = gts[block + a]
@@ -583,43 +524,48 @@
             parts = jnp.where(
                 lane == 0, high, jnp.where(lane == 1, middle, jnp.where(lane == 2, low, 0.0))
             ).astype(bf16)
-            picked = jnp.sum(contract_first(pick, parts), axis=1, keepdims=True)
+            pick_t = pick.T
+            left_ffn[a, pl.ds(0, slots), :] = pick_t
+            left_grad[a, pl.ds(0, slots), :] = pick_t
+            picked = jnp.sum(nn(pick_t, parts), axis=1, keepdims=True)
             gate_col[pl.ds(a * slots, slots), :] = jnp.broadcast_to(picked, (slots, 128))
+
+        both = pl.ds(block, 2)
+        pre = contract_last(blk[both].reshape(2 * rows_here, features), s_in[...])
+        grad_hidden = contract_last(g_buf[here].reshape(2 * rows_here, features), s_out[...])
+        act, slope = swish_parts(pre[:, :128])
+        up_pre = pre[:, 128:]
+        shared_units = (
+            (act * up_pre).astype(bf16),
+            (grad_hidden * up_pre * slope).astype(bf16),
+            (grad_hidden * act).astype(bf16),
+        )
+        for a in range(2):
+            mine = slice(a * rows_here, (a + 1) * rows_here)
+            out_l[a, :, pl.ds(slots, 128)] = shared_units[0][mine]
+            dx_l[a, :, pl.ds(slots, 128)] = shared_units[1][mine]
+            dx_l[a, :, pl.ds(slots + 128, 128)] = shared_units[2][mine]
+            left_ffn[a, pl.ds(slots, 128), :] = shared_units[1][mine].T
+            left_ffn[a, pl.ds(slots + 128, 128), :] = shared_units[2][mine].T
+            left_grad[a, pl.ds(slots, 128), :] = shared_units[0][mine].T
 
         def pick_rows(n, _):
             cols = pl.ds(pl.multiple_of(n * wide, wide), wide)
             for a in range(2):
                 mine = pl.ds(a * slots, slots)
-                pick = out_l[a, :, pl.ds(0, slots)]
-                rows_b[mine, cols] = contract_first(pick, blk[block + a, :, cols]).astype(bf16)
-                grows = contract_first(pick, g_buf[here, a, :, cols])
+                product = nn(left_ffn[a], blk[block + a, :, cols])
+                rows_b[mine, cols] = product[:slots].astype(bf16)
+                acc[pl.ds(0, 256), cols] += product[slots:]
+                product = nn(left_grad[a], g_buf[here, a, :, cols])
+                grows = product[:slots]
+                acc[pl.ds(256, 128), cols] += product[slots:]
                 grow_b[mine, cols] = grows.astype(bf16)
                 dy_b[mine, cols] = (gate_col[mine, pl.ds(0, 1)] * grows).astype(bf16)
             return 0
 
+        wait_staged(k, (0, 1))
         lax.fori_loop(0, features // wide, pick_rows, 0)
-
-        for a in range(2):
-            pre = contract_last(blk[block + a], s_in[...])
-            grad_hidden = contract_last(g_buf[here, a], s_out[...])
-            act, slope = swish_parts(pre[:, :128])
-            up_pre = pre[:, 128:]
-            out_l[a, :, pl.ds(slots, 128)] = (act * up_pre).astype(bf16)
-            dx_l[a, :, pl.ds(slots, 128)] = (grad_hidden * up_pre * slope).astype(bf16)
-            dx_l[a, :, pl.ds(slots + 128, 128)] = (grad_hidden * act).astype(bf16)
-
-        def shared_weights(n, _):
-            cols = pl.ds(pl.multiple_of(n * wide, wide), wide)
-            for a in range(2):
-                acc[pl.ds(0, 256), cols] += contract_first(
-                    dx_l[a, :, pl.ds(slots, 256)], blk[block + a, :, cols]
-                )
-                acc[pl.ds(256, 128), cols] += contract_first(
-                    out_l[a, :, pl.ds(slots, 128)], g_buf[here, a, :, cols]
-                )
-            return 0
-
-        lax.fori_loop(0, features // wide, shared_weights, 0)
+        start_staged(pair, (0, 1))
 
         def hidden_units(n, _):
             units = pl.ds(pl.multiple_of(n * 256, 256), 256)
@@ -632,7 +578,9 @@
             due_b[:, units] = (grad_hidden * act).astype(bf16)
             return 0
 
+        wait_staged(k, (2, 3, 4))
         lax.fori_loop(0, gate_v.shape[0] // 256, hidden_units, 0)
+        start_staged(pair, (2, 3, 4))
         dgate_acc[...] = jnp.zeros(dgate_acc.shape, f32)
 
         def back(n, _):
@@ -651,6 +599,7 @@
                 dx_st[a, :, cols] = nn(dx_l[a], dx_r[a, :, cols]).astype(bf16)
             return 0
 
+        wait_staged(k, (5, 6))
         lax.fori_loop(0, features // wide, back, 0)
         dgate = jnp.sum(dgate_acc[...], axis=1, keepdims=True)
         high = dgate.astype(bf16).astype(f32)
@@ -662,13 +611,11 @@
             dx_st[a, :, pl.ds(features, 128)] = nn(
                 out_l[a, :, pl.ds(0, slots)], spread[a * slots : (a + 1) * slots]
             ).astype(bf16)
-        for copy in staged(pair):
-            copy.start()
+        start_staged(pair, (5, 6))
         return 0
 
     lax.fori_loop(0, 8, body, 0)
-    for copy in staged(0):
-        copy.wait()
+    wait_staged(1, range(7))
     shared_grads[...] = acc[...].astype(bf16)
     for a in range(2):
         for w in range(z_size):
@@ -726,6 +673,8 @@
             pltpu.VMEM((384, features), f32),
             pltpu.VMEM((2 * slots, 128), f32),
             pltpu.VMEM((2 * slots, 128), f32),
+            pltpu.VMEM((2, slots + 256, rows), bf16),
+            pltpu.VMEM((2, slots + 128, rows), bf16),
             dma((2,)),
         ]
         + [dma((2, 4))] * 6
@@ -747,22 +696,481 @@
     )
 
 
-def tuned():
-    return lax.axis_size("dp") == 16 and lax.axis_size("tensor") == 2
-
-
-def sum_home(arrays, collective_id, pair=False):
-    if tuned():
-        return scatter_sums(arrays, 2, collective_id, jnp.float32, pair)
+def first_half(shape):
+    return lax.broadcasted_iota(jnp.int32, shape, 1) % 64 < 32
+
+
+def turn(values, cosine, sine):
+    partner = jnp.where(
+        first_half(values.shape), pltpu.roll(values, 96, 1), pltpu.roll(values, 32, 1)
+    )
+    return values * cosine + partner * sine
+
+
+def layout_of(lengths, rows, width):
+    row = lax.broadcasted_iota(jnp.int32, (rows, width), 0)
+    across = lax.broadcasted_iota(jnp.int32, (rows, rows), 1)
+    down = lax.broadcasted_iota(jnp.int32, (rows, rows), 0)
+    place, met, end = row, across <= down, 0
+    for i in range(lengths.shape[1]):
+        end = end + lengths[0, i]
+        place = place - jnp.where(row >= end, lengths[0, i], 0)
+        met = met & ((across >= end) == (down >= end))
+    return place, met
+
+
+def turn_tables(lengths, freqs, rows):
+    place, met = layout_of(lengths, rows, 128)
+    angles = place.astype(jnp.float32) * freqs[...]
+    sine = jnp.sin(angles)
+    return jnp.cos(angles), jnp.where(first_half(angles.shape), -sine, sine), met
+
+
+def pair_copy(src, dst, send_sem, recv_sem):
+    return pltpu.make_async_remote_copy(
+        src_ref=src,
+        dst_ref=dst,
+        send_sem=send_sem,
+        recv_sem=recv_sem,
+        device_id={"tensor": 1 - lax.axis_index("tensor")},
+        device_id_type=pl.DeviceIdType.MESH,
+    )
+
+
+def greet_pair():
+    barrier = pltpu.get_barrier_semaphore()
+    pl.semaphore_signal(
+        barrier,
+        inc=1,
+        device_id={"tensor": 1 - lax.axis_index("tensor")},
+        device_id_type=pl.DeviceIdType.MESH,
+    )
+    pl.semaphore_wait(barrier, 1)
+
+
+def forward_kernel(
+    lengths,
+    freqs,
+    tokens,
+    routes,
+    g_attn,
+    g_latent,
+    g_ffn,
+    router_t,
+    w_query,
+    down_t,
+    kv_up,
+    w_out,
+    hidden,
+    ffn_bf,
+    gates,
+    probs,
+    normed,
+    queries,
+    kv,
+    key_turned,
+    latent_bf,
+    latent,
+    context,
+    log_totals,
+    wq_v,
+    down_v,
+    up_v,
+    out_v,
+    sent,
+    got,
+    w_sem,
+    s_sem,
+    r_sem,
+):
+    bf16, f32 = jnp.bfloat16, jnp.float32
+    rows, features = tokens.shape
+    rank = kv_up.shape[0]
+    heads = kv_up.shape[1] // 256
+    turned = down_t.shape[0] - rank
+    tail = pl.ds(rank, turned)
+    loads = [
+        pltpu.make_async_copy(down_t, down_v.at[pl.ds(0, rank + turned)], w_sem.at[0]),
+        pltpu.make_async_copy(down_t.at[tail], down_v.at[pl.ds(rank + turned, turned)], w_sem.at[1]),
+        pltpu.make_async_copy(kv_up, up_v, w_sem.at[2]),
+        pltpu.make_async_copy(w_query, wq_v, w_sem.at[3]),
+        pltpu.make_async_copy(w_out, out_v, w_sem.at[4]),
+    ]
+    for copy in loads:
+        copy.start()
+    greet_pair()
+    cosine, sine, met = turn_tables(lengths, freqs, rows)
+    values, _, _ = rms_normalize_pieces(tokens[...].astype(f32), g_attn[...])
+    normed[...] = values.astype(bf16)
+    loads[0].wait()
+    loads[1].wait()
+    low = contract_last(normed[...], down_v[...])
+    latent[...] = low[:, :rank]
+    key_turned[...] = turn(low[:, rank:], cosine, sine).astype(bf16)
+    values, _, _ = rms_normalize_pieces(latent[...], g_latent[...])
+    latent_bf[...] = values.astype(bf16)
+    loads[2].wait()
+
+    def keys(n, _):
+        cols = pl.ds(pl.multiple_of(n * 512, 512), 512)
+        kv[:, cols] = nn(latent_bf[...], up_v[:, cols]).astype(bf16)
+        return 0
+
+    lax.fori_loop(0, kv.shape[1] // 512, keys, 0)
+    loads[3].wait()
+    lane = lax.broadcasted_iota(jnp.int32, (rows, 128), 1)
+    log_totals[...] = jnp.zeros(log_totals.shape, f32)
+
+    def two_heads(i, _):
+        three = nn(normed[...], wq_v[:, pl.ds(pl.multiple_of(i * 384, 384), 384)])
+        middle, last = three[:, 128:256], three[:, 256:]
+        plain = (
+            three[:, :128],
+            jnp.where(lane < 64, pltpu.roll(middle, 64, 1), pltpu.roll(last, 64, 1)),
+        )
+        spun = turn(jnp.where(lane < 64, middle, last), cosine, sine)
+        for b in range(2):
+            head = 2 * i + b
+            queries[head, :, pl.ds(0, 128)] = plain[b].astype(bf16)
+            queries[head, :, pl.ds(128, 128)] = jnp.where(
+                (lane < 64) == (b == 0), spun, 0.0
+            ).astype(bf16)
+            at = pl.multiple_of(head * 256, 256)
+            key = jnp.concatenate([kv[:, pl.ds(at, 128)], key_turned[...]], axis=1)
+            raw = contract_last(queries[head], key)
+            scores = jnp.where(met, raw * QK ** (-0.5), -jnp.inf)
+            top = jnp.max(scores, axis=1, keepdims=True)
+            expo = jnp.exp(scores - top)
+            total = jnp.sum(expo, axis=1, keepdims=True)
+            log_totals[...] = jnp.where(lane == head, top + jnp.log(total), log_totals[...])
+            context[:, pl.ds(pl.multiple_of(head * 128, 128), 128)] = nn(
+                (expo / total).astype(bf16), kv[:, pl.ds(at + 128, 128)]
+            ).astype(bf16)
+        return 0
+
+    lax.fori_loop(0, heads // 2, two_heads, 0)
+    loads[4].wait()
+    chunks, width = sent.shape[0], sent.shape[2]
+    chunk = lambda i: pair_copy(sent.at[i], got.at[i], s_sem.at[i], r_sem.at[i])
+
+    def project(i, _):
+        sent[i] = contract_last(
+            context[...], out_v[pl.ds(pl.multiple_of(i * width, width), width), :]
+        ).astype(bf16)
+        chunk(i).start()
+        return 0
+
+    lax.fori_loop(0, chunks, project, 0)
+
+    def join(i, _):
+        chunk(i).wait()
+        cols = pl.ds(pl.multiple_of(i * width, width), width)
+        hidden[:, cols] = tokens[:, cols].astype(f32) + (sent[i].astype(f32) + got[i].astype(f32))
+        return 0
+
+    lax.fori_loop(0, chunks, join, 0)
+    values, _, _ = rms_normalize_pieces(hidden[...], g_ffn[...])
+    ffn_bf[...] = values.astype(bf16)
+    experts = lax.axis_size("dp")
+    logits = lax.dot_general(
+        values,
+        router_t[...],
+        (((1,), (1,)), ((), ())),
+        precision=lax.Precision.HIGHEST,
+        preferred_element_type=f32,
+    )
+    logits = jnp.where(lane < experts, logits, -jnp.inf)
+    expo = jnp.exp(logits - jnp.max(logits, axis=1, keepdims=True))
+    share = expo / jnp.sum(expo, axis=1, keepdims=True)
+    probs[...] = share
+    named = lane < 0
+    for i in range(routes.shape[1]):
+        named = named | (lane == routes[:, pl.ds(i, 1)])
+    gates[...] = jnp.where(named, share, -1.0)
+
+
+def forward_tuned(
+    lengths, freqs, tokens, routes, g_attn, g_latent, g_ffn, router_t, w_query, down_t, kv_up, w_out
+):
+    rows, features = tokens.shape
+    rank, columns = kv_up.shape
+    heads = columns // 256
+    bf16, f32, dma = jnp.bfloat16, jnp.float32, pltpu.SemaphoreType.DMA
+    vmem, anywhere = pl.BlockSpec(memory_space=pltpu.VMEM), pl.BlockSpec(memory_space=pl.ANY)
+    smem = pl.BlockSpec(memory_space=pltpu.SMEM)
+    shape = jax.ShapeDtypeStruct
+    chunks = 8
+    return pl.pallas_call(
+        forward_kernel,
+        out_shape=[
+            shape((rows, features), f32),
+            shape((rows, features), bf16),
+            shape((rows, 128), f32),
+            shape((rows, 128), f32),
+            shape((rows, features), bf16),
+            shape((heads, rows, 256), bf16),
+            shape((rows, columns), bf16),
+            shape((rows, 128), bf16),
+            shape((rows, rank), bf16),
+            shape((rows, rank), f32),
+            shape((rows, heads * 128), bf16),
+            shape((rows, 128), f32),
+        ],
+        in_specs=[smem] + [vmem] * 7 + [anywhere] * 4,
+        out_specs=[vmem] * 12,
+        scratch_shapes=[
+            pltpu.VMEM(w_query.shape, bf16),
+            pltpu.VMEM((rank + 128, features), bf16),
+            pltpu.VMEM(kv_up.shape, bf16),
+            pltpu.VMEM(w_out.shape, bf16),
+            pltpu.VMEM((chunks, rows, features // chunks), bf16),
+            pltpu.VMEM((chunks, rows, features // chunks), bf16),
+            dma((5,)),
+            dma((chunks,)),
+            dma((chunks,)),
+        ],
+        compiler_params=pltpu.CompilerParams(
+            collective_id=2, has_side_effects=True, vmem_limit_bytes=VMEM_LIMIT
+        ),
+        name="attention_forward",
+    )(lengths, freqs, tokens, routes, g_attn, g_latent, g_ffn, router_t, w_query, down_t, kv_up, w_out)
+
+
+def backward_kernel(
+    lengths,
+    freqs,
+    sums,
+    hidden,
+    grad_out,
+    tokens,
+    probs,
+    g_attn,
+    g_latent,
+    g_ffn,
+    router_t,
+    queries,
+    kv,
+    key_turned,
+    latent,
+    log_totals,
+    w_query,
+    down_t,
+    kv_up,
+    w_out,
+    grad_tokens,
+    grad_hidden_bf,
+    grad_query,
+    grad_kv,
+    grad_low,
+    vectors,
+    wq_v,
+    down_v,
+    up_v,
+    out_v,
+    unit,
+    grad_hidden,
+    grad_context,
+    grad_turned,
+    sent,
+    got,
+    low_sent,
+    low_got,
+    w_sem,
+    s_sem,
+    r_sem,
+    e_sem,
+):
+    bf16, f32 = jnp.bfloat16, jnp.float32
+    highest = lax.Precision.HIGHEST
+    rows, features = tokens.shape
+    rank = kv_up.shape[0]
+    heads = kv_up.shape[1] // 256
+    turned = down_t.shape[0] - rank
+    tail = pl.ds(rank, turned)
+    loads = [
+        pltpu.make_async_copy(w_out, out_v, w_sem.at[0]),
+        pltpu.make_async_copy(kv_up, up_v, w_sem.at[1]),
+        pltpu.make_async_copy(w_query, wq_v, w_sem.at[2]),
+        pltpu.make_async_copy(down_t, down_v.at[pl.ds(0, rank + turned)], w_sem.at[3]),
+        pltpu.make_async_copy(down_t.at[tail], down_v.at[pl.ds(rank + turned, turned)], w_sem.at[4]),
+    ]
+    for copy in loads:
+        copy.start()
+    greet_pair()
+    cosine, sine, met = turn_tables(lengths, freqs, rows)
+    lane = lax.broadcasted_iota(jnp.int32, (rows, 128), 1)
+    experts = lax.axis_size("dp")
+
+    extra = sums[:, pl.ds(features, 128)]
+    dense = extra + pltpu.roll(extra, 128 - experts, 1)
+    share = probs[...]
+    dense = jnp.where(lane < experts, dense, 0.0)
+    logits = share * (dense - jnp.sum(share * dense, axis=1, keepdims=True))
+    grad_in = sums[:, pl.ds(0, features)] + lax.dot_general(
+        logits,
+        router_t[...],
+        (((1,), (0,)), ((), ())),
+        precision=highest,
+        preferred_element_type=f32,
+    )
+    values, unit_rows, factor = rms_normalize_pieces(hidden[...], g_ffn[...])
+    unit[...] = unit_rows
+    vectors[pl.ds(0, experts), :] = lax.dot_general(
+        logits, values, (((0,), (0,)), ((), ())), precision=highest, preferred_element_type=f32
+    )[:experts]
+    vectors[pl.ds(experts, 8), :] = jnp.zeros((8, features), f32)
+    vectors[pl.ds(experts + 1, 1), :] = jnp.sum(grad_in * unit[...], axis=0, keepdims=True)
+    grad_hidden[...] = grad_out[...].astype(f32) + normalize_back(
+        grad_in, unit[...], factor, g_ffn[...]
+    )
+    grad_hidden_bf[...] = grad_hidden[...].astype(bf16)
+    loads[0].wait()
+
+    def back_out(n, _):
+        cols = pl.ds(pl.multiple_of(n * 256, 256), 256)
+        grad_context[:, cols] = nn(grad_hidden_bf[...], out_v[:, cols]).astype(bf16)
+        return 0
+
+    lax.fori_loop(0, grad_context.shape[1] // 256, back_out, 0)
+    grad_turned[...] = jnp.zeros(grad_turned.shape, f32)
+
+    def two_heads(i, _):
+        pieces = []
+        for b in range(2):
+            head = 2 * i + b
+            at = pl.multiple_of(head * 256, 256)
+            key = jnp.concatenate([kv[:, pl.ds(at, 128)], key_turned[...]], axis=1)
+            value = kv[:, pl.ds(at + 128, 128)]
+            raw = contract_last(queries[head], key)
+            log_total = jnp.sum(
+                jnp.where(lane == head, log_totals[...], 0.0), axis=1, keepdims=True
+            )
+            weights = jnp.exp(jnp.where(met, raw * QK ** (-0.5), -jnp.inf) - log_total)
+            grad_ctx = grad_context[:, pl.ds(pl.multiple_of(head * 128, 128), 128)]
+            grad_weights = contract_last(grad_ctx, value)
+            inner = jnp.sum(weights * grad_weights, axis=1, keepdims=True)
+            grad_raw = (weights * (grad_weights - inner) * QK ** (-0.5)).astype(bf16)
+            pieces.append(nn(grad_raw, key))
+            back_key = contract_first(grad_raw, queries[head])
+            grad_kv[:, pl.ds(at, 128)] = back_key[:, :128].astype(bf16)
+            grad_turned[...] += back_key[:, 128:]
+            grad_kv[:, pl.ds(at + 128, 128)] = contract_first(
+                weights.astype(bf16), grad_ctx
+            ).astype(bf16)
+        even, odd = pieces
+        spun = turn(jnp.where(lane < 64, even[:, 128:], odd[:, 128:]), cosine, -sine)
+        moved = pltpu.roll(odd[:, :128], 64, 1)
+        start = pl.multiple_of(i * 384, 384)
+        grad_query[:, pl.ds(start, 128)] = even[:, :128].astype(bf16)
+        grad_query[:, pl.ds(start + 128, 128)] = jnp.where(lane < 64, spun, moved).astype(bf16)
+        grad_query[:, pl.ds(start + 256, 128)] = jnp.where(lane < 64, moved, spun).astype(bf16)
+        return 0
+
+    lax.fori_loop(0, heads // 2, two_heads, 0)
+    loads[1].wait()
+    low_sent[:, pl.ds(0, rank)] = contract_last(grad_kv[...], up_v[...]).astype(bf16)
+    folded = turn(grad_turned[...] + pltpu.roll(grad_turned[...], 64, 1), cosine, -sine)
+    low_sent[:, pl.ds(rank, 128)] = jnp.where(lane < turned, folded, 0.0).astype(bf16)
+    low_copy = pair_copy(low_sent, low_got, e_sem.at[0], e_sem.at[1])
+    low_copy.start()
+    loads[2].wait()
+    chunks, width = sent.shape[0], sent.shape[2]
+    chunk = lambda i: pair_copy(sent.at[i], got.at[i], s_sem.at[i], r_sem.at[i])
+
+    def project(i, _):
+        sent[i] = contract_last(
+            grad_query[...], wq_v[pl.ds(pl.multiple_of(i * width, width), width), :]
+        ).astype(bf16)
+        chunk(i).start()
+        return 0
+
+    lax.fori_loop(0, chunks, project, 0)
+    loads[3].wait()
+    loads[4].wait()
+    low_copy.wait()
+    low = low_sent[...].astype(f32) + low_got[...].astype(f32)
+    grad_normed = low[:, :rank]
+    _, latent_unit, latent_factor = rms_normalize_pieces(latent[...], g_latent[...])
+    grad_gain = jnp.sum(grad_normed * latent_unit, axis=0, keepdims=True)
+    for i in range(rank // 128):
+        vectors[pl.ds(experts + 2 + i, 1), pl.ds(0, 128)] = grad_gain[:, i * 128 : (i + 1) * 128]
+    grad_low[:, pl.ds(0, rank)] = normalize_back(
+        grad_normed, latent_unit, latent_factor, g_latent[...]
+    ).astype(bf16)
+    grad_low[:, pl.ds(rank, 128)] = low[:, rank:].astype(bf16)
+
+    def join(i, _):
+        cols = pl.ds(pl.multiple_of(i * width, width), width)
+        product = nn(grad_low[...], down_v[:, cols])
+        chunk(i).wait()
+        unit[:, cols] = product + (sent[i].astype(f32) + got[i].astype(f32))
+        return 0
+
+    lax.fori_loop(0, chunks, join, 0)
+    _, attn_unit, attn_factor = rms_normalize_pieces(tokens[...].astype(f32), g_attn[...])
+    vectors[pl.ds(experts, 1), :] = jnp.sum(unit[...] * attn_unit, axis=0, keepdims=True)
+    grad_tokens[...] = grad_hidden[...] + normalize_back(
+        unit[...], attn_unit, attn_factor, g_attn[...]
+    )
+
+
+def backward_tuned(lengths, freqs, sums, values, gains, router_t, saved, weights):
+    hidden, grad_out, tokens, probs = values
+    w_query, down_t, kv_up, w_out = weights
+    rows, features = tokens.shape
+    rank, columns = kv_up.shape
+    heads = columns // 256
+    bf16, f32, dma = jnp.bfloat16, jnp.float32, pltpu.SemaphoreType.DMA
+    vmem, anywhere = pl.BlockSpec(memory_space=pltpu.VMEM), pl.BlockSpec(memory_space=pl.ANY)
+    smem = pl.BlockSpec(memory_space=pltpu.SMEM)
+    shape = jax.ShapeDtypeStruct
+    chunks = 8
+    experts = lax.axis_size("dp")
+    return pl.pallas_call(
+        backward_kernel,
+        out_shape=[
+            shape((rows, features), f32),
+            shape((rows, features), bf16),
+            shape((rows, w_query.shape[1]), bf16),
+            shape((rows, columns), bf16),
+            shape((rows, rank + 128), bf16),
+            shape((experts + 8, features), f32),
+        ],
+        in_specs=[smem] + [vmem] * 15 + [anywhere] * 4,
+        out_specs=[vmem] * 6,
+        scratch_shapes=[
+            pltpu.VMEM(w_query.shape, bf16),
+            pltpu.VMEM((rank + 128, features), bf16),
+            pltpu.VMEM(kv_up.shape, bf16),
+            pltpu.VMEM(w_out.shape, bf16),
+            pltpu.VMEM((rows, features), f32),
+            pltpu.VMEM((rows, features), f32),
+            pltpu.VMEM((rows, heads * 128), bf16),
+            pltpu.VMEM((rows, 128), f32),
+            pltpu.VMEM((chunks, rows, features // chunks), bf16),
+            pltpu.VMEM((chunks, rows, features // chunks), bf16),
+            pltpu.VMEM((rows, rank + 128), bf16),
+            pltpu.VMEM((rows, rank + 128), bf16),
+            dma((5,)),
+            dma((chunks,)),
+            dma((chunks,)),
+            dma((2,)),
+        ],
+        compiler_params=pltpu.CompilerParams(
+            collective_id=4, has_side_effects=True, vmem_limit_bytes=VMEM_LIMIT
+        ),
+        name="attention_backward",
+    )(lengths, freqs, sums, hidden, grad_out, tokens, probs, *gains, router_t, *saved, *weights)
+
+
+def sum_home(arrays, pair=False):
     sums = [lax.psum_scatter(a, "dp", scatter_dimension=0) for a in arrays]
     if pair:
         sums = [lax.psum(a.astype(jnp.float32), "tensor") for a in sums]
     return [a.astype(jnp.float32) for a in sums]
 
 
-def product_sum(left, right, extras, collective_id):
-    if tuned():
-        return pair_product(left, right, extras, collective_id)
+def product_sum(left, right, extras):
     product = contract_last(left, right).astype(jnp.bfloat16)
     return [lax.psum(a, "tensor").astype(jnp.float32) for a in [product] + extras]
 
@@ -896,6 +1304,135 @@
         grad_expert_up,
         grad_expert_down,
         shared_grads,
+    )
+
+
+def shared_home(grads, part):
+    devices = lax.axis_size("dp")
+    share_rows = grads.shape[1] // devices
+    grads = lax.all_to_all(
+        grads.reshape(3 * part, devices, share_rows).transpose(1, 2, 0).astype(jnp.bfloat16),
+        "dp",
+        split_axis=0,
+        concat_axis=0,
+    ).astype(jnp.float32)
+    return [
+        grads[:, :, i * part : (i + 1) * part].transpose(1, 0, 2).reshape(share_rows, -1)
+        for i in range(3)
+    ]
+
+
+def shards_tuned(
+    tokens,
+    lengths,
+    routes,
+    grad_out,
+    g_attn,
+    w_query,
+    key_value_down_weight,
+    latent_norm_gain,
+    key_value_up_weight,
+    w_out,
+    g_ffn,
+    router,
+    shared_gate,
+    shared_up,
+    shared_down,
+    expert_gate,
+    expert_up,
+    expert_down,
+):
+    rows_here, features = tokens.shape
+    devices, ranks = lax.axis_size("dp"), lax.axis_size("tensor")
+    own, rank = lax.axis_index("dp"), lax.axis_index("tensor")
+    experts = router.shape[1]
+    capacity = rows_here * TOPK * 4 // (3 * devices)
+    half = (key_value_down_weight.shape[1] - LATENT_RANK) // 2
+    freqs = 10000.0 ** (-jnp.arange(half, dtype=jnp.float32) / half)
+    freqs = jnp.tile(freqs, 128 // half)[None, :]
+    router_t = jnp.pad(router.T, ((0, 128 - experts), (0, 0)))
+    gains = [g_attn[None, :], latent_norm_gain[None, :], g_ffn[None, :]]
+    weights = [w_query, key_value_down_weight.T, key_value_up_weight, w_out]
+    everyone_grad = lax.all_gather(grad_out, "dp")
+    hidden, ffn_bf, dense_gates, probs, normed, *saved = forward_tuned(
+        lengths, freqs, tokens, routes, *gains, router_t, *weights
+    )
+    queries, kv, key_turned, latent_bf, latent, context, log_totals = saved
+    part = shared_gate.shape[1] // devices
+    shared_parts = [
+        lax.dynamic_slice_in_dim(w, own * part, part, 1)
+        for w in (shared_gate, shared_up, shared_down)
+    ]
+    ffn_part, grad_ffn_part, *expert_grads, shared_grads = ffn_with_kernel(
+        ffn_bf,
+        dense_gates,
+        everyone_grad,
+        [w[0] for w in (expert_gate, expert_up, expert_down)],
+        shared_parts,
+        capacity,
+        experts,
+    )
+    shared_grads = shared_home(shared_grads, part)
+    ffn_total = lax.psum_scatter(
+        ffn_part.reshape(devices * rows_here, features), "dp", scatter_dimension=0, tiled=True
+    )
+    ffn_total = lax.psum(ffn_total, "tensor").astype(jnp.float32)
+    output = (hidden + ffn_total).astype(jnp.bfloat16)
+    (sums,) = scatter_sums([grad_ffn_part], 2, 3, jnp.float32, True)
+    grad_tokens, grad_hidden_bf, grad_query, grad_kv, grad_low, vectors = backward_tuned(
+        lengths,
+        freqs,
+        sums,
+        [hidden, grad_out, tokens, probs],
+        gains,
+        router_t,
+        [queries, kv, key_turned, latent, log_totals],
+        weights,
+    )
+    share_rows = features // devices
+    columns = key_value_down_weight.shape[1]
+    grad_columns = lax.dynamic_slice_in_dim(
+        grad_low, rank * (columns // ranks), columns // ranks, 1
+    )
+    products = [
+        contract_first(normed, grad_query),
+        contract_first(grad_hidden_bf, context),
+        contract_first(latent_bf, grad_kv),
+        contract_first(normed, grad_columns),
+    ]
+    blocks = [
+        a.astype(jnp.bfloat16).reshape(devices, a.shape[0] // devices, a.shape[1])
+        for a in products
+    ]
+    vectors = vectors.reshape(experts + 8, devices, share_rows).transpose(1, 0, 2)
+    vectors = vectors.at[:, experts + 2 : experts + 2 + LATENT_RANK // 128].set(
+        vectors[:1, experts + 2 : experts + 2 + LATENT_RANK // 128]
+    )
+    grad_w_query, grad_w_out, grad_w_kv_up, grad_w_kv_down, vectors = scatter_sums(
+        blocks + [vectors], 2, 5, jnp.float32
+    )
+    router_rows = share_rows // ranks
+    grad_router = lax.dynamic_slice_in_dim(vectors[:experts], rank * router_rows, router_rows, 1).T
+    latent_rows = LATENT_RANK // devices // ranks
+    grad_g_kv = lax.dynamic_slice_in_dim(
+        vectors[experts + 2 : experts + 2 + LATENT_RANK // 128].reshape(-1),
+        (own * ranks + rank) * latent_rows,
+        latent_rows,
+        0,
+    )
+    return (
+        output,
+        grad_tokens,
+        vectors[experts],
+        grad_w_query,
+        grad_w_kv_down,
+        grad_g_kv,
+        grad_w_kv_up,
+        grad_w_out,
+        vectors[experts + 1],
+        grad_router,
+        *shared_grads,
+        *expert_grads,
     )
 
 
@@ -982,7 +1519,7 @@
     attn_weights = (expo / total).astype(jnp.bfloat16)
     context = jnp.einsum("hts,shd->thd", attn_weights, value, preferred_element_type=jnp.float32)
     context = context.astype(jnp.bfloat16).reshape(rows_here, heads_local * VALUE_HEAD_SIZE)
-    (attn,) = product_sum(context, w_out, [], 2)
+    (attn,) = product_sum(context, w_out, [])
     hidden = tokens_f + attn
     ffn_normed, ffn_unit, ffn_factor = rms_normalize_pieces(hidden, g_ffn)
     ffn_bf = ffn_normed.astype(jnp.bfloat16)
@@ -997,7 +1534,6 @@
         lax.dynamic_slice_in_dim(w, own * part, part, 1)
         for w in (shared_gate, shared_up, shared_down)
     ]
-    feed_forward = ffn_with_kernel if tuned() else ffn_plain
     (
         ffn_part,
         grad_ffn_part,
@@ -1005,7 +1541,7 @@
         grad_expert_up,
         grad_expert_down,
         shared_grads,
-    ) = feed_forward(
+    ) = ffn_plain(
         ffn_bf,
         dense_gates,
         everyone_grad,
@@ -1015,18 +1551,7 @@
         experts,
     )
     share_rows = features // devices
-    shared_grads = lax.all_to_all(
-        shared_grads.reshape(3 * part, devices, share_rows).transpose(1, 2, 0),
-        "dp",
-        split_axis=0,
-        concat_axis=0,
-    ).astype(jnp.float32)
-    grad_shared_gate, grad_shared_up, grad_shared_down = (
-        shared_grads[:, :, i * part : (i + 1) * part]
-        .transpose(1, 0, 2)
-        .reshape(share_rows, devices * part)
-        for i in range(3)
-    )
+    grad_shared_gate, grad_shared_up, grad_shared_down = shared_home(shared_grads, part)
 
     grad_top = grad_out.astype(jnp.float32)
     ffn_total = lax.psum_scatter(
@@ -1034,7 +1559,7 @@
     )
     ffn_total = lax.psum(ffn_total, "tensor").astype(jnp.float32)
     output = (hidden + ffn_total).astype(jnp.bfloat16)
-    (grad_ffn_sum,) = sum_home([grad_ffn_part], 3, True)
+    (grad_ffn_sum,) = sum_home([grad_ffn_part], True)
     dense_grad = (
         grad_ffn_sum[:, features : features + experts]
         + grad_ffn_sum[:, features + experts : features + 2 * experts]
@@ -1093,7 +1618,7 @@
     grad_latent_part = jnp.concatenate(
         [grad_latent_normed, apply_rotation(grad_key_rot, -token_position)], axis=1
     ).astype(jnp.bfloat16)
-    grad_in_summed, grad_latent_sum = product_sum(grad_query, w_query, [grad_latent_part], 4)
+    grad_in_summed, grad_latent_sum = product_sum(grad_query, w_query, [grad_latent_part])
     grad_latent_normed = grad_latent_sum[:, :LATENT_RANK]
     grad_g_kv = jnp.sum(grad_latent_normed * latent_unit_scale, axis=0)
     grad_latent = normalize_back(
@@ -1126,7 +1651,7 @@
         for a in (grad_w_query, grad_w_out, grad_w_kv_up, grad_w_kv_down)
     ]
     grad_w_query, grad_w_out, grad_w_kv_up, grad_w_kv_down, vectors = sum_home(
-        blocks + [vectors.reshape(devices, share_rows, 128)], 5
+        blocks + [vectors.reshape(devices, share_rows, 128)]
     )
     rank, ranks = lax.axis_index("tensor"), lax.axis_size("tensor")
     router_rows = share_rows // ranks
@@ -1194,4 +1719,6 @@
         P("dp", None, "tensor"),
         P("dp", None, "tensor"),
     )
-    return jax.shard_map(shards, mesh=mesh, in_specs=in_specs, out_specs=out_specs, check_vma=False)
+    tuned = mesh.shape["dp"] == 16 and mesh.shape["tensor"] == 2
+    return jax.shard_map(
+        shards_tuned if tuned else shards, mesh=mesh, in_specs=in_specs, out_specs=out_specs, check_vma=False)

time: 842 us -> 691 us (0.82)
  matrix products: 105 us -> 42.6 us
  local copies, waits for them, and re-layouts: 69 us -> 27.5 us
  other arithmetic: 38.1 us -> 3.72 us
  starting transfers between devices: 18.1 us -> 7.78 us
  Pallas kernels: 496 us -> 506 us
    dot_general x17 -> x0, matrix products: 53.6 us -> none  [the longest x3 10.7 us: contract_last(): lax.dot_general(left, right, (((1,), (1,)), ((), ())), precision=precisio...]
    all_gather x1, waiting for transfers between devices: 44.4 us -> 81.3 us  [shards_tuned(): everyone_grad = lax.all_gather(grad_out, 'dp')]
    reduce_scatter x1, waiting for transfers between devices: 28.9 us -> 0.01 us  [shards_tuned(): lax.psum_scatter(ffn_part.reshape(devices * rows_here, features), 'dp', s...]
    pallas_call x2, Pallas kernels: 67.2 us -> 93.1 us  [the longest x1 51 us: backward_tuned(): pl.pallas_call(backward_kernel, out_shape=[shape((rows, features), f32),...]
    psum x1, waiting for transfers between devices: 15 us -> 0.01 us  [shards_tuned(): ffn_total = lax.psum(ffn_total, 'tensor').astype(jnp.float32)]
    unnamed x144 -> x49, local copies, waits for them, and re-layouts: 26.1 us -> 12.1 us
    pallas_call x1, Pallas kernels: 151 us -> 137 us  [ffn_tuned(): pl.pallas_call(functools.partial(ffn_kernel, 2), out_shape=[shape((8, 2,...]
    add x3 -> x0, other arithmetic: 10.2 us -> none  [the longest x1 4.66 us: shards(): grad_top + normalize_back(grad_ffn_total, ffn_unit, ffn_factor, g_ffn)]
  transfers between devices with their start and end apart: 4 -> 4, of which waited for: 3 -> 1; matrix products, arithmetic and copies ran while one was open for 14% -> 10% of each run, Pallas kernels for 26% -> 54%
where the time goes in v4:
time: 691 us; the launch traced here: 684 us
  Pallas kernels  506 us (73%)
  waiting for transfers between devices  82 us (12%)
  matrix products  42.6 us (6%)
  local copies, waits for them, and re-layouts  27.5 us (4%)
  between operations  14.5 us (2%)
  starting transfers between devices  7.78 us (1%)
    pallas_call x2, Pallas kernels, scatter_sums(): pl.pallas_call(functools.partial(scatter_kernel, x_size, parts, pair), ou...  276 us
    pallas_call x1, Pallas kernels, ffn_tuned(): pl.pallas_call(functools.partial(ffn_kernel, 2), out_shape=[shape((8, 2,...  137 us
    all_gather x1, waiting for transfers between devices, shards_tuned(): everyone_grad = lax.all_gather(grad_out, 'dp')  81.3 us
    pallas_call x1, Pallas kernels, backward_tuned(): pl.pallas_call(backward_kernel, out_shape=[shape((rows, features), f32),...  51 us
    dot_general x7, matrix products, contract_first(): lax.dot_general(left, right, (((0,), (0,)), ((), ())), precision=precisio...  42.6 us
    pallas_call x1, Pallas kernels, forward_tuned(): pl.pallas_call(forward_kernel, out_shape=[shape((rows, features), f32), s...  42.1 us
  transfers between devices with their start and end apart: 4, of which 1 were waited for; matrix products, arithmetic and copies ran while one was open for 10% of the time, Pallas kernels for 54%

profile of v4, /device:TPU:0, one launch (start us, length us, event | category | flops | bytes accessed | tf_op | source)
XLA Modules:
  0.0 684.1 jit_solution(6247002451943012224)
XLA Ops:
  8.0 2.0 constant_dynamic-slice_fusion
  10.2 1.5 constant_dynamic-slice_fusion.2
  12.4 0.8 copy.64.routes
  13.5 1.1 pad.16.router_t
  14.5 0.8 pad.19.shared_out
  15.4 42.1 %attention_forward.1 = (f32[256,2048]{1,0:T(8,128)}, bf16[256,2048]{1,0:T(8,128)(2,1)}, f32[256,128]{1,0:T(8,128)}, f32[256,128]{1,0:T(8,128)}, bf16[256,2048]{1...) custom-call(s32[1,4]{1,0:T(1,128)} %lengths.3, ...), custom_call_target="tpu_custom_call" | custom-call | tf_op jit(solution)/shard_map/attention_forward/pallas_call | solution.py:903
  57.5 1.1 fusion.5.shared_in
  58.6 81.3 %all-gather.3.cloned.1.call-done = bf16[4096,2048]{1,0:T(8,128)(2,1)} async-done(((bf16[256,2048]{1,0:T(8,128)(2,1)}), bf16[4096,2048]{1,0:T(8,128)(2,1)}) %all-gather.3.cloned.1.call-update) | async-done | bytes 16777232 | tf_op jit(solution)/shard_map/all_gather | solution.py:1356
  139.9 136.6 %ffn.1 = (bf16[8,2,256,2048]{3,2,1,0:T(8,128)(2,1)}, bf16[8,2,256,2176]{3,2,1,0:T(8,128)(2,1)}, bf16[8,256,2048]{2,1,0:T(8,128)(2,1)}, bf16[8,256,2048]{2,1,0:T(...) custom-call(bf16[256,2048]{1,0:T(8,128)(2,1)} %get-tuple-element.60., ...), custom_call_target="tpu_custom_call" | custom-call | tf_op jit(solution)/shard_map/ffn/pallas_call | solution.py:638
  276.5 189.7 %scatter_sums.2.sums = f32[256,2176]{1,0:T(8,128)} custom-call(bf16[16,256,2176]{2,1,0:T(8,128)(2,1)} %bitcast.79), custom_call_target="tpu_custom_call" | custom-call | tf_op jit(solution)/shard_map/scatter_sums/pallas_call | solution.py:275
  466.3 51.0 %attention_backward.1 = (f32[256,2048]{1,0:T(8,128)}, bf16[256,2048]{1,0:T(8,128)(2,1)}, bf16[256,1536]{1,0:T(8,128)(2,1)}, bf16[256,2048]{1,0:T(8,128)(2,1)}, b...) custom-call(s32[1,4]{1,0:T(1,128)} %lengths.3, f32[1,128]{1,0:T(1,128)} %broadcast_in_dim_tile.5.freqs, ...), custom_call_target="tpu_custom_call" | custom-call | tf_op jit(solution)/shard_map/attention_backward/pallas_call | solution.py:1129
  517.3 1.5 convolution_convert_fusion.3
  518.9 1.6 copy.68
  520.4 1.3 slice.71
  522.0 1.3 copy.70
  523.3 7.4 %all-to-all-start = ((bf16[16,128,264]{1,2,0:T(8,128)(2,1)}), bf16[16,128,264]{1,2,0:T(8,128)(2,1)S(1)}, u32[]{:S(2)}, u32[]{:S(2)}) async-start(bf16[16,128,264]{1,2,0:T(8,128)(2,1)} %copy.70), calls=%async_computation.1 | async-start | bytes 2162688 | tf_op jit(solution)/shard_map/all_to_all | solution.py:1313
  531.1 11.3 %convolution_bitcast_fusion.1 = f32[1,2048,704]{1,2,0:T(8,128)} fusion(bf16[2048,2048]{1,0:T(8,128)(2,1)} %bitcast.108, bf16[2048,768]{1,0:T(8,128)(2,1)} %bitcast.112), kind=kOutput, calls=%fused_computation.3 | convolution fusion | flops 5905580032 | bytes 17301504 | tf_op jit(solution)/shard_map/dot_general | solution.py:66
  542.4 10.5 %convolution_bitcast_fusion.2 = f32[1,2048,704]{1,2,0:T(8,128)} fusion(bf16[2048,2048]{1,0:T(8,128)(2,1)} %bitcast.109, bf16[2048,768]{1,0:T(8,128)(2,1)S(1)} %bitcast.111), kind=kOutput, calls=%fused_computation.4 | convolution fusion | flops 5905580032 | bytes 17301504 | tf_op jit(solution)/shard_map/dot_general | solution.py:66
  552.9 8.3 %convolution_bitcast_fusion = f32[1,2048,704]{1,2,0:T(8,128)} fusion(bf16[2048,2048]{1,0:T(8,128)(2,1)S(1)} %bitcast.107, bf16[2048,768]{1,0:T(8,128)(2,1)S(1)} %bitcast.110), kind=kOutput, calls=%fused_computation.2 | convolution fusion | flops 5905580032 | bytes 17301504 | tf_op jit(solution)/shard_map/dot_general | solution.py:66
  561.7 4.5 convolution_convert_fusion.1
  566.2 4.5 convolution_convert_fusion
  570.7 2.1 convolution_convert_fusion.2
  572.7 86.5 %scatter_sums.3 = (f32[128,1536]{1,0:T(8,128)}, f32[128,1024]{1,0:T(8,128)}, f32[32,2048]{1,0:T(8,128)}, f32[128,288]{1,0:T(8,128)}, f32[24,128]{1,0:T(8,128)}) custom-call(bf16[16,128,1536]{2,1,0:T(8,128)(2,1)} %bitcast.77, bf16[16,128,1024]{2,1,0:T(8,128)(2,1)} %bitcast.78, bf16[16,32,2048]{2,1,0:T(8,128)(2,1)} %bitcast.82, ...), custom_call_target="tpu_custom_call" | custom-call | tf_op jit(solution)/shard_map/scatter_sums/pallas_call | solution.py:275
  659.3 1.7 copy.71
  663.6 1.3 slice_bitcast_fusion.2
  664.9 1.0 fusion.8
  665.9 2.4 copy.72
  668.3 1.1 copy.73
  669.4 1.1 copy.74
  670.5 2.6 add_convert_fusion
  673.2 1.3 copy.87
  674.8 0.9 copy.88
  (63 shorter events, 7.5 us)
Async XLA Ops:
  7.2 5.3 copy-start.13
  7.2 132.7 %all-gather.3.cloned.1.call-start = ((), (), s32[]{:S(2)}) async-start(), calls=%async_computation.4 | async-start | bytes 17825792 | tf_op jit(solution)/shard_map/all_gather | solution.py:1356
  7.9 5.5 copy-start.12
  7.9 562.7 %reduce-scatter.2.cloned.1.call-start = ((), (), s32[]{:S(2)}) async-start(), calls=%async_computation.2 | async-start | bytes 17825792 | tf_op jit(solution)/shard_map/reduce_scatter | solution.py:1376
  466.3 51.0 %copy-start.1 = (bf16[256,2048]{1,0:T(8,128)(2,1)S(1)}, bf16[256,2048]{1,0:T(8,128)(2,1)}, u32[]{:S(2)}) copy-start(bf16[256,2048]{1,0:T(8,128)(2,1)} %get-tuple-element.71) | copy-start | bytes 3145732
  523.3 141.5 %all-to-all-start = ((bf16[16,128,264]{1,2,0:T(8,128)(2,1)}), bf16[16,128,264]{1,2,0:T(8,128)(2,1)S(1)}, u32[]{:S(2)}, u32[]{:S(2)}) async-start(bf16[16,128,264]{1,2,0:T(8,128)(2,1)} %copy.70), calls=%async_computation.1 | async-start | bytes 2162688 | tf_op jit(solution)/shard_map/all_to_all | solution.py:1313
  530.8 139.7 %all-reduce.6.cloned.1.call-start = ((), (), s32[]{:S(2)}) async-start(), calls=%async_computation.3 | async-start | bytes 2097152 | tf_op jit(solution)/shard_map/psum | solution.py:1379
  531.0 11.3 %copy-start.15 = (bf16[8,256,768]{2,1,0:T(8,128)(2,1)S(1)}, bf16[8,256,768]{2,1,0:T(8,128)(2,1)}, u32[]{:S(2)}) copy-start(bf16[8,256,768]{2,1,0:T(8,128)(2,1)} %get-tuple-element.86) | copy-start | bytes 9437188
  531.0 21.8 %slice-start = ((s8[8388608]{0:T(1024)(128)(4,1)}), s8[4194304]{0:T(1024)(128)(4,1)S(1)}, s32[]{:S(2)}) async-start(s8[8388608]{0:T(1024)(128)(4,1)} %bitcast.105), calls=%async_computation.5 | async-start | bytes 8388608
  542.4 10.5 %slice-start.1 = ((s8[8388608]{0:T(1024)(128)(4,1)}), s8[4194304]{0:T(1024)(128)(4,1)S(1)}, s32[]{:S(2)}) async-start(s8[8388608]{0:T(1024)(128)(4,1)} %bitcast.105), calls=%async_computation.6 | async-start | bytes 8388608
  542.4 10.5 %copy-start.14 = (bf16[8,256,768]{2,1,0:T(8,128)(2,1)S(1)}, bf16[8,256,768]{2,1,0:T(8,128)(2,1)}, u32[]{:S(2)}) copy-start(bf16[8,256,768]{2,1,0:T(8,128)(2,1)} %get-tuple-element.89) | copy-start | bytes 9437188
  552.9 8.3 %copy-start.11 = (f32[24,2048]{1,0:T(8,128)S(1)}, f32[24,2048]{1,0:T(8,128)}, u32[]{:S(2)}) copy-start(f32[24,2048]{1,0:T(8,128)} %get-tuple-element.78) | copy-start | bytes 589828
  552.9 8.8 %copy-start.2 = (bf16[256,2048]{1,0:T(8,128)(2,1)S(1)}, bf16[256,2048]{1,0:T(8,128)(2,1)}, u32[]{:S(2)}) copy-start(bf16[256,2048]{1,0:T(8,128)(2,1)} %get-tuple-element.73) | copy-start | bytes 3145732
  561.6 4.5 copy-start.5
  561.7 4.5 copy-start.7
  566.2 4.5 copy-start.4
  566.2 4.5 copy-start.8
  665.9 4.6 copy-start
  670.5 2.6 copy-start.3
  673.1 1.7 copy-start.6
  673.1 2.5 copy-start.10
  673.1 3.2 copy-start.9
Sparse Core Ops, SparseCore 0:
  10.2 129.6 all-gather.2
  276.6 239.5 reduce-scatter.1
  570.8 40.4 all-reduce.5

commit v5 on v4

--- a/solution.py
+++ b/solution.py
@@ -131,6 +131,11 @@
             device_id_type=pl.DeviceIdType.MESH,
         )
     pl.semaphore_wait(barrier, 3 + inner + (1 if pair else 0))
+
+
+def near_first(z):
+    half = z // 2
+    return [z, (1 - z) * (1 - 2 * half), 2 * (1 - half) + half * (7 - 2 * z), 3 - 3 * half]
 
 
 def add_into(dst, *srcs):
@@ -308,7 +313,7 @@
     x_size,
     own_ffn,
     own_gates,
-    grad_all,
+    grad_half,
     gate_t,
     up_t,
     down_t,
@@ -322,6 +327,7 @@
     dge_all,
     due_all,
     shared_grads,
+    grad_all,
     blk,
     gts,
     gate_v,
@@ -359,6 +365,12 @@
     w_sem,
     g_sem,
     st_sem,
+    h_s,
+    h_r,
+    y_s,
+    y_r,
+    hc_s,
+    hc_r,
 ):
     z_size, bf16, f32 = 4, jnp.bfloat16, jnp.float32
     hidden = gate_t.shape[0]
@@ -369,8 +381,7 @@
     own = lax.axis_index("dp")
     at = functools.partial(index_of, x_size=x_size)
     ins, outs = (own_ffn, own_gates), (blk, gts)
-    half = z // 2
-    order = [z, (1 - z) * (1 - 2 * half), 2 * (1 - half) + half * (7 - 2 * z), 3 - 3 * half]
+    order = near_first(z)
 
     def place(j):
         return sum(is_at(j, i) * order[i] for i in range(4))
@@ -395,7 +406,7 @@
     for copy in keep + weights:
         copy.start()
     grad_copy(0).start()
-    greet(z, x, core, z_size, x_size)
+    greet(z, x, core, z_size, x_size, True)
 
     def up(a, d):
         block = outs[a].at[at(z - d, x, core)]
@@ -416,6 +427,43 @@
         block = outs[a].at[at(w, v, core)]
         src = ins[a] if first else block
         return remote(src, block, c_s.at[a, w, v], c_r.at[a, w, v], at(z, x, 1 - core))
+
+    rank = lax.axis_index("tensor")
+    edge = 1 - ((z + 3) // 4) * ((6 - z) // 4)
+    part_rows = rows_here // 2
+
+    def part(j, v, which):
+        store = blk if j in (1, 4) else grad_all
+        rows = pl.ds(pl.multiple_of(which * part_rows, part_rows), part_rows)
+        return store.at[at(order[2 if j < 2 else 3], v, core), rows]
+
+    def link(j, target=0):
+        block = part(j, x, rank)
+        target = at(target, x, core) if j == 2 else at(z, 1 - x, core)
+        return remote(block, block, h_s.at[j], h_r.at[j], target)
+
+    landed = lambda j: x if j == 2 else 1 - x
+
+    def swap(j):
+        block = part(j, landed(j), rank)
+        return pair_copy(block, block, y_s.at[j], y_r.at[j])
+
+    def half_beside(j, i):
+        block = part(j, landed(j), rank + i * (1 - 2 * rank))
+        return remote(block, block, hc_s.at[j, i], hc_r.at[j, i], at(z, x, 1 - core))
+
+    def link_done(j):
+        link(j).wait_recv()
+        swap(j).start()
+        half_beside(j, 0).start()
+
+    def swap_done(j):
+        swap(j).wait_recv()
+        half_beside(j, 1).start()
+
+    def ready(j):
+        half_beside(j, 0).wait_recv()
+        half_beside(j, 1).wait_recv()
 
     for a in (1, 0):
         beside(a, z, x, True).start()
@@ -430,20 +478,98 @@
             def _():
                 up(a, d - 1).wait_recv()
                 pl.when(z < z_size - 1)(lambda: up(a, d).start())
-                across(a, z - d).start()
                 beside(a, z - d, x).start()
 
             @pl.when(z + d < z_size)
             def _():
                 down(a, d - 1).wait_recv()
                 pl.when(z > 0)(lambda: down(a, d).start())
-                across(a, z + d).start()
                 beside(a, z + d, x).start()
 
-    def from_across(w):
-        for a in (1, 0):
+    def from_across(w, arrays=(1, 0)):
+        for a in arrays:
             across(a, w).wait_recv()
             beside(a, w, 1 - x).start()
+
+    def at_ends(do):
+        pl.when(edge == 1)(do)
+
+    def inside(do):
+        pl.when(edge == 0)(do)
+
+    def far_over_x():
+        link(4).start()
+        across(1, order[3]).start()
+
+    def early(k):
+        @pl.when(k == 1)
+        def _():
+            pass_on(1)
+            for a in (1, 0):
+                across(a, order[1]).start()
+            link(0).start()
+            from_across(order[0])
+
+        @pl.when((k == 2) & (edge == 0))
+        def _():
+            link(2, 3 * (z - 1)).start()
+
+        @pl.when(k == 3)
+        def _():
+            pass_on(2)
+            link(1).start()
+            across(1, order[2]).start()
+
+            @inside
+            def _():
+                link(3).start()
+                far_over_x()
+
+            from_across(order[1])
+
+        @pl.when((k == 4) & (edge == 1))
+        def _():
+            link_done(2)
+            link(3).start()
+
+        @pl.when(k == 5)
+        def _():
+            ready(0)
+            grad_copy(5).start()
+            pass_on(3)
+            at_ends(far_over_x)
+            swap_done(1)
+            at_ends(lambda: swap_done(2))
+            from_across(order[2], (1,))
+            ready(1)
+
+        @pl.when(k == 6)
+        def _():
+            link_done(4)
+            from_across(order[3], (1,))
+
+        @pl.when(k == 7)
+        def _():
+            ready(3)
+            grad_copy(7).start()
+            swap_done(4)
+            ready(4)
+
+    def midway(k):
+        pl.when(k == 3)(lambda: link_done(0))
+
+        @pl.when(k == 4)
+        def _():
+            link_done(1)
+            swap_done(0)
+
+        @pl.when(k == 5)
+        def _():
+            at_ends(lambda: ready(2))
+            grad_copy(6).start()
+            link_done(3)
+
+        pl.when(k == 6)(lambda: swap_done(3))
 
     gate_v[pl.ds(hidden, gate_v.shape[0] - hidden), :] = jnp.zeros(
         (gate_v.shape[0] - hidden, features), bf16
@@ -497,18 +623,11 @@
         pair = w * x_size + v
         block = 2 * pair
         here = k % 2
-        for r in range(1, 5):
-
-            @pl.when(k == 2 * r - 1)
-            def _():
-                if r < 4:
-                    pass_on(r)
-                from_across(order[r - 1])
-
+        early(k)
         grad_copy(k).wait()
-        pl.when(k < 7)(lambda: grad_copy(k + 1).start())
-        for a in (1, 0):
-            beside(a, w, v).wait_recv()
+        pl.when(k < 4)(lambda: grad_copy(k + 1).start())
+        pl.when((k != 5) & (k != 7))(lambda: beside(0, w, v).wait_recv())
+        beside(1, w, v).wait_recv()
 
         for a in range(2):
             gates = gts[block + a]
@@ -581,6 +700,7 @@
         wait_staged(k, (2, 3, 4))
         lax.fori_loop(0, gate_v.shape[0] // 256, hidden_units, 0)
         start_staged(pair, (2, 3, 4))
+        midway(k)
         dgate_acc[...] = jnp.zeros(dgate_acc.shape, f32)
 
         def back(n, _):
@@ -618,14 +738,28 @@
     wait_staged(1, range(7))
     shared_grads[...] = acc[...].astype(bf16)
     for a in range(2):
-        for w in range(z_size):
-            for v in range(x_size):
-                beside(a, w, v).wait_send()
-            across(a, w).wait_send()
+        for i in range(z_size):
+            beside(a, order[i], x).wait_send()
+            if a == 1 or i < 2:
+                beside(a, order[i], 1 - x).wait_send()
+                across(a, order[i]).wait_send()
     for d in range(z_size):
         for a in range(2):
             pl.when((z >= d) & (z < z_size - 1))(lambda: up(a, d).wait_send())
             pl.when((z + d < z_size) & (z > 0))(lambda: down(a, d).wait_send())
+    inside(lambda: link(2, 3 * (z - 1)).wait_send())
+    for j in range(5):
+
+        def sent_on(j=j):
+            swap(j).wait_send()
+            half_beside(j, 0).wait_send()
+            half_beside(j, 1).wait_send()
+
+        if j == 2:
+            at_ends(sent_on)
+        else:
+            link(j).wait_send()
+            sent_on()
 
 
 def ffn_tuned(own_ffn, own_gates, grad_all, gate_t, up_t, down_t, shared_in, shared_out, slots):
@@ -646,9 +780,11 @@
             shape((8, 2 * slots, padded), bf16),
             shape((8, 2 * slots, padded), bf16),
             shape((384, features), bf16),
+            shape((16, rows, features), bf16),
         ],
         in_specs=[anywhere] * 8,
-        out_specs=[anywhere] * 7 + [pl.BlockSpec(memory_space=pltpu.VMEM)],
+        out_specs=[anywhere] * 7 + [pl.BlockSpec(memory_space=pltpu.VMEM), anywhere],
+        input_output_aliases={2: 8},
         scratch_shapes=[
             pltpu.VMEM((16, rows, features), bf16),
             pltpu.VMEM((16, rows, 128), f32),
@@ -679,7 +815,9 @@
         ]
         + [dma((2, 4))] * 6
         + [dma((2, 4, 2))] * 2
-        + [dma((5,)), dma((2,)), dma((7,))],
+        + [dma((5,)), dma((2,)), dma((7,))]
+        + [dma((5,))] * 4
+        + [dma((5, 2))] * 2,
         compiler_params=pltpu.CompilerParams(
             collective_id=1, has_side_effects=True, vmem_limit_bytes=VMEM_LIMIT
         ),
@@ -761,6 +899,7 @@
     down_t,
     kv_up,
     w_out,
+    grad_out,
     hidden,
     ffn_bf,
     gates,
@@ -773,6 +912,7 @@
     latent,
     context,
     log_totals,
+    everyone,
     wq_v,
     down_v,
     up_v,
@@ -782,8 +922,20 @@
     w_sem,
     s_sem,
     r_sem,
+    own_sem,
+    up_s,
+    up_r,
+    dn_s,
+    dn_r,
+    x_s,
+    x_r,
+    c_s,
+    c_r,
 ):
     bf16, f32 = jnp.bfloat16, jnp.float32
+    z_size, x_size = 4, 2
+    z, x, core = place_of(x_size)
+    at = functools.partial(index_of, x_size=x_size)
     rows, features = tokens.shape
     rank = kv_up.shape[0]
     heads = kv_up.shape[1] // 256
@@ -796,9 +948,33 @@
         pltpu.make_async_copy(w_query, wq_v, w_sem.at[3]),
         pltpu.make_async_copy(w_out, out_v, w_sem.at[4]),
     ]
+    keep = pltpu.make_async_copy(grad_out, everyone.at[at(z, x, core)], own_sem.at[0])
+
+    def move(w, v, first, sems, target):
+        block = everyone.at[at(w, v, core)]
+        return remote(grad_out if first else block, block, *sems, target)
+
+    up = lambda d: move(z - d, x, d == 0, (up_s.at[d], up_r.at[d]), at(z + 1, x, core))
+    down = lambda d: move(z + d, x, d == 0, (dn_s.at[d], dn_r.at[d]), at(z - 1, x, core))
+    across = lambda i, w: move(w, x, i == 0, (x_s.at[i], x_r.at[i]), at(z, 1 - x, core))
+    beside = lambda w, v, first=False: move(
+        w, v, first, (c_s.at[w, v], c_r.at[w, v]), at(z, x, 1 - core)
+    )
+    near = near_first(z)[1]
+
+    def from_across(i, w):
+        block = everyone.at[at(w, 1 - x, core)]
+        remote(block, block, x_s.at[i], x_r.at[i], at(z, 1 - x, core)).wait_recv()
+        beside(w, 1 - x).start()
+
+    keep.start()
     for copy in loads:
         copy.start()
-    greet_pair()
+    greet(z, x, core, z_size, x_size, True)
+    beside(z, x, True).start()
+    across(0, z).start()
+    pl.when(z < z_size - 1)(lambda: up(0).start())
+    pl.when(z > 0)(lambda: down(0).start())
     cosine, sine, met = turn_tables(lengths, freqs, rows)
     values, _, _ = rms_normalize_pieces(tokens[...].astype(f32), g_attn[...])
     normed[...] = values.astype(bf16)
@@ -849,6 +1025,7 @@
         return 0
 
     lax.fori_loop(0, heads // 2, two_heads, 0)
+
     loads[4].wait()
     chunks, width = sent.shape[0], sent.shape[2]
     chunk = lambda i: pair_copy(sent.at[i], got.at[i], s_sem.at[i], r_sem.at[i])
@@ -861,6 +1038,22 @@
         return 0
 
     lax.fori_loop(0, chunks, project, 0)
+
+    @pl.when(z > 0)
+    def _():
+        up(0).wait_recv()
+        across(1, z - 1).start()
+        pl.when(z < z_size - 1)(lambda: up(1).start())
+        beside(z - 1, x).start()
+
+    @pl.when(z < z_size - 1)
+    def _():
+        down(0).wait_recv()
+        pl.when(z == 0)(lambda: across(1, z + 1).start())
+        pl.when(z > 0)(lambda: down(1).start())
+        beside(z + 1, x).start()
+
+    from_across(0, z)
 
     def join(i, _):
         chunk(i).wait()
@@ -888,9 +1081,47 @@
         named = named | (lane == routes[:, pl.ds(i, 1)])
     gates[...] = jnp.where(named, share, -1.0)
 
+    @pl.when(z >= 2)
+    def _():
+        up(1).wait_recv()
+        beside(z - 2, x).start()
+
+    @pl.when(z < z_size - 2)
+    def _():
+        down(1).wait_recv()
+        beside(z + 2, x).start()
+
+    from_across(1, near)
+    beside(z, x).wait()
+    beside(z, 1 - x).wait()
+    beside(near, 1 - x).wait()
+    pl.when(z > 0)(lambda: beside(z - 1, x).wait())
+    pl.when(z < z_size - 1)(lambda: beside(z + 1, x).wait())
+    pl.when(z >= 2)(lambda: beside(z - 2, x).wait())
+    pl.when(z < z_size - 2)(lambda: beside(z + 2, x).wait())
+    across(0, z).wait_send()
+    across(1, near).wait_send()
+    pl.when(z < z_size - 1)(lambda: up(0).wait_send())
+    pl.when(z > 0)(lambda: down(0).wait_send())
+    pl.when((z > 0) & (z < z_size - 1))(lambda: up(1).wait_send())
+    pl.when((z > 0) & (z < z_size - 1))(lambda: down(1).wait_send())
+    keep.wait()
+
 
 def forward_tuned(
-    lengths, freqs, tokens, routes, g_attn, g_latent, g_ffn, router_t, w_query, down_t, kv_up, w_out
+    lengths,
+    freqs,
+    tokens,
+    routes,
+    g_attn,
+    g_latent,
+    g_ffn,
+    router_t,
+    w_query,
+    down_t,
+    kv_up,
+    w_out,
+    grad_out,
 ):
     rows, features = tokens.shape
     rank, columns = kv_up.shape
@@ -915,9 +1146,10 @@
             shape((rows, rank), f32),
             shape((rows, heads * 128), bf16),
             shape((rows, 128), f32),
+            shape((16,) + grad_out.shape, bf16),
         ],
-        in_specs=[smem] + [vmem] * 7 + [anywhere] * 4,
-        out_specs=[vmem] * 12,
+        in_specs=[smem] + [vmem] * 7 + [anywhere] * 5,
+        out_specs=[vmem] * 12 + [anywhere],
         scratch_shapes=[
             pltpu.VMEM(w_query.shape, bf16),
             pltpu.VMEM((rank + 128, features), bf16),
@@ -928,12 +1160,29 @@
             dma((5,)),
             dma((chunks,)),
             dma((chunks,)),
-        ],
+            dma((1,)),
+        ]
+        + [dma((2,))] * 6
+        + [dma((4, 2))] * 2,
         compiler_params=pltpu.CompilerParams(
             collective_id=2, has_side_effects=True, vmem_limit_bytes=VMEM_LIMIT
         ),
         name="attention_forward",
-    )(lengths, freqs, tokens, routes, g_attn, g_latent, g_ffn, router_t, w_query, down_t, kv_up, w_out)
+    )(
+        lengths,
+        freqs,
+        tokens,
+        routes,
+        g_attn,
+        g_latent,
+        g_ffn,
+        router_t,
+        w_query,
+        down_t,
+        kv_up,
+        w_out,
+        grad_out,
+    )
 
 
 def backward_kernel(
@@ -1163,6 +1412,218 @@
     )(lengths, freqs, sums, hidden, grad_out, tokens, probs, *gains, router_t, *saved, *weights)
 
 
+def add_window(dst, start, width, *srcs):
+    rows = dst.shape[0]
+    step = 32 if rows % 32 == 0 else 8
+    cols = pl.ds(pl.multiple_of(start, 128), width)
+
+    def body(i, _):
+        here = pl.ds(pl.multiple_of(i * step, step), step)
+        total = dst[here, cols].astype(jnp.float32)
+        for src in srcs:
+            total = total + src[here, :].astype(jnp.float32)
+        dst[here, cols] = total.astype(dst.dtype)
+        return 0
+
+    lax.fori_loop(0, rows // step, body, 0)
+
+
+def home_kernel(x_size, parts, share, whole, total, *refs):
+    z_size, f32 = 4, jnp.float32
+    rows = whole.shape[1] // parts
+    piece = lambda p: pl.ds(p * rows, rows)
+    own, c_buf, x_buf, z_buf, y_buf, f_buf = (refs[i * parts : (i + 1) * parts] for i in range(6))
+    refs = refs[6 * parts :]
+    l_sem, c_s, c_r, x_s, x_r, z_s, z_r, y_s, y_r, f_s, f_r = refs
+    z, x, core = place_of(x_size)
+    rank = lax.axis_index("tensor")
+    at = functools.partial(index_of, x_size=x_size)
+    half = z // 2
+    inner = ((z + 3) // 4) * ((6 - z) // 4)
+    order = [3 - 3 * half, 2 - half, 1 - z + 4 * half, z]
+    width = [c.shape[3] for c in c_buf]
+    window = [w - share for w in width]
+    begin = pl.multiple_of(rank * share, 128)
+    mine = lambda p: pl.multiple_of(rank * window[p], 128)
+    theirs = lambda p: pl.multiple_of((1 - rank) * window[p], 128)
+
+    slots = own[0].shape[0]
+    blocks = [(w, v) for v in (1 - x, x) for w in order]
+    load = lambda p, i: pltpu.make_async_copy(
+        whole.at[at(blocks[i][0], blocks[i][1], core), piece(p)],
+        own[p].at[i % slots],
+        l_sem.at[p, i % slots],
+    )
+    beside = lambda p, w, v: remote(
+        whole.at[at(w, v, 1 - core), piece(p)],
+        c_buf[p].at[w, v],
+        c_s.at[p, w, v],
+        c_r.at[p, w, v],
+        at(z, x, 1 - core),
+    )
+    twin = lambda p, w, v: pair_copy(
+        c_buf[p].at[w, v, :, pl.ds(theirs(p), share)],
+        y_buf[p].at[w, v],
+        y_s.at[p, w, v],
+        y_r.at[p, w, v],
+    )
+    across = lambda p, w: remote(
+        c_buf[p].at[w, 1 - x, :, pl.ds(begin, window[p])],
+        x_buf[p].at[w],
+        x_s.at[p, w],
+        x_r.at[p, w],
+        at(z, 1 - x, core),
+    )
+
+    def along(p, w, slot, target):
+        return remote(
+            c_buf[p].at[w, x, :, pl.ds(begin, window[p])],
+            z_buf[p].at[slot],
+            z_s.at[p, w],
+            z_r.at[p, slot],
+            at(target, x, core),
+        )
+
+    final = lambda p: pair_copy(
+        c_buf[p].at[z, x, :, pl.ds(begin, window[p])], f_buf[p], f_s.at[p], f_r.at[p]
+    )
+
+    for p in range(parts):
+        for i in range(slots):
+            load(p, i).start()
+    greet(z, x, core, z_size, x_size, True)
+    for p in range(parts):
+        for w, v in blocks:
+            beside(p, w, v).start()
+    def on_chip(p, i):
+        w, v = blocks[i]
+        load(p, i).wait()
+        beside(p, w, v).wait_recv()
+        add_into(c_buf[p].at[w, v], own[p].at[i % slots])
+        if i + slots < len(blocks):
+            load(p, i + slots).start()
+        twin(p, w, v).start()
+
+    def go_across(p, i):
+        w, v = blocks[i]
+        twin(p, w, v).wait()
+        add_window(c_buf[p].at[w, v], mine(p), share, y_buf[p].at[w, v])
+        across(p, w).start()
+
+    def go_along(p, k):
+        w = order[k]
+        twin(p, w, x).wait()
+        add_window(c_buf[p].at[w, x], mine(p), share, y_buf[p].at[w, x])
+        across(p, w).wait_recv()
+        if k < 3:
+
+            @pl.when(inner == 1)
+            def _():
+                along(p, w, w, z).wait_recv()
+                add_window(c_buf[p].at[w, x], begin, window[p], x_buf[p].at[w], z_buf[p].at[w])
+
+            @pl.when(inner == 0)
+            def _():
+                add_window(c_buf[p].at[w, x], begin, window[p], x_buf[p].at[w])
+
+            @pl.when(w > z)
+            def _():
+                along(p, w, w, z + 1).start()
+
+            @pl.when(w < z - 1)
+            def _():
+                along(p, w, w, z - 1).start()
+
+            @pl.when(w == z - 1)
+            def _():
+                along(p, w, z_size, z - 1).start()
+
+        else:
+            add_window(c_buf[p].at[w, x], begin, window[p], x_buf[p].at[w])
+
+            @pl.when(z > 0)
+            def _():
+                along(p, w, z, z).wait_recv()
+                add_window(c_buf[p].at[w, x], begin, window[p], z_buf[p].at[z])
+
+            @pl.when(z < z_size - 1)
+            def _():
+                along(p, w, z_size, z).wait_recv()
+                add_window(c_buf[p].at[w, x], begin, window[p], z_buf[p].at[z_size])
+
+            final(p).start()
+
+    def begin_part(p, between):
+        for i in range(5):
+            on_chip(p, i)
+            if i >= 1:
+                go_across(p, i - 1)
+            between(i)
+        for i in range(5, 8):
+            on_chip(p, i)
+
+    begin_part(0, lambda i: None)
+    for p in range(parts):
+        if p + 1 < parts:
+
+            def between(i):
+                if i < 4:
+                    go_along(p, i)
+
+            begin_part(p + 1, between)
+        else:
+            for k in range(4):
+                go_along(p, k)
+    for p in range(parts):
+        final(p).wait()
+        common = window[p] - share
+        near, far = c_buf[p].at[z, x], f_buf[p]
+        total[piece(p), pl.ds(mine(p), share)] = near[:, pl.ds(mine(p), share)].astype(f32)
+        total[piece(p), pl.ds(theirs(p), share)] = far[
+            :, pl.ds(pl.multiple_of((1 - rank) * common, 128), share)
+        ].astype(f32)
+        total[piece(p), pl.ds(share, common)] = near[:, pl.ds(share, common)].astype(f32) + far[
+            :, pl.ds(pl.multiple_of(rank * share, 128), common)
+        ].astype(f32)
+    for p in range(parts):
+        for w in range(z_size):
+            for v in range(x_size):
+                beside(p, w, v).wait_send()
+            across(p, w).wait_send()
+
+            @pl.when(z != w)
+            def _():
+                along(p, w, w, z).wait_send()
+
+
+def home_sums(array, collective_id, parts, share=512):
+    bf16, f32, dma = jnp.bfloat16, jnp.float32, pltpu.SemaphoreType.DMA
+    rows, width = array.shape[1:]
+    block = lambda *lead, cut=0: [pltpu.VMEM(lead + (rows // parts, width - cut), bf16)] * parts
+    return pl.pallas_call(
+        functools.partial(home_kernel, 2, parts, share),
+        out_shape=jax.ShapeDtypeStruct((rows, width), f32),
+        in_specs=[pl.BlockSpec(memory_space=pl.ANY)],
+        out_specs=pl.BlockSpec(memory_space=pltpu.VMEM),
+        scratch_shapes=block(3)
+        + block(4, 2)
+        + block(4, cut=share)
+        + block(5, cut=share)
+        + block(4, 2, cut=width - share)
+        + block(cut=share)
+        + [dma((parts, 3))]
+        + [dma((parts, 4, 2))] * 2
+        + [dma((parts, 4))] * 3
+        + [dma((parts, 5))]
+        + [dma((parts, 4, 2))] * 2
+        + [dma((parts,))] * 2,
+        compiler_params=pltpu.CompilerParams(
+            collective_id=collective_id, has_side_effects=True, vmem_limit_bytes=VMEM_LIMIT
+        ),
+        name="home_sums",
+    )(array)
+
+
 def sum_home(arrays, pair=False):
     sums = [lax.psum_scatter(a, "dp", scatter_dimension=0) for a in arrays]
     if pair:
@@ -1179,7 +1640,7 @@
     part = shared[0].shape[1]
     hidden, features = weights[0].shape[1], own_ffn.shape[1]
     gate_t, up_t, down_t = (jnp.pad(w.T, ((0, 128 - part), (0, 0))) for w in shared)
-    out_part, grad_part, rows, dy, he, dge, due, shared_grads = ffn_tuned(
+    out_part, grad_part, rows, dy, he, dge, due, shared_grads, _ = ffn_tuned(
         own_ffn,
         gates,
         everyone_grad,
@@ -1353,11 +1814,10 @@
     router_t = jnp.pad(router.T, ((0, 128 - experts), (0, 0)))
     gains = [g_attn[None, :], latent_norm_gain[None, :], g_ffn[None, :]]
     weights = [w_query, key_value_down_weight.T, key_value_up_weight, w_out]
-    everyone_grad = lax.all_gather(grad_out, "dp")
     hidden, ffn_bf, dense_gates, probs, normed, *saved = forward_tuned(
-        lengths, freqs, tokens, routes, *gains, router_t, *weights
-    )
-    queries, kv, key_turned, latent_bf, latent, context, log_totals = saved
+        lengths, freqs, tokens, routes, *gains, router_t, *weights, grad_out
+    )
+    queries, kv, key_turned, latent_bf, latent, context, log_totals, everyone_grad = saved
     part = shared_gate.shape[1] // devices
     shared_parts = [
         lax.dynamic_slice_in_dim(w, own * part, part, 1)
@@ -1378,7 +1838,7 @@
     )
     ffn_total = lax.psum(ffn_total, "tensor").astype(jnp.float32)
     output = (hidden + ffn_total).astype(jnp.bfloat16)
-    (sums,) = scatter_sums([grad_ffn_part], 2, 3, jnp.float32, True)
+    sums = home_sums(grad_ffn_part, 3, 2)
     grad_tokens, grad_hidden_bf, grad_query, grad_kv, grad_low, vectors = backward_tuned(
         lengths,
         freqs,

time: 691 us -> 608 us (0.88)
  waiting for transfers between devices: 82 us -> 0.04 us
    pallas_call x2 -> x1, Pallas kernels: 276 us -> 88.9 us  [scatter_sums(): pl.pallas_call(functools.partial(scatter_kernel, x_size, parts, pair), ou...]
    pallas_call x0 -> x1, Pallas kernels: none -> 155 us  [home_sums(): pl.pallas_call(functools.partial(home_kernel, 2, parts, share), out_shape...]
    all_gather x1 -> x0, waiting for transfers between devices: 81.3 us -> none  [shards_tuned(): everyone_grad = lax.all_gather(grad_out, 'dp')]
    pallas_call x1, Pallas kernels: 137 us -> 156 us  [ffn_tuned(): pl.pallas_call(functools.partial(ffn_kernel, 2), out_shape=[shape((8, 2,...]
    pallas_call x1, Pallas kernels: 42.1 us -> 61.5 us  [forward_tuned(): pl.pallas_call(forward_kernel, out_shape=[shape((rows, features), f32), s...]
  transfers between devices with their start and end apart: 4 -> 3, of which waited for: 1 -> 0; matrix products, arithmetic and copies ran while one was open for 10% -> 10% of each run, Pallas kernels for 54% -> 48%
where the time goes in v5:
time: 608 us; the launch traced here: 601 us
  Pallas kernels  508 us (84%)
  matrix products  42.9 us (7%)
  local copies, waits for them, and re-layouts  27.4 us (5%)
  between operations  14.5 us (2%)
    pallas_call x1, Pallas kernels, ffn_tuned(): pl.pallas_call(functools.partial(ffn_kernel, 2), out_shape=[shape((8, 2,...  156 us
    pallas_call x1, Pallas kernels, home_sums(): pl.pallas_call(functools.partial(home_kernel, 2, parts, share), out_shape...  155 us
    pallas_call x1, Pallas kernels, scatter_sums(): pl.pallas_call(functools.partial(scatter_kernel, x_size, parts, pair), ou...  88.9 us
    pallas_call x1, Pallas kernels, forward_tuned(): pl.pallas_call(forward_kernel, out_shape=[shape((rows, features), f32), s...  61.5 us
    pallas_call x1, Pallas kernels, backward_tuned(): pl.pallas_call(backward_kernel, out_shape=[shape((rows, features), f32),...  46.5 us
    dot_general x7, matrix products, contract_first(): lax.dot_general(left, right, (((0,), (0,)), ((), ())), precision=precisio...  42.9 us
    unnamed x51, local copies, waits for them, and re-layouts  13.4 us
  transfers between devices with their start and end apart: 3, of which 0 were waited for; matrix products, arithmetic and copies ran while one was open for 10% of the time, Pallas kernels for 48%

profile of v5, /device:TPU:0, one launch (start us, length us, event | category | flops | bytes accessed | tf_op | source)
XLA Modules:
  0.0 600.9 jit_solution(16771730370041562703)
XLA Ops:
  7.3 2.0 constant_dynamic-slice_fusion
  9.4 1.5 constant_dynamic-slice_fusion.2
  11.7 0.8 copy.65.routes
  12.7 1.1 fusion.5.shared_in
  13.8 1.1 pad.16.router_t
  14.9 0.8 pad.19.shared_out
  15.7 61.5 %attention_forward.1 = (f32[256,2048]{1,0:T(8,128)}, bf16[256,2048]{1,0:T(8,128)(2,1)}, f32[256,128]{1,0:T(8,128)}, f32[256,128]{1,0:T(8,128)}, bf16[256,2048]{1...) custom-call(s32[1,4]{1,0:T(1,128)} %lengths.3, ...), custom_call_target="tpu_custom_call" | custom-call | tf_op jit(solution)/shard_map/attention_forward/pallas_call | solution.py:1134
  77.2 156.4 %ffn.1 = (bf16[8,2,256,2048]{3,2,1,0:T(8,128)(2,1)}, bf16[8,2,256,2176]{3,2,1,0:T(8,128)(2,1)}, bf16[8,256,2048]{2,1,0:T(8,128)(2,1)}, bf16[8,256,2048]{2,1,0:T(...) custom-call(bf16[256,2048]{1,0:T(8,128)(2,1)} %get-tuple-element.61., ...), custom_call_target="tpu_custom_call", output_to_operand_aliasing={{8}: (2, {})} | custom-call | tf_op jit(solution)/shard_map/ffn/pallas_call | solution.py:772
  233.7 1.4 copy-done.8
  235.4 1.3 copy.71
  236.7 3.8 all-to-all-start
  240.5 155.1 %home_sums.1.sums = f32[256,2176]{1,0:T(8,128)} custom-call(bf16[16,256,2176]{2,1,0:T(8,128)(2,1)} %bitcast.78), custom_call_target="tpu_custom_call" | custom-call | tf_op jit(solution)/shard_map/home_sums/pallas_call | solution.py:1603
  395.6 46.5 %attention_backward.1 = (f32[256,2048]{1,0:T(8,128)}, bf16[256,2048]{1,0:T(8,128)(2,1)}, bf16[256,1536]{1,0:T(8,128)(2,1)}, bf16[256,2048]{1,0:T(8,128)(2,1)}, b...) custom-call(s32[1,4]{1,0:T(1,128)} %lengths.3, f32[1,128]{1,0:T(1,128)} %broadcast_in_dim_tile.5.freqs, ...), custom_call_target="tpu_custom_call" | custom-call | tf_op jit(solution)/shard_map/attention_backward/pallas_call | solution.py:1378
  442.1 1.5 convolution_convert_fusion.3
  443.7 1.6 copy.69
  445.2 11.4 %convolution_bitcast_fusion.1 = f32[1,2048,704]{1,2,0:T(8,128)} fusion(bf16[2048,2048]{1,0:T(8,128)(2,1)} %bitcast.106, bf16[2048,768]{1,0:T(8,128)(2,1)} %bitcast.110), kind=kOutput, calls=%fused_computation.3 | convolution fusion | flops 5905580032 | bytes 17301504 | tf_op jit(solution)/shard_map/dot_general | solution.py:66
  456.6 10.6 %convolution_bitcast_fusion.2 = f32[1,2048,704]{1,2,0:T(8,128)} fusion(bf16[2048,2048]{1,0:T(8,128)(2,1)} %bitcast.107, bf16[2048,768]{1,0:T(8,128)(2,1)S(1)} %bitcast.109), kind=kOutput, calls=%fused_computation.4 | convolution fusion | flops 5905580032 | bytes 17301504 | tf_op jit(solution)/shard_map/dot_general | solution.py:66
  467.2 8.4 %convolution_bitcast_fusion = f32[1,2048,704]{1,2,0:T(8,128)} fusion(bf16[2048,2048]{1,0:T(8,128)(2,1)S(1)} %bitcast.105, bf16[2048,768]{1,0:T(8,128)(2,1)S(1)} %bitcast.108), kind=kOutput, calls=%fused_computation.2 | convolution fusion | flops 5905580032 | bytes 17301504 | tf_op jit(solution)/shard_map/dot_general | solution.py:66
  475.9 4.5 convolution_convert_fusion.1
  480.4 4.5 convolution_convert_fusion
  484.9 2.1 convolution_convert_fusion.2
  487.0 88.9 %scatter_sums.1 = (f32[128,1536]{1,0:T(8,128)}, f32[128,1024]{1,0:T(8,128)}, f32[32,2048]{1,0:T(8,128)}, f32[128,288]{1,0:T(8,128)}, f32[24,128]{1,0:T(8,128)}) custom-call(bf16[16,128,1536]{2,1,0:T(8,128)(2,1)} %bitcast.76, bf16[16,128,1024]{2,1,0:T(8,128)(2,1)} %bitcast.77, bf16[16,32,2048]{2,1,0:T(8,128)(2,1)} %bitcast.80, ...), custom_call_target="tpu_custom_call" | custom-call | tf_op jit(solution)/shard_map/scatter_sums/pallas_call | solution.py:280
  575.9 1.7 copy.72
  580.3 1.3 slice_bitcast_fusion.2
  581.5 1.0 fusion.8
  582.5 2.4 copy.73
  584.9 1.1 copy.74
  586.0 1.1 copy.75
  587.2 2.6 add_convert_fusion
  589.8 1.3 copy.89
  591.5 0.9 copy.90
  593.1 0.8 copy.92
  (62 shorter events, 5.6 us)
Async XLA Ops:
  7.2 4.5 copy-start.14
  7.2 477.7 %reduce-scatter.2.cloned.1.call-start = ((), (), s32[]{:S(2)}) async-start(), calls=%async_computation.2 | async-start | bytes 17825792 | tf_op jit(solution)/shard_map/reduce_scatter | solution.py:1836
  9.2 4.6 copy-start.13
  233.7 1.4 copy-start.8
  236.7 344.9 %all-to-all-start = ((bf16[16,128,264]{1,2,0:T(8,128)(2,1)}), bf16[16,128,264]{1,2,0:T(8,128)(2,1)S(1)}, u32[]{:S(2)}, u32[]{:S(2)}) async-start(bf16[16,128,264]{1,2,0:T(8,128)(2,1)} %copy.71), calls=%async_computation.1 | async-start | bytes 2162688 | tf_op jit(solution)/shard_map/all_to_all | solution.py:1774
  240.5 346.7 %all-reduce.6.cloned.1.call-start = ((), (), s32[]{:S(2)}) async-start(), calls=%async_computation.3 | async-start | bytes 2097152 | tf_op jit(solution)/shard_map/psum | solution.py:1839
  395.6 46.5 %copy-start.1 = (bf16[256,2048]{1,0:T(8,128)(2,1)S(1)}, bf16[256,2048]{1,0:T(8,128)(2,1)}, u32[]{:S(2)}) copy-start(bf16[256,2048]{1,0:T(8,128)(2,1)} %get-tuple-element.73) | copy-start | bytes 3145732
  445.2 11.4 %copy-start.16 = (bf16[8,256,768]{2,1,0:T(8,128)(2,1)S(1)}, bf16[8,256,768]{2,1,0:T(8,128)(2,1)}, u32[]{:S(2)}) copy-start(bf16[8,256,768]{2,1,0:T(8,128)(2,1)} %get-tuple-element.88) | copy-start | bytes 9437188
  445.2 22.0 %slice-start = ((s8[8388608]{0:T(1024)(128)(4,1)}), s8[4194304]{0:T(1024)(128)(4,1)S(1)}, s32[]{:S(2)}) async-start(s8[8388608]{0:T(1024)(128)(4,1)} %bitcast.103), calls=%async_computation.4 | async-start | bytes 8388608
  456.6 10.6 %slice-start.1 = ((s8[8388608]{0:T(1024)(128)(4,1)}), s8[4194304]{0:T(1024)(128)(4,1)S(1)}, s32[]{:S(2)}) async-start(s8[8388608]{0:T(1024)(128)(4,1)} %bitcast.103), calls=%async_computation.5 | async-start | bytes 8388608
  456.6 10.6 %copy-start.15 = (bf16[8,256,768]{2,1,0:T(8,128)(2,1)S(1)}, bf16[8,256,768]{2,1,0:T(8,128)(2,1)}, u32[]{:S(2)}) copy-start(bf16[8,256,768]{2,1,0:T(8,128)(2,1)} %get-tuple-element.91) | copy-start | bytes 9437188
  467.2 8.5 %copy-start.12 = (f32[24,2048]{1,0:T(8,128)S(1)}, f32[24,2048]{1,0:T(8,128)}, u32[]{:S(2)}) copy-start(f32[24,2048]{1,0:T(8,128)} %get-tuple-element.80) | copy-start | bytes 589828
  467.2 8.7 %copy-start.2 = (bf16[256,2048]{1,0:T(8,128)(2,1)S(1)}, bf16[256,2048]{1,0:T(8,128)(2,1)}, u32[]{:S(2)}) copy-start(bf16[256,2048]{1,0:T(8,128)(2,1)} %get-tuple-element.75) | copy-start | bytes 3145732
  475.9 4.5 copy-start.5
  475.9 4.5 copy-start.7
  480.4 4.5 copy-start.4
  480.4 4.5 copy-start.9
  582.5 4.6 copy-start
  587.2 2.6 copy-start.3
  589.8 1.7 copy-start.6
  589.8 2.5 copy-start.11
  589.8 3.2 copy-start.10
Sparse Core Ops, SparseCore 0:
  233.8 226.7 reduce-scatter.1
  485.0 44.2 all-reduce.5

commit v6 on v5

--- a/solution.py
+++ b/solution.py
@@ -151,150 +151,6 @@
         return 0
 
     lax.fori_loop(0, rows // step, body, 0)
-
-
-def scatter_kernel(x_size, parts, pair, *refs):
-    z_size = 4
-    ins, outs, refs = refs[:parts], refs[parts : 2 * parts], refs[2 * parts :]
-    own, c_buf, x_buf, z_buf = (refs[i * parts : (i + 1) * parts] for i in range(4))
-    refs = refs[4 * parts :]
-    y_buf = None
-    if pair:
-        y_buf, y_s, y_r, refs = refs[:parts], refs[parts], refs[parts + 1], refs[parts + 2 :]
-    l_sem, c_s, c_r, x_s, x_r, z_s, z_r = refs
-    z, x, core = place_of(x_size)
-    at = functools.partial(index_of, x_size=x_size)
-    half = z // 2
-    inner = ((z + 3) // 4) * ((6 - z) // 4)
-    order = [3 - 3 * half, 2 - half, 1 - z + 4 * half, z]
-    load = lambda p, w, v: pltpu.make_async_copy(
-        ins[p].at[at(w, v, core)], own[p].at[w, v], l_sem.at[p, w, v]
-    )
-    beside = lambda p, w, v: remote(
-        ins[p].at[at(w, v, 1 - core)],
-        c_buf[p].at[w, v],
-        c_s.at[p, w, v],
-        c_r.at[p, w, v],
-        at(z, x, 1 - core),
-    )
-    across = lambda p, w: remote(
-        c_buf[p].at[w, 1 - x], x_buf[p].at[w], x_s.at[p, w], x_r.at[p, w], at(z, 1 - x, core)
-    )
-
-    def along(p, w, slot, target):
-        return remote(
-            c_buf[p].at[w, x], z_buf[p].at[slot], z_s.at[p, w], z_r.at[p, slot], at(target, x, core)
-        )
-
-    twin = lambda p: pltpu.make_async_remote_copy(
-        src_ref=c_buf[p].at[z, x],
-        dst_ref=y_buf[p],
-        send_sem=y_s.at[p],
-        recv_sem=y_r.at[p],
-        device_id={"tensor": 1 - lax.axis_index("tensor")},
-        device_id_type=pl.DeviceIdType.MESH,
-    )
-
-    for v in (1 - x, x):
-        for w in order:
-            for p in range(parts):
-                load(p, w, v).start()
-    greet(z, x, core, z_size, x_size, pair)
-    for v in (1 - x, x):
-        for w in order:
-            for p in range(parts):
-                beside(p, w, v).start()
-    for w in order:
-        for p in range(parts):
-            load(p, w, 1 - x).wait()
-            beside(p, w, 1 - x).wait_recv()
-            add_into(c_buf[p].at[w, 1 - x], own[p].at[w, 1 - x])
-            across(p, w).start()
-    for k, w in enumerate(order):
-        for p in range(parts):
-            load(p, w, x).wait()
-            beside(p, w, x).wait_recv()
-            add_into(c_buf[p].at[w, x], own[p].at[w, x])
-            across(p, w).wait_recv()
-            if k < 3:
-
-                @pl.when(inner == 1)
-                def _():
-                    along(p, w, w, z).wait_recv()
-                    add_into(c_buf[p].at[w, x], x_buf[p].at[w], z_buf[p].at[w])
-
-                @pl.when(inner == 0)
-                def _():
-                    add_into(c_buf[p].at[w, x], x_buf[p].at[w])
-
-                @pl.when(w > z)
-                def _():
-                    along(p, w, w, z + 1).start()
-
-                @pl.when(w < z - 1)
-                def _():
-                    along(p, w, w, z - 1).start()
-
-                @pl.when(w == z - 1)
-                def _():
-                    along(p, w, z_size, z - 1).start()
-
-            else:
-                add_into(c_buf[p].at[w, x], x_buf[p].at[w])
-
-                @pl.when(z > 0)
-                def _():
-                    along(p, w, z, z).wait_recv()
-                    add_into(c_buf[p].at[w, x], z_buf[p].at[z])
-
-                @pl.when(z < z_size - 1)
-                def _():
-                    along(p, w, z_size, z).wait_recv()
-                    add_into(c_buf[p].at[w, x], z_buf[p].at[z_size])
-
-                if pair:
-                    twin(p).start()
-                else:
-                    outs[p][...] = c_buf[p][z, x].astype(outs[p].dtype)
-    if pair:
-        for p in range(parts):
-            twin(p).wait()
-            outs[p][...] = (
-                c_buf[p][z, x].astype(jnp.float32) + y_buf[p][...].astype(jnp.float32)
-            ).astype(outs[p].dtype)
-    for w in range(z_size):
-        for p in range(parts):
-            for v in range(x_size):
-                beside(p, w, v).wait_send()
-            across(p, w).wait_send()
-
-            @pl.when(z != w)
-            def _():
-                along(p, w, w, z).wait_send()
-
-
-def scatter_sums(arrays, x_size, collective_id, out_dtype, pair=False):
-    parts = len(arrays)
-    dma = pltpu.SemaphoreType.DMA
-    blocks = [a.shape[1:] for a in arrays]
-    return pl.pallas_call(
-        functools.partial(scatter_kernel, x_size, parts, pair),
-        out_shape=[jax.ShapeDtypeStruct(b, out_dtype) for b in blocks],
-        in_specs=[pl.BlockSpec(memory_space=pl.ANY)] * parts,
-        out_specs=[pl.BlockSpec(memory_space=pltpu.VMEM)] * parts,
-        scratch_shapes=[pltpu.VMEM((4, x_size) + b, a.dtype) for a, b in zip(arrays, blocks)]
-        + [pltpu.VMEM((4, x_size) + b, a.dtype) for a, b in zip(arrays, blocks)]
-        + [pltpu.VMEM((4,) + b, a.dtype) for a, b in zip(arrays, blocks)]
-        + [pltpu.VMEM((5,) + b, a.dtype) for a, b in zip(arrays, blocks)]
-        + ([pltpu.VMEM(b, a.dtype) for a, b in zip(arrays, blocks)] + [dma((parts,))] * 2 if pair else [])
-        + [dma((parts, 4, x_size))] * 3
-        + [dma((parts, 4))] * 3
-        + [dma((parts, 5))],
-        compiler_params=pltpu.CompilerParams(
-            collective_id=collective_id, has_side_effects=True, vmem_limit_bytes=VMEM_LIMIT
-        ),
-        name="scatter_sums",
-    )(*arrays)
 
 
 def nn(left, right):
@@ -431,25 +287,36 @@
     rank = lax.axis_index("tensor")
     edge = 1 - ((z + 3) // 4) * ((6 - z) // 4)
     part_rows = rows_here // 2
-
-    def part(j, v, which):
-        store = blk if j in (1, 4) else grad_all
+    whose = (order[2], order[2], order[3], order[3], order[3], z, (z + 2) % 4, order[3])
+
+    def part(store, w, v, which):
         rows = pl.ds(pl.multiple_of(which * part_rows, part_rows), part_rows)
-        return store.at[at(order[2 if j < 2 else 3], v, core), rows]
-
-    def link(j, target=0):
-        block = part(j, x, rank)
-        target = at(target, x, core) if j == 2 else at(z, 1 - x, core)
-        return remote(block, block, h_s.at[j], h_r.at[j], target)
-
-    landed = lambda j: x if j == 2 else 1 - x
+        return store.at[at(w, v, core), rows]
+
+    store_of = lambda j: grad_all if j in (0, 2, 3) else blk
+
+    def link(j, w=None, target=None):
+        block = part(store_of(j), whose[j] if w is None else w, x, rank)
+        src = block
+        if j == 5:
+            src = own_ffn.at[pl.ds(pl.multiple_of(rank * part_rows, part_rows), part_rows)]
+        way = 0
+        if j in (2, 6, 7):
+            target = z if target is None else target
+            way = (target - z + 1) // 2
+            target = at(target, x, core)
+        else:
+            target = at(z, 1 - x, core)
+        return remote(src, block, h_s.at[j, way], h_r.at[j], target)
+
+    landed = lambda j: x if j in (2, 6, 7) else 1 - x
 
     def swap(j):
-        block = part(j, landed(j), rank)
+        block = part(store_of(j), whose[j], landed(j), rank)
         return pair_copy(block, block, y_s.at[j], y_r.at[j])
 
     def half_beside(j, i):
-        block = part(j, landed(j), rank + i * (1 - 2 * rank))
+        block = part(store_of(j), whose[j], landed(j), rank + i * (1 - 2 * rank))
         return remote(block, block, hc_s.at[j, i], hc_r.at[j, i], at(z, x, 1 - core))
 
     def link_done(j):
@@ -465,41 +332,47 @@
         half_beside(j, 0).wait_recv()
         half_beside(j, 1).wait_recv()
 
+    def at_ends(do):
+        pl.when(edge == 1)(do)
+
+    def inside(do):
+        pl.when(edge == 0)(do)
+
     for a in (1, 0):
         beside(a, z, x, True).start()
-        across(a, z, True).start()
+        if a == 1:
+            across(a, z, True).start()
+        else:
+            link(5).start()
         pl.when(z < z_size - 1)(lambda: up(a, 0).start())
         pl.when(z > 0)(lambda: down(a, 0).start())
+    link(0).start()
 
     def pass_on(d):
-        for a in (1, 0):
+        for a in (1, 0) if d == 1 else (1,):
 
             @pl.when(z >= d)
             def _():
                 up(a, d - 1).wait_recv()
-                pl.when(z < z_size - 1)(lambda: up(a, d).start())
+                if a == 1:
+                    pl.when(z < z_size - 1)(lambda: up(a, d).start())
+                else:
+                    inside(lambda: link(6, z - 1, z + 1).start())
                 beside(a, z - d, x).start()
 
             @pl.when(z + d < z_size)
             def _():
                 down(a, d - 1).wait_recv()
-                pl.when(z > 0)(lambda: down(a, d).start())
+                if a == 1:
+                    pl.when(z > 0)(lambda: down(a, d).start())
+                else:
+                    inside(lambda: link(6, z + 1, z - 1).start())
                 beside(a, z + d, x).start()
 
     def from_across(w, arrays=(1, 0)):
         for a in arrays:
             across(a, w).wait_recv()
             beside(a, w, 1 - x).start()
-
-    def at_ends(do):
-        pl.when(edge == 1)(do)
-
-    def inside(do):
-        pl.when(edge == 0)(do)
-
-    def far_over_x():
-        link(4).start()
-        across(1, order[3]).start()
 
     def early(k):
         @pl.when(k == 1)
@@ -507,69 +380,87 @@
             pass_on(1)
             for a in (1, 0):
                 across(a, order[1]).start()
-            link(0).start()
-            from_across(order[0])
-
-        @pl.when((k == 2) & (edge == 0))
+            swap_done(5)
+            link_done(0)
+            from_across(z, (1,))
+            ready(5)
+
+        @pl.when(k == 2)
         def _():
-            link(2, 3 * (z - 1)).start()
+            link_done(6)
+            link(1).start()
+
+            @inside
+            def _():
+                link(7, None, 3 * (z - 1)).start()
+                link(2, None, 3 * (z - 1)).start()
+                link(4).start()
+                link(3).start()
+
+            pass_on(2)
+            across(1, order[2]).start()
+            swap_done(0)
 
         @pl.when(k == 3)
         def _():
-            pass_on(2)
-            link(1).start()
-            across(1, order[2]).start()
-
-            @inside
+            from_across(order[1])
+            swap_done(6)
+
+            @at_ends
             def _():
+                link_done(7)
+                link(4).start()
+
+        @pl.when(k == 4)
+        def _():
+            ready(0)
+            link_done(1)
+
+            @at_ends
+            def _():
+                ready(6)
+                link_done(2)
                 link(3).start()
-                far_over_x()
-
-            from_across(order[1])
-
-        @pl.when((k == 4) & (edge == 1))
-        def _():
-            link_done(2)
-            link(3).start()
+
+            pass_on(3)
+            across(1, order[3]).start()
+            from_across(order[2], (1,))
 
         @pl.when(k == 5)
         def _():
-            ready(0)
             grad_copy(5).start()
-            pass_on(3)
-            at_ends(far_over_x)
+            at_ends(lambda: swap_done(7))
             swap_done(1)
-            at_ends(lambda: swap_done(2))
-            from_across(order[2], (1,))
             ready(1)
 
         @pl.when(k == 6)
         def _():
-            link_done(4)
             from_across(order[3], (1,))
+            at_ends(lambda: ready(7))
+            inside(lambda: ready(6))
 
         @pl.when(k == 7)
         def _():
+            swap_done(3)
             ready(3)
             grad_copy(7).start()
-            swap_done(4)
             ready(4)
 
     def midway(k):
-        pl.when(k == 3)(lambda: link_done(0))
-
-        @pl.when(k == 4)
-        def _():
-            link_done(1)
-            swap_done(0)
+        pl.when(k == 0)(lambda: link_done(5))
+        pl.when(k == 4)(lambda: link_done(4))
 
         @pl.when(k == 5)
         def _():
-            at_ends(lambda: ready(2))
+            @at_ends
+            def _():
+                swap_done(2)
+                ready(2)
+
             grad_copy(6).start()
             link_done(3)
 
-        pl.when(k == 6)(lambda: swap_done(3))
+        pl.when(k == 6)(lambda: swap_done(4))
 
     gate_v[pl.ds(hidden, gate_v.shape[0] - hidden), :] = jnp.zeros(
         (gate_v.shape[0] - hidden, features), bf16
@@ -626,8 +517,9 @@
         early(k)
         grad_copy(k).wait()
         pl.when(k < 4)(lambda: grad_copy(k + 1).start())
-        pl.when((k != 5) & (k != 7))(lambda: beside(0, w, v).wait_recv())
         beside(1, w, v).wait_recv()
+        whole = (k == 0) | (k == 2) | (k == 3) | ((k == 4) & (edge == 0))
+        pl.when(whole)(lambda: beside(0, w, v).wait_recv())
 
         for a in range(2):
             gates = gts[block + a]
@@ -737,29 +629,40 @@
     lax.fori_loop(0, 8, body, 0)
     wait_staged(1, range(7))
     shared_grads[...] = acc[...].astype(bf16)
-    for a in range(2):
-        for i in range(z_size):
-            beside(a, order[i], x).wait_send()
-            if a == 1 or i < 2:
-                beside(a, order[i], 1 - x).wait_send()
-                across(a, order[i]).wait_send()
+    for i in range(z_size):
+        beside(1, order[i], x).wait_send()
+        beside(1, order[i], 1 - x).wait_send()
+        across(1, order[i]).wait_send()
+    for i in range(2):
+        beside(0, order[i], x).wait_send()
+    inside(lambda: beside(0, order[2], x).wait_send())
+    beside(0, order[1], 1 - x).wait_send()
+    across(0, order[1]).wait_send()
     for d in range(z_size):
-        for a in range(2):
+        for a in range(2) if d == 0 else (1,):
             pl.when((z >= d) & (z < z_size - 1))(lambda: up(a, d).wait_send())
             pl.when((z + d < z_size) & (z > 0))(lambda: down(a, d).wait_send())
-    inside(lambda: link(2, 3 * (z - 1)).wait_send())
-    for j in range(5):
+
+    @inside
+    def _():
+        link(2, None, 3 * (z - 1)).wait_send()
+        link(7, None, 3 * (z - 1)).wait_send()
+        link(6, z - 1, z + 1).wait_send()
+        link(6, z + 1, z - 1).wait_send()
+
+    for j in range(8):
 
         def sent_on(j=j):
             swap(j).wait_send()
             half_beside(j, 0).wait_send()
             half_beside(j, 1).wait_send()
 
-        if j == 2:
+        if j in (2, 7):
             at_ends(sent_on)
         else:
+            sent_on()
+        if j not in (2, 6, 7):
             link(j).wait_send()
-            sent_on()
 
 
 def ffn_tuned(own_ffn, own_gates, grad_all, gate_t, up_t, down_t, shared_in, shared_out, slots):
@@ -816,8 +719,9 @@
         + [dma((2, 4))] * 6
         + [dma((2, 4, 2))] * 2
         + [dma((5,)), dma((2,)), dma((7,))]
-        + [dma((5,))] * 4
-        + [dma((5, 2))] * 2,
+        + [dma((8, 2))]
+        + [dma((8,))] * 3
+        + [dma((8, 2))] * 2,
         compiler_params=pltpu.CompilerParams(
             collective_id=1, has_side_effects=True, vmem_limit_bytes=VMEM_LIMIT
         ),
@@ -1202,22 +1106,51 @@
     key_turned,
     latent,
     log_totals,
+    normed,
+    context,
+    latent_bf,
     w_query,
     down_t,
     kv_up,
     w_out,
     grad_tokens,
+    out_grad,
+    query_grad,
+    up_grad,
+    down_grad,
+    vector_grad,
+    wq_v,
+    down_v,
+    up_v,
+    unit,
     grad_hidden_bf,
     grad_query,
     grad_kv,
     grad_low,
     vectors,
-    wq_v,
-    down_v,
-    up_v,
-    out_v,
-    unit,
-    grad_hidden,
+    hidden_t,
+    normed_t,
+    latent_t,
+    low_t,
+    send_wide,
+    send_up,
+    send_down,
+    send_vector,
+    out_c,
+    query_c,
+    up_c,
+    down_c,
+    vector_c,
+    out_x,
+    query_x,
+    up_x,
+    down_x,
+    vector_x,
+    out_z,
+    query_z,
+    up_z,
+    down_z,
+    vector_z,
     grad_context,
     grad_turned,
     sent,
@@ -1228,7 +1161,116 @@
     s_sem,
     r_sem,
     e_sem,
+    c_s,
+    c_r,
+    x_s,
+    x_r,
+    z_s,
+    z_r,
 ):
+    grad_hidden = grad_tokens
+    z_size, x_size = 4, 2
+    z, x, core = place_of(x_size)
+    place_rank = lax.axis_index("tensor")
+    at = functools.partial(index_of, x_size=x_size)
+    half = z // 2
+    inner = ((z + 3) // 4) * ((6 - z) // 4)
+    order = [3 - 3 * half, 2 - half, 1 - z + 4 * half, z]
+    blocks = [(w, v) for v in (1 - x, x) for w in order]
+    outs = (out_grad, query_grad, up_grad, down_grad, vector_grad)
+    c_buf = (out_c, query_c, up_c, down_c, vector_c)
+    x_buf = (out_x, query_x, up_x, down_x, vector_x)
+    z_buf = (out_z, query_z, up_z, down_z, vector_z)
+
+    def product(p, owner):
+        rows = lambda size: pl.ds(pl.multiple_of(owner * size, size), size)
+        if p == 0:
+            return nn(hidden_t[rows(128), :], context[...])
+        if p == 1:
+            return nn(normed_t[rows(128), :], grad_query[...])
+        if p == 2:
+            size = up_grad.shape[0]
+            return nn(latent_t[rows(size), :], grad_kv[...])
+        if p == 3:
+            size = down_grad.shape[0]
+            mine = pl.ds(pl.multiple_of(place_rank * size, 32), size)
+            return nn(low_t[mine, :], normed[:, rows(128)])
+        return vectors[:, rows(128)]
+
+    def staging(p, i):
+        if p == 0:
+            return send_wide.at[i, :, pl.ds(0, out_grad.shape[1])]
+        return (None, send_wide, send_up, send_down, send_vector)[p].at[i]
+
+    def beside(p, i):
+        w, v = blocks[i]
+        return remote(
+            staging(p, i), c_buf[p].at[w, v], c_s.at[p, i], c_r.at[p, w, v], at(z, x, 1 - core)
+        )
+
+    across = lambda p, w: remote(
+        c_buf[p].at[w, 1 - x], x_buf[p].at[w], x_s.at[p, w], x_r.at[p, w], at(z, 1 - x, core)
+    )
+
+    def along(p, w, slot, target):
+        return remote(
+            c_buf[p].at[w, x], z_buf[p].at[slot], z_s.at[p, w], z_r.at[p, slot], at(target, x, core)
+        )
+
+    def to_sibling(p):
+        for i, (w, v) in enumerate(blocks):
+            staging(p, i)[...] = product(p, at(w, v, 1 - core)).astype(c_buf[p].dtype)
+            beside(p, i).start()
+
+    def over_x(p):
+        for i, (w, v) in enumerate(blocks):
+            beside(p, i).wait_recv()
+            total = c_buf[p][w, v].astype(jnp.float32) + product(p, at(w, v, core))
+            c_buf[p][w, v] = total.astype(c_buf[p].dtype)
+            if i < 4:
+                across(p, w).start()
+
+    def over_z(p, k):
+        w = order[k]
+        across(p, w).wait_recv()
+        if k < 3:
+
+            @pl.when(inner == 1)
+            def _():
+                along(p, w, w, z).wait_recv()
+                add_into(c_buf[p].at[w, x], x_buf[p].at[w], z_buf[p].at[w])
+
+            @pl.when(inner == 0)
+            def _():
+                add_into(c_buf[p].at[w, x], x_buf[p].at[w])
+
+            @pl.when(w > z)
+            def _():
+                along(p, w, w, z + 1).start()
+
+            @pl.when(w < z - 1)
+            def _():
+                along(p, w, w, z - 1).start()
+
+            @pl.when(w == z - 1)
+            def _():
+                along(p, w, z_size, z - 1).start()
+
+        else:
+            add_into(c_buf[p].at[w, x], x_buf[p].at[w])
+
+            @pl.when(z > 0)
+            def _():
+                along(p, w, z, z).wait_recv()
+                add_into(c_buf[p].at[w, x], z_buf[p].at[z])
+
+            @pl.when(z < z_size - 1)
+            def _():
+                along(p, w, z_size, z).wait_recv()
+                add_into(c_buf[p].at[w, x], z_buf[p].at[z_size])
+
+            outs[p][...] = c_buf[p][z, x].astype(outs[p].dtype)
+
     bf16, f32 = jnp.bfloat16, jnp.float32
     highest = lax.Precision.HIGHEST
     rows, features = tokens.shape
@@ -1236,6 +1278,7 @@
     heads = kv_up.shape[1] // 256
     turned = down_t.shape[0] - rank
     tail = pl.ds(rank, turned)
+    out_v = wq_v.at[:, pl.ds(0, w_out.shape[1])]
     loads = [
         pltpu.make_async_copy(w_out, out_v, w_sem.at[0]),
         pltpu.make_async_copy(kv_up, up_v, w_sem.at[1]),
@@ -1243,9 +1286,11 @@
         pltpu.make_async_copy(down_t, down_v.at[pl.ds(0, rank + turned)], w_sem.at[3]),
         pltpu.make_async_copy(down_t.at[tail], down_v.at[pl.ds(rank + turned, turned)], w_sem.at[4]),
     ]
-    for copy in loads:
+    rows_copy = pltpu.make_async_copy(hidden, unit, w_sem.at[5])
+    rows_copy.start()
+    for copy in loads[:2] + loads[3:]:
         copy.start()
-    greet_pair()
+    greet(z, x, core, z_size, x_size, True)
     cosine, sine, met = turn_tables(lengths, freqs, rows)
     lane = lax.broadcasted_iota(jnp.int32, (rows, 128), 1)
     experts = lax.axis_size("dp")
@@ -1262,7 +1307,8 @@
         precision=highest,
         preferred_element_type=f32,
     )
-    values, unit_rows, factor = rms_normalize_pieces(hidden[...], g_ffn[...])
+    rows_copy.wait()
+    values, unit_rows, factor = rms_normalize_pieces(unit[...], g_ffn[...])
     unit[...] = unit_rows
     vectors[pl.ds(0, experts), :] = lax.dot_general(
         logits, values, (((0,), (0,)), ((), ())), precision=highest, preferred_element_type=f32
@@ -1273,6 +1319,8 @@
         grad_in, unit[...], factor, g_ffn[...]
     )
     grad_hidden_bf[...] = grad_hidden[...].astype(bf16)
+    hidden_t[...] = grad_hidden_bf[...].T
+    to_sibling(0)
     loads[0].wait()
 
     def back_out(n, _):
@@ -1281,7 +1329,11 @@
         return 0
 
     lax.fori_loop(0, grad_context.shape[1] // 256, back_out, 0)
+    loads[2].start()
     grad_turned[...] = jnp.zeros(grad_turned.shape, f32)
+    over_x(0)
+    normed_t[...] = normed[...].T
+    latent_t[...] = latent_bf[...].T
 
     def two_heads(i, _):
         pieces = []
@@ -1316,6 +1368,9 @@
         return 0
 
     lax.fori_loop(0, heads // 2, two_heads, 0)
+    for i in range(8):
+        beside(0, i).wait_send()
+    to_sibling(1)
     loads[1].wait()
     low_sent[:, pl.ds(0, rank)] = contract_last(grad_kv[...], up_v[...]).astype(bf16)
     folded = turn(grad_turned[...] + pltpu.roll(grad_turned[...], 64, 1), cosine, -sine)
@@ -1334,6 +1389,11 @@
         return 0
 
     lax.fori_loop(0, chunks, project, 0)
+    over_x(1)
+    to_sibling(2)
+    for k in range(3):
+        over_z(0, k)
+    over_x(2)
     loads[3].wait()
     loads[4].wait()
     low_copy.wait()
@@ -1342,11 +1402,17 @@
     _, latent_unit, latent_factor = rms_normalize_pieces(latent[...], g_latent[...])
     grad_gain = jnp.sum(grad_normed * latent_unit, axis=0, keepdims=True)
     for i in range(rank // 128):
-        vectors[pl.ds(experts + 2 + i, 1), pl.ds(0, 128)] = grad_gain[:, i * 128 : (i + 1) * 128]
+        vectors[pl.ds(experts + 2 + i, 1), :] = jnp.concatenate(
+            [grad_gain[:, i * 128 : (i + 1) * 128]] * (features // 128), axis=1
+        )
     grad_low[:, pl.ds(0, rank)] = normalize_back(
         grad_normed, latent_unit, latent_factor, g_latent[...]
     ).astype(bf16)
     grad_low[:, pl.ds(rank, 128)] = low[:, rank:].astype(bf16)
+    low_t[...] = grad_low[...].T
+    to_sibling(3)
+    over_x(3)
+    over_z(0, 3)
 
     def join(i, _):
         cols = pl.ds(pl.multiple_of(i * width, width), width)
@@ -1358,9 +1424,24 @@
     lax.fori_loop(0, chunks, join, 0)
     _, attn_unit, attn_factor = rms_normalize_pieces(tokens[...].astype(f32), g_attn[...])
     vectors[pl.ds(experts, 1), :] = jnp.sum(unit[...] * attn_unit, axis=0, keepdims=True)
+    to_sibling(4)
     grad_tokens[...] = grad_hidden[...] + normalize_back(
         unit[...], attn_unit, attn_factor, g_attn[...]
     )
+    over_x(4)
+    for p in range(1, 5):
+        for k in range(4):
+            over_z(p, k)
+    for p in range(5):
+        for i in range(8):
+            if p > 0:
+                beside(p, i).wait_send()
+        for w in range(z_size):
+            across(p, w).wait_send()
+
+            @pl.when(z != w)
+            def _():
+                along(p, w, w, z).wait_send()
 
 
 def backward_tuned(lengths, freqs, sums, values, gains, router_t, saved, weights):
@@ -1374,36 +1455,58 @@
     smem = pl.BlockSpec(memory_space=pltpu.SMEM)
     shape = jax.ShapeDtypeStruct
     chunks = 8
-    experts = lax.axis_size("dp")
+    experts, ranks = lax.axis_size("dp"), lax.axis_size("tensor")
+    devices = experts
+    share_rows = features // devices
+    blocks = [
+        ((share_rows, w_out.shape[1]), bf16),
+        ((share_rows, w_query.shape[1]), bf16),
+        ((rank // devices, columns), bf16),
+        ((down_t.shape[0] // ranks, share_rows), bf16),
+        ((experts + 8, share_rows), f32),
+    ]
+    several = lambda *lead: [pltpu.VMEM(lead + b, kind) for b, kind in blocks]
     return pl.pallas_call(
         backward_kernel,
-        out_shape=[
-            shape((rows, features), f32),
-            shape((rows, features), bf16),
-            shape((rows, w_query.shape[1]), bf16),
-            shape((rows, columns), bf16),
-            shape((rows, rank + 128), bf16),
-            shape((experts + 8, features), f32),
-        ],
-        in_specs=[smem] + [vmem] * 15 + [anywhere] * 4,
+        out_shape=[shape((rows, features), f32)] + [shape(b, f32) for b, _ in blocks],
+        in_specs=[smem, vmem, vmem, anywhere] + [vmem] * 15 + [anywhere] * 4,
         out_specs=[vmem] * 6,
         scratch_shapes=[
             pltpu.VMEM(w_query.shape, bf16),
             pltpu.VMEM((rank + 128, features), bf16),
             pltpu.VMEM(kv_up.shape, bf16),
-            pltpu.VMEM(w_out.shape, bf16),
             pltpu.VMEM((rows, features), f32),
-            pltpu.VMEM((rows, features), f32),
+            pltpu.VMEM((rows, features), bf16),
+            pltpu.VMEM((rows, w_query.shape[1]), bf16),
+            pltpu.VMEM((rows, columns), bf16),
+            pltpu.VMEM((rows, rank + 128), bf16),
+            pltpu.VMEM((experts + 8, features), f32),
+            pltpu.VMEM((features, rows), bf16),
+            pltpu.VMEM((features, rows), bf16),
+            pltpu.VMEM((rank, rows), bf16),
+            pltpu.VMEM((rank + 128, rows), bf16),
+        ]
+        + several(8)[1:]
+        + several(4, 2)
+        + several(4)
+        + several(5)
+        + [
             pltpu.VMEM((rows, heads * 128), bf16),
             pltpu.VMEM((rows, 128), f32),
             pltpu.VMEM((chunks, rows, features // chunks), bf16),
             pltpu.VMEM((chunks, rows, features // chunks), bf16),
             pltpu.VMEM((rows, rank + 128), bf16),
             pltpu.VMEM((rows, rank + 128), bf16),
-            dma((5,)),
+            dma((6,)),
             dma((chunks,)),
             dma((chunks,)),
             dma((2,)),
+            dma((5, 8)),
+            dma((5, 4, 2)),
+            dma((5, 4)),
+            dma((5, 4)),
+            dma((5, 4)),
+            dma((5, 5)),
         ],
         compiler_params=pltpu.CompilerParams(
             collective_id=4, has_side_effects=True, vmem_limit_bytes=VMEM_LIMIT
@@ -1650,14 +1753,12 @@
         capacity,
     )
     rows, dy = rows.reshape(-1, features), dy.reshape(-1, features)
-    he, dge, due = (a.reshape(-1, a.shape[2])[:, :hidden] for a in (he, dge, due))
+    he, dge, due = (a.reshape(-1, a.shape[2]) for a in (he, dge, due))
     devices, rows_here = everyone_grad.shape[:2]
     return (
-        out_part.reshape(devices, rows_here, -1),
+        out_part.reshape(devices * rows_here, -1),
         grad_part.reshape(devices, rows_here, -1),
-        contract_first(rows, dge)[None],
-        contract_first(rows, due)[None],
-        contract_first(dy, he)[None],
+        [rows, dy, he, dge, due],
         shared_grads.reshape(3, 128, features)[:, :part].reshape(3 * part, features),
     )
 
@@ -1823,7 +1924,7 @@
         lax.dynamic_slice_in_dim(w, own * part, part, 1)
         for w in (shared_gate, shared_up, shared_down)
     ]
-    ffn_part, grad_ffn_part, *expert_grads, shared_grads = ffn_with_kernel(
+    ffn_part, grad_ffn_part, expert_saved, shared_grads = ffn_with_kernel(
         ffn_bf,
         dense_gates,
         everyone_grad,
@@ -1833,44 +1934,40 @@
         experts,
     )
     shared_grads = shared_home(shared_grads, part)
-    ffn_total = lax.psum_scatter(
-        ffn_part.reshape(devices * rows_here, features), "dp", scatter_dimension=0, tiled=True
-    )
-    ffn_total = lax.psum(ffn_total, "tensor").astype(jnp.float32)
-    output = (hidden + ffn_total).astype(jnp.bfloat16)
+    ffn_sum = lax.psum_scatter(ffn_part, "dp", scatter_dimension=0, tiled=True)
     sums = home_sums(grad_ffn_part, 3, 2)
-    grad_tokens, grad_hidden_bf, grad_query, grad_kv, grad_low, vectors = backward_tuned(
+    (
+        grad_tokens,
+        grad_w_out,
+        grad_w_query,
+        grad_w_kv_up,
+        grad_w_kv_down,
+        vectors,
+    ) = backward_tuned(
         lengths,
         freqs,
         sums,
         [hidden, grad_out, tokens, probs],
         gains,
         router_t,
-        [queries, kv, key_turned, latent, log_totals],
+        [queries, kv, key_turned, latent, log_totals, normed, context, latent_bf],
         weights,
     )
+    grad_tokens, ffn_sum, *expert_saved = lax.optimization_barrier(
+        (grad_tokens, ffn_sum, *expert_saved)
+    )
+    ffn_twin = lax.ppermute(ffn_sum, "tensor", [(0, 1), (1, 0)])
+    rows, dy, he, dge, due = expert_saved
+    units = expert_gate.shape[2]
+    expert_grads = [
+        contract_first(rows, dge[:, :units])[None],
+        contract_first(rows, due[:, :units])[None],
+        contract_first(dy, he[:, :units])[None],
+    ]
+    output = (
+        hidden + (ffn_sum.astype(jnp.float32) + ffn_twin.astype(jnp.float32))
+    ).astype(jnp.bfloat16)
     share_rows = features // devices
-    columns = key_value_down_weight.shape[1]
-    grad_columns = lax.dynamic_slice_in_dim(
-        grad_low, rank * (columns // ranks), columns // ranks, 1
-    )
-    products = [
-        contract_first(normed, grad_query),
-        contract_first(grad_hidden_bf, context),
-        contract_first(latent_bf, grad_kv),
-        contract_first(normed, grad_columns),
-    ]
-    blocks = [
-        a.astype(jnp.bfloat16).reshape(devices, a.shape[0] // devices, a.shape[1])
-        for a in products
-    ]
-    vectors = vectors.reshape(experts + 8, devices, share_rows).transpose(1, 0, 2)
-    vectors = vectors.at[:, experts + 2 : experts + 2 + LATENT_RANK // 128].set(
-        vectors[:1, experts + 2 : experts + 2 + LATENT_RANK // 128]
-    )
-    grad_w_query, grad_w_out, grad_w_kv_up, grad_w_kv_down, vectors = scatter_sums(
-        blocks + [vectors], 2, 5, jnp.float32
-    )
     router_rows = share_rows // ranks
     grad_router = lax.dynamic_slice_in_dim(vectors[:experts], rank * router_rows, router_rows, 1).T
     latent_rows = LATENT_RANK // devices // ranks
@@ -1885,7 +1982,7 @@
         grad_tokens,
         vectors[experts],
         grad_w_query,
-        grad_w_kv_down,
+        grad_w_kv_down.T,
         grad_g_kv,
         grad_w_kv_up,
         grad_w_out,

time: 608 us -> 609 us (level)
  starting transfers between devices: 3.89 us -> 19.6 us
  matrix products: 42.9 us -> 28.3 us
    dot_general x7 -> x3, matrix products: 42.9 us -> 28.3 us  [contract_first(): lax.dot_general(left, right, (((0,), (0,)), ((), ())), precision=precisio...]
    all_to_all x1, starting transfers between devices: 3.81 us -> 18.1 us  [shared_home(): lax.all_to_all(grads.reshape(3 * part, devices, share_rows).transpose(1,...]
    pallas_call x2 -> x1, Pallas kernels: 135 us -> 148 us  [backward_tuned(): pl.pallas_call(backward_kernel, out_shape=[shape((rows, features), f32)]...]
    unnamed x51 -> x43, local copies, waits for them, and re-layouts: 13.4 us -> 11.9 us
  transfers between devices with their start and end apart: 3 -> 3, of which waited for: 0 -> 0; matrix products, arithmetic and copies ran while one was open for 10% -> 6% of each run, Pallas kernels for 48% -> 50%
where the time goes in v6:
time: 609 us; the launch traced here: 600 us
  Pallas kernels  512 us (84%)
  matrix products  28.3 us (5%)
  local copies, waits for them, and re-layouts  23.2 us (4%)
  starting transfers between devices  19.6 us (3%)
  between operations  14.5 us (2%)
    pallas_call x1, Pallas kernels, ffn_tuned(): pl.pallas_call(functools.partial(ffn_kernel, 2), out_shape=[shape((8, 2,...  152 us
    pallas_call x1, Pallas kernels, home_sums(): pl.pallas_call(functools.partial(home_kernel, 2, parts, share), out_shape...  150 us
    pallas_call x1, Pallas kernels, backward_tuned(): pl.pallas_call(backward_kernel, out_shape=[shape((rows, features), f32)]...  148 us
    pallas_call x1, Pallas kernels, forward_tuned(): pl.pallas_call(forward_kernel, out_shape=[shape((rows, features), f32), s...  61.6 us
    dot_general x3, matrix products, contract_first(): lax.dot_general(left, right, (((0,), (0,)), ((), ())), precision=precisio...  28.3 us
    all_to_all x1, starting transfers between devices, shared_home(): lax.all_to_all(grads.reshape(3 * part, devices, share_rows).transpose(1,...  18.1 us
  transfers between devices with their start and end apart: 3, of which 0 were waited for; matrix products, arithmetic and copies ran while one was open for 6% of the time, Pallas kernels for 50%

profile of v6, /device:TPU:0, one launch (start us, length us, event | category | flops | bytes accessed | tf_op | source)
XLA Modules:
  0.0 599.9 jit_solution(4975683650631345058)
XLA Ops:
  7.3 0.6 broadcast_in_dim_tile.5.freqs
  7.9 1.5 copy.57.routes
  9.3 1.4 constant_dynamic-slice_fusion.2
  11.0 2.0 constant_dynamic-slice_fusion
  13.4 0.8 pad.17.shared_out
  14.3 1.1 fusion.5.shared_in
  15.3 1.1 pad.14.router_t
  16.4 61.6 %attention_forward.1 = (f32[256,2048]{1,0:T(8,128)}, bf16[256,2048]{1,0:T(8,128)(2,1)}, f32[256,128]{1,0:T(8,128)}, f32[256,128]{1,0:T(8,128)}, bf16[256,2048]{1...) custom-call(s32[1,4]{1,0:T(1,128)} %lengths.3, ...), custom_call_target="tpu_custom_call" | custom-call | tf_op jit(solution)/shard_map/attention_forward/pallas_call | solution.py:1038
  78.0 151.6 %ffn.1 = (bf16[8,2,256,2048]{3,2,1,0:T(8,128)(2,1)}, bf16[8,2,256,2176]{3,2,1,0:T(8,128)(2,1)}, bf16[8,256,2048]{2,1,0:T(8,128)(2,1)}, bf16[8,256,2048]{2,1,0:T(...) custom-call(bf16[256,2048]{1,0:T(8,128)(2,1)} %get-tuple-element.51., ...), custom_call_target="tpu_custom_call", output_to_operand_aliasing={{8}: (2, {})} | custom-call | tf_op jit(solution)/shard_map/ffn/pallas_call | solution.py:675
  229.7 1.4 copy-done.4
  231.3 1.3 copy.61
  232.6 18.1 %all-to-all-start = ((bf16[16,128,264]{1,2,0:T(8,128)(2,1)}), bf16[16,128,264]{1,2,0:T(8,128)(2,1)S(1)}, u32[]{:S(2)}, u32[]{:S(2)}) async-start(bf16[16,128,264]{1,2,0:T(8,128)(2,1)} %copy.61), calls=%async_computation.1 | async-start | bytes 2162688 | tf_op jit(solution)/shard_map/all_to_all | solution.py:1875
  250.7 150.5 %home_sums.1.sums = f32[256,2176]{1,0:T(8,128)} custom-call(bf16[16,256,2176]{2,1,0:T(8,128)(2,1)} %bitcast.57), custom_call_target="tpu_custom_call" | custom-call | tf_op jit(solution)/shard_map/home_sums/pallas_call | solution.py:1706
  401.2 148.1 %attention_backward.1 = (f32[256,2048]{1,0:T(8,128)}, f32[128,1024]{1,0:T(8,128)}, f32[128,1536]{1,0:T(8,128)}, f32[32,2048]{1,0:T(8,128)}, f32[288,128]{1,0:T(8,128)}, /*index=5*/f32[24,128]{1,0:T(8,128)}) custom-call(s32[1,4]{1,0:T(1,128)} %lengths.3, f32[1,128]{1,0:T(1,128)} %broadcast_in_dim_tile.5.freqs, f32[256,2176]{1,0:T(8,128)} %home_sums.1.sums, ...), custom_call_target="tpu_custom_call" | custom-call | tf_op jit(solution)/shard_map/attention_backward/pallas_call | solution.py:1469
  549.3 0.7 slice.36
  550.0 0.7 slice_bitcast_fusion
  550.7 0.6 dynamic_slice.18
  551.3 0.7 dynamic-slice_bitcast_fusion
  551.9 1.3 slice_bitcast_fusion.1
  553.3 1.1 copy.64
  554.5 1.1 copy.63
  555.6 1.1 copy.62
  556.7 1.4 collective-permute-start
  558.2 11.8 %convolution_bitcast_fusion.2 = f32[1,2048,704]{1,2,0:T(8,128)} fusion(bf16[2048,2048]{1,0:T(8,128)(2,1)} %bitcast.84, bf16[2048,768]{1,0:T(8,128)(2,1)} %bitcast.90), kind=kOutput, calls=%fused_computation.2 | convolution fusion | flops 5905580032 | bytes 17301504 | tf_op jit(solution)/shard_map/dot_general | solution.py:66
  570.0 8.3 %convolution_bitcast_fusion.1 = f32[1,2048,704]{1,2,0:T(8,128)} fusion(bf16[2048,2048]{1,0:T(8,128)(2,1)S(1)} %bitcast.87, bf16[2048,768]{1,0:T(8,128)(2,1)S(1)} %bitcast.89), kind=kOutput, calls=%fused_computation.1 | convolution fusion | flops 5905580032 | bytes 17301504 | tf_op jit(solution)/shard_map/dot_general | solution.py:66
  578.3 8.3 %convolution_bitcast_fusion = f32[1,2048,704]{1,2,0:T(8,128)} fusion(bf16[2048,2048]{1,0:T(8,128)(2,1)S(1)} %bitcast.83, bf16[2048,768]{1,0:T(8,128)(2,1)S(1)} %bitcast.88), kind=kOutput, calls=%fused_computation | convolution fusion | flops 5905580032 | bytes 17301504 | tf_op jit(solution)/shard_map/dot_general | solution.py:66
  586.6 1.4 add_convert_fusion
  588.5 1.3 copy.75
  589.8 0.9 copy.76
  590.7 0.7 copy.77
  591.3 0.7 copy.78
  592.0 0.8 copy.79
  (44 shorter events, 1.6 us)
Async XLA Ops:
  7.2 549.5 %reduce-scatter.2.cloned.1.call-start = ((), (), s32[]{:S(2)}) async-start(), calls=%async_computation.2 | async-start | bytes 17825792 | tf_op jit(solution)/shard_map/reduce_scatter | solution.py:1937
  11.0 4.3 copy-start.8
  229.6 1.4 copy-start.4
  232.6 320.6 %all-to-all-start = ((bf16[16,128,264]{1,2,0:T(8,128)(2,1)}), bf16[16,128,264]{1,2,0:T(8,128)(2,1)S(1)}, u32[]{:S(2)}, u32[]{:S(2)}) async-start(bf16[16,128,264]{1,2,0:T(8,128)(2,1)} %copy.61), calls=%async_computation.1 | async-start | bytes 2162688 | tf_op jit(solution)/shard_map/all_to_all | solution.py:1875
  556.7 13.2 %slice-start.2 = ((s8[8388608]{0:T(1024)(128)(4,1)}), s8[4194304]{0:T(1024)(128)(4,1)S(1)}, s32[]{:S(2)}) async-start(s8[8388608]{0:T(1024)(128)(4,1)} %bitcast.85), calls=%async_computation.5 | async-start | bytes 8388608
  556.7 13.2 %slice-start.3 = ((s8[8388608]{0:T(1024)(128)(4,1)}), s8[4194304]{0:T(1024)(128)(4,1)S(1)}, s32[]{:S(2)}) async-start(s8[8388608]{0:T(1024)(128)(4,1)} %bitcast.85), calls=%async_computation.6 | async-start | bytes 8388608
  556.7 13.2 %copy-start.10 = (bf16[8,256,768]{2,1,0:T(8,128)(2,1)S(1)}, bf16[8,256,768]{2,1,0:T(8,128)(2,1)}, u32[]{:S(2)}) copy-start(bf16[8,256,768]{2,1,0:T(8,128)(2,1)} %get-tuple-element.70) | copy-start | bytes 9437188
  556.7 29.8 %collective-permute-start = (bf16[256,2048]{1,0:T(8,128)(2,1)}, bf16[256,2048]{1,0:T(8,128)(2,1)S(1)}, u32[]{:S(2)}, u32[]{:S(2)}) collective-permute-start(bf16[256,2048]{1,0:T(8,128)(2,1)} %reduce-scatter.2.cloned.1.call-done), channel_id=1, source_target_pairs={{0,1},{1,0},{2,3},{3,2},{4,5},{5,4},{6,7},{7,6},{8,9},{9,8},{10,11... | collective-permute-start | bytes 3145736 | tf_op jit(solution)/shard_map/ppermute | solution.py:1959
  558.2 20.1 %slice-start = ((s8[8388608]{0:T(1024)(128)(4,1)}), s8[4194304]{0:T(1024)(128)(4,1)S(1)}, s32[]{:S(2)}) async-start(s8[8388608]{0:T(1024)(128)(4,1)} %bitcast.81), calls=%async_computation.3 | async-start | bytes 8388608
  570.0 8.3 %slice-start.1 = ((s8[8388608]{0:T(1024)(128)(4,1)}), s8[4194304]{0:T(1024)(128)(4,1)S(1)}, s32[]{:S(2)}) async-start(s8[8388608]{0:T(1024)(128)(4,1)} %bitcast.81), calls=%async_computation.4 | async-start | bytes 8388608
  570.0 8.3 %copy-start.9 = (bf16[8,256,768]{2,1,0:T(8,128)(2,1)S(1)}, bf16[8,256,768]{2,1,0:T(8,128)(2,1)}, u32[]{:S(2)}) copy-start(bf16[8,256,768]{2,1,0:T(8,128)(2,1)} %get-tuple-element.68) | copy-start | bytes 9437188
  578.3 8.3 %copy-start = (f32[256,2048]{1,0:T(8,128)S(1)}, f32[256,2048]{1,0:T(8,128)}, u32[]{:S(2)}) copy-start(f32[256,2048]{1,0:T(8,128)} %get-tuple-element.50.hidden) | copy-start | bytes 6291460
  578.3 8.3 %copy-start.2 = (bf16[256,2048]{1,0:T(8,128)(2,1)S(1)}, bf16[256,2048]{1,0:T(8,128)(2,1)}, u32[]{:S(2)}) copy-start(bf16[256,2048]{1,0:T(8,128)(2,1)} %reduce-scatter.2.cloned.1.call-done) | copy-start | bytes 3145732
  586.6 1.9 copy-start.1
  588.0 1.7 copy-start.3
  588.0 2.6 copy-start.7
  588.0 3.3 copy-start.6
  588.4 3.6 copy-start.5
Sparse Core Ops, SparseCore 0:
  229.8 253.3 reduce-scatter.1

commit v7 on v6

--- a/solution.py
+++ b/solution.py
@@ -2,6 +2,7 @@
 
 import jax
 import jax.numpy as jnp
+import numpy as np
 from jax import lax
 from jax.experimental import pallas as pl
 from jax.experimental.pallas import tpu as pltpu
@@ -479,6 +480,7 @@
         dx_r[a, pl.ds(slots, 256), :] = s_in[...]
     for copy in keep:
         copy.wait()
+    expert = lax.broadcasted_iota(jnp.int32, (rows_here, own_gates.shape[0]), 1)
     lane = lax.broadcasted_iota(jnp.int32, (rows_here, 128), 1)
     earlier = lax.broadcasted_iota(jnp.int32, (rows_here, rows_here), 1)
     later = lax.broadcasted_iota(jnp.int32, (rows_here, rows_here), 0)
@@ -522,10 +524,10 @@
         pl.when(whole)(lambda: beside(0, w, v).wait_recv())
 
         for a in range(2):
-            gates = gts[block + a]
+            gates = gts[block + a].T
             count = nn(upto, (gates >= 0.0).astype(bf16))
-            gate = jnp.sum(jnp.where(lane == own, gates, 0.0), axis=1, keepdims=True)
-            slot = jnp.sum(jnp.where(lane == own, count, 0.0), axis=1, keepdims=True) - 1.0
+            gate = jnp.sum(jnp.where(expert == own, gates, 0.0), axis=1, keepdims=True)
+            slot = jnp.sum(jnp.where(expert == own, count, 0.0), axis=1, keepdims=True) - 1.0
             pick = ((slot_lane == slot) & (gate >= 0.0)).astype(f32).astype(bf16)
             out_l[a, :, pl.ds(0, slots)] = pick
             dx_l[a, :, pl.ds(0, slots)] = pick
@@ -690,7 +692,7 @@
         input_output_aliases={2: 8},
         scratch_shapes=[
             pltpu.VMEM((16, rows, features), bf16),
-            pltpu.VMEM((16, rows, 128), f32),
+            pltpu.VMEM((16,) + own_gates.shape, f32),
             pltpu.VMEM((padded, features), bf16),
             pltpu.VMEM((padded, features), bf16),
             pltpu.VMEM((padded, features), bf16),
@@ -983,7 +985,7 @@
     named = lane < 0
     for i in range(routes.shape[1]):
         named = named | (lane == routes[:, pl.ds(i, 1)])
-    gates[...] = jnp.where(named, share, -1.0)
+    gates[...] = jnp.where(named, share, -1.0).T[: gates.shape[0]]
 
     @pl.when(z >= 2)
     def _():
@@ -1040,7 +1042,7 @@
         out_shape=[
             shape((rows, features), f32),
             shape((rows, features), bf16),
-            shape((rows, 128), f32),
+            shape((lax.axis_size("dp"), rows), f32),
             shape((rows, 128), f32),
             shape((rows, features), bf16),
             shape((heads, rows, 256), bf16),
@@ -1910,8 +1912,8 @@
     experts = router.shape[1]
     capacity = rows_here * TOPK * 4 // (3 * devices)
     half = (key_value_down_weight.shape[1] - LATENT_RANK) // 2
-    freqs = 10000.0 ** (-jnp.arange(half, dtype=jnp.float32) / half)
-    freqs = jnp.tile(freqs, 128 // half)[None, :]
+    freqs = (10000.0 ** (-np.arange(half) / half)).astype(np.float32)
+    freqs = np.tile(freqs, 128 // half)[None, :]
     router_t = jnp.pad(router.T, ((0, 128 - experts), (0, 0)))
     gains = [g_attn[None, :], latent_norm_gain[None, :], g_ffn[None, :]]
     weights = [w_query, key_value_down_weight.T, key_value_up_weight, w_out]

time: 609 us -> 602 us (0.989)
  transfers between devices with their start and end apart: 3 -> 3, of which waited for: 0 -> 0; matrix products, arithmetic and copies ran while one was open for 6% -> 7% of each run, Pallas kernels for 50% -> 50%
where the time goes in v7:
time: 602 us; the launch traced here: 594 us
  Pallas kernels  509 us (85%)
  matrix products  30.7 us (5%)
  local copies, waits for them, and re-layouts  22.6 us (4%)
  between operations  14.4 us (2%)
  starting transfers between devices  14.3 us (2%)
    pallas_call x1, Pallas kernels, home_sums(): pl.pallas_call(functools.partial(home_kernel, 2, parts, share), out_shape...  151 us
    pallas_call x1, Pallas kernels, ffn_tuned(): pl.pallas_call(functools.partial(ffn_kernel, 2), out_shape=[shape((8, 2,...  149 us
    pallas_call x1, Pallas kernels, backward_tuned(): pl.pallas_call(backward_kernel, out_shape=[shape((rows, features), f32)]...  148 us
    pallas_call x1, Pallas kernels, forward_tuned(): pl.pallas_call(forward_kernel, out_shape=[shape((rows, features), f32), s...  61.5 us
    dot_general x3, matrix products, contract_first(): lax.dot_general(left, right, (((0,), (0,)), ((), ())), precision=precisio...  30.7 us
    all_to_all x1, starting transfers between devices, shared_home(): lax.all_to_all(grads.reshape(3 * part, devices, share_rows).transpose(1,...  12.5 us
  transfers between devices with their start and end apart: 3, of which 0 were waited for; matrix products, arithmetic and copies ran while one was open for 7% of the time, Pallas kernels for 50%

profile of v7, /device:TPU:0, one launch (start us, length us, event | category | flops | bytes accessed | tf_op | source)
XLA Modules:
  0.0 593.5 jit_solution(11420677210456903817)
XLA Ops:
  7.2 1.5 copy.58.routes
  8.7 1.4 constant_dynamic-slice_fusion.2
  10.4 2.0 constant_dynamic-slice_fusion
  12.8 0.8 pad.17.shared_out
  13.6 1.1 fusion.5.shared_in
  14.7 1.1 pad.14.router_t
  15.8 61.5 %attention_forward.1 = (f32[256,2048]{1,0:T(8,128)}, bf16[256,2048]{1,0:T(8,128)(2,1)}, f32[16,256]{1,0:T(8,128)}, f32[256,128]{1,0:T(8,128)}, bf16[256,2048]{1,...) custom-call(s32[1,4]{1,0:T(1,128)} %lengths.3, ...), custom_call_target="tpu_custom_call" | custom-call | tf_op jit(solution)/shard_map/attention_forward/pallas_call | solution.py:1040
  77.3 149.1 %ffn.1 = (bf16[8,2,256,2048]{3,2,1,0:T(8,128)(2,1)}, bf16[8,2,256,2176]{3,2,1,0:T(8,128)(2,1)}, bf16[8,256,2048]{2,1,0:T(8,128)(2,1)}, bf16[8,256,2048]{2,1,0:T(...) custom-call(bf16[256,2048]{1,0:T(8,128)(2,1)} %get-tuple-element.51., ...), custom_call_target="tpu_custom_call", output_to_operand_aliasing={{8}: (2, {})} | custom-call | tf_op jit(solution)/shard_map/ffn/pallas_call | solution.py:677
  226.4 1.4 copy-done.4
  228.1 1.3 copy.62
  229.3 12.5 %all-to-all-start = ((bf16[16,128,264]{1,2,0:T(8,128)(2,1)}), bf16[16,128,264]{1,2,0:T(8,128)(2,1)S(1)}, u32[]{:S(2)}, u32[]{:S(2)}) async-start(bf16[16,128,264]{1,2,0:T(8,128)(2,1)} %copy.62), calls=%async_computation.1 | async-start | bytes 2162688 | tf_op jit(solution)/shard_map/all_to_all | solution.py:1877
  241.9 150.5 %home_sums.1.sums = f32[256,2176]{1,0:T(8,128)} custom-call(bf16[16,256,2176]{2,1,0:T(8,128)(2,1)} %bitcast.57), custom_call_target="tpu_custom_call" | custom-call | tf_op jit(solution)/shard_map/home_sums/pallas_call | solution.py:1708
  392.4 147.9 %attention_backward.1 = (f32[256,2048]{1,0:T(8,128)}, f32[128,1024]{1,0:T(8,128)}, f32[128,1536]{1,0:T(8,128)}, f32[32,2048]{1,0:T(8,128)}, f32[288,128]{1,0:T(8,128)}, /*index=5*/f32[24,128]{1,0:T(8,128)}) custom-call(s32[1,4]{1,0:T(1,128)} %lengths.3, f32[1,128]{1,0:T(1,128)} %constant.30.clone.freqs, f32[256,2176]{1,0:T(8,128)} %home_sums.1.sums, ...), custom_call_target="tpu_custom_call" | custom-call | tf_op jit(solution)/shard_map/attention_backward/pallas_call | solution.py:1471
  540.3 0.7 slice.36
  541.0 0.7 slice_bitcast_fusion
  541.7 0.6 dynamic_slice.18
  542.3 0.7 dynamic-slice_bitcast_fusion
  543.0 1.3 slice_bitcast_fusion.1
  544.4 1.1 copy.65
  545.5 1.1 copy.64
  546.6 1.1 copy.63
  547.8 1.8 collective-permute-start
  549.5 11.9 %convolution_bitcast_fusion.2 = f32[1,2048,704]{1,2,0:T(8,128)} fusion(bf16[2048,2048]{1,0:T(8,128)(2,1)} %bitcast.82, bf16[2048,768]{1,0:T(8,128)(2,1)} %bitcast.88), kind=kOutput, calls=%fused_computation.2 | convolution fusion | flops 5905580032 | bytes 17301504 | tf_op jit(solution)/shard_map/dot_general | solution.py:67
  561.4 8.3 %convolution_bitcast_fusion.1 = f32[1,2048,704]{1,2,0:T(8,128)} fusion(bf16[2048,2048]{1,0:T(8,128)(2,1)S(1)} %bitcast.85, bf16[2048,768]{1,0:T(8,128)(2,1)S(1)} %bitcast.87), kind=kOutput, calls=%fused_computation.1 | convolution fusion | flops 5905580032 | bytes 17301504 | tf_op jit(solution)/shard_map/dot_general | solution.py:67
  569.7 10.5 %convolution_bitcast_fusion = f32[1,2048,704]{1,2,0:T(8,128)} fusion(bf16[2048,2048]{1,0:T(8,128)(2,1)} %bitcast.81, bf16[2048,768]{1,0:T(8,128)(2,1)S(1)} %bitcast.86), kind=kOutput, calls=%fused_computation | convolution fusion | flops 5905580032 | bytes 17301504 | tf_op jit(solution)/shard_map/dot_general | solution.py:67
  580.2 1.4 add_convert_fusion
  581.7 0.4 copy-done.1
  582.1 1.3 copy.76
  583.4 0.9 copy.77
  584.3 0.7 copy.78
  585.0 0.7 copy.79
  585.7 0.8 copy.80
  (36 shorter events, 1.2 us)
Async XLA Ops:
  7.2 540.6 %reduce-scatter.2.cloned.1.call-start = ((), (), s32[]{:S(2)}) async-start(), calls=%async_computation.2 | async-start | bytes 17825792 | tf_op jit(solution)/shard_map/reduce_scatter | solution.py:1939
  10.4 4.3 copy-start.8
  226.4 1.4 copy-start.4
  229.3 314.9 %all-to-all-start = ((bf16[16,128,264]{1,2,0:T(8,128)(2,1)}), bf16[16,128,264]{1,2,0:T(8,128)(2,1)S(1)}, u32[]{:S(2)}, u32[]{:S(2)}) async-start(bf16[16,128,264]{1,2,0:T(8,128)(2,1)} %copy.62), calls=%async_computation.1 | async-start | bytes 2162688 | tf_op jit(solution)/shard_map/all_to_all | solution.py:1877
  547.8 13.7 %slice-start = ((s8[8388608]{0:T(1024)(128)(4,1)}), s8[4194304]{0:T(1024)(128)(4,1)S(1)}, s32[]{:S(2)}) async-start(s8[8388608]{0:T(1024)(128)(4,1)} %bitcast.83), calls=%async_computation.3 | async-start | bytes 8388608
  547.8 13.7 %slice-start.1 = ((s8[8388608]{0:T(1024)(128)(4,1)}), s8[4194304]{0:T(1024)(128)(4,1)S(1)}, s32[]{:S(2)}) async-start(s8[8388608]{0:T(1024)(128)(4,1)} %bitcast.83), calls=%async_computation.4 | async-start | bytes 8388608
  547.8 13.7 %copy-start.10 = (bf16[8,256,768]{2,1,0:T(8,128)(2,1)S(1)}, bf16[8,256,768]{2,1,0:T(8,128)(2,1)}, u32[]{:S(2)}) copy-start(bf16[8,256,768]{2,1,0:T(8,128)(2,1)} %get-tuple-element.70) | copy-start | bytes 9437188
  547.8 32.5 %collective-permute-start = (bf16[256,2048]{1,0:T(8,128)(2,1)}, bf16[256,2048]{1,0:T(8,128)(2,1)S(1)}, u32[]{:S(2)}, u32[]{:S(2)}) collective-permute-start(bf16[256,2048]{1,0:T(8,128)(2,1)} %reduce-scatter.2.cloned.1.call-done), channel_id=1, source_target_pairs={{0,1},{1,0},{2,3},{3,2},{4,5},{5,4},{6,7},{7,6},{8,9},{9,8},{10,11... | collective-permute-start | bytes 3145736 | tf_op jit(solution)/shard_map/ppermute | solution.py:1961
  561.4 8.3 %copy-start.9 = (bf16[8,256,768]{2,1,0:T(8,128)(2,1)S(1)}, bf16[8,256,768]{2,1,0:T(8,128)(2,1)}, u32[]{:S(2)}) copy-start(bf16[8,256,768]{2,1,0:T(8,128)(2,1)} %get-tuple-element.68) | copy-start | bytes 9437188
  569.7 10.5 %copy-start = (f32[256,2048]{1,0:T(8,128)S(1)}, f32[256,2048]{1,0:T(8,128)}, u32[]{:S(2)}) copy-start(f32[256,2048]{1,0:T(8,128)} %get-tuple-element.50.hidden) | copy-start | bytes 6291460
  569.7 10.5 %copy-start.2 = (bf16[256,2048]{1,0:T(8,128)(2,1)S(1)}, bf16[256,2048]{1,0:T(8,128)(2,1)}, u32[]{:S(2)}) copy-start(bf16[256,2048]{1,0:T(8,128)(2,1)} %reduce-scatter.2.cloned.1.call-done) | copy-start | bytes 3145732
  580.2 1.9 copy-start.1
  581.7 1.7 copy-start.3
  581.7 2.6 copy-start.7
  581.7 3.3 copy-start.6
  582.1 3.6 copy-start.5
Sparse Core Ops, SparseCore 0:
  226.5 247.8 reduce-scatter.1

commit v8 on v7

--- a/solution.py
+++ b/solution.py
@@ -1701,7 +1701,7 @@
                 along(p, w, w, z).wait_send()
 
 
-def home_sums(array, collective_id, parts, share=512):
+def home_sums(array, collective_id, parts, share=768):
     bf16, f32, dma = jnp.bfloat16, jnp.float32, pltpu.SemaphoreType.DMA
     rows, width = array.shape[1:]
     block = lambda *lead, cut=0: [pltpu.VMEM(lead + (rows // parts, width - cut), bf16)] * parts

time: 602 us -> 595 us (0.988)
  no operation moved by 1% of the time
where the time goes in v8:
time: 595 us; the launch traced here: 588 us
  Pallas kernels  504 us (85%)
  matrix products  30.6 us (5%)
  local copies, waits for them, and re-layouts  22.6 us (4%)
  between operations  14.4 us (2%)
  starting transfers between devices  14 us (2%)
    pallas_call x1, Pallas kernels, ffn_tuned(): pl.pallas_call(functools.partial(ffn_kernel, 2), out_shape=[shape((8, 2,...  149 us
    pallas_call x1, Pallas kernels, backward_tuned(): pl.pallas_call(backward_kernel, out_shape=[shape((rows, features), f32)]...  147 us
    pallas_call x1, Pallas kernels, home_sums(): pl.pallas_call(functools.partial(home_kernel, 2, parts, share), out_shape...  146 us
    pallas_call x1, Pallas kernels, forward_tuned(): pl.pallas_call(forward_kernel, out_shape=[shape((rows, features), f32), s...  61.5 us
    dot_general x3, matrix products, contract_first(): lax.dot_general(left, right, (((0,), (0,)), ((), ())), precision=precisio...  30.6 us
    all_to_all x1, starting transfers between devices, shared_home(): lax.all_to_all(grads.reshape(3 * part, devices, share_rows).transpose(1,...  12.5 us
  transfers between devices with their start and end apart: 3, of which 0 were waited for; matrix products, arithmetic and copies ran while one was open for 7% of the time, Pallas kernels for 50%

profile of v8, /device:TPU:0, one launch (start us, length us, event | category | flops | bytes accessed | tf_op | source)
XLA Modules:
  0.0 588.0 jit_solution(7285676813646109958)
XLA Ops:
  7.2 1.5 copy.58.routes
  8.7 1.4 constant_dynamic-slice_fusion.2
  10.4 2.0 constant_dynamic-slice_fusion
  12.8 0.8 pad.17.shared_out
  13.6 1.1 fusion.5.shared_in
  14.7 1.1 pad.14.router_t
  15.8 61.5 %attention_forward.1 = (f32[256,2048]{1,0:T(8,128)}, bf16[256,2048]{1,0:T(8,128)(2,1)}, f32[16,256]{1,0:T(8,128)}, f32[256,128]{1,0:T(8,128)}, bf16[256,2048]{1,...) custom-call(s32[1,4]{1,0:T(1,128)} %lengths.3, ...), custom_call_target="tpu_custom_call" | custom-call | tf_op jit(solution)/shard_map/attention_forward/pallas_call | solution.py:1040
  77.3 149.1 %ffn.1 = (bf16[8,2,256,2048]{3,2,1,0:T(8,128)(2,1)}, bf16[8,2,256,2176]{3,2,1,0:T(8,128)(2,1)}, bf16[8,256,2048]{2,1,0:T(8,128)(2,1)}, bf16[8,256,2048]{2,1,0:T(...) custom-call(bf16[256,2048]{1,0:T(8,128)(2,1)} %get-tuple-element.51., ...), custom_call_target="tpu_custom_call", output_to_operand_aliasing={{8}: (2, {})} | custom-call | tf_op jit(solution)/shard_map/ffn/pallas_call | solution.py:677
  226.4 1.4 copy-done.4
  228.1 1.3 copy.62
  229.3 12.5 %all-to-all-start = ((bf16[16,128,264]{1,2,0:T(8,128)(2,1)}), bf16[16,128,264]{1,2,0:T(8,128)(2,1)S(1)}, u32[]{:S(2)}, u32[]{:S(2)}) async-start(bf16[16,128,264]{1,2,0:T(8,128)(2,1)} %copy.62), calls=%async_computation.1 | async-start | bytes 2162688 | tf_op jit(solution)/shard_map/all_to_all | solution.py:1877
  241.9 146.1 %home_sums.1.sums = f32[256,2176]{1,0:T(8,128)} custom-call(bf16[16,256,2176]{2,1,0:T(8,128)(2,1)} %bitcast.57), custom_call_target="tpu_custom_call" | custom-call | tf_op jit(solution)/shard_map/home_sums/pallas_call | solution.py:1708
  388.0 147.1 %attention_backward.1 = (f32[256,2048]{1,0:T(8,128)}, f32[128,1024]{1,0:T(8,128)}, f32[128,1536]{1,0:T(8,128)}, f32[32,2048]{1,0:T(8,128)}, f32[288,128]{1,0:T(8,128)}, /*index=5*/f32[24,128]{1,0:T(8,128)}) custom-call(s32[1,4]{1,0:T(1,128)} %lengths.3, f32[1,128]{1,0:T(1,128)} %constant.30.clone.freqs, f32[256,2176]{1,0:T(8,128)} %home_sums.1.sums, ...), custom_call_target="tpu_custom_call" | custom-call | tf_op jit(solution)/shard_map/attention_backward/pallas_call | solution.py:1471
  535.2 0.7 slice.36
  535.9 0.7 slice_bitcast_fusion
  536.6 0.6 dynamic_slice.18
  537.1 0.7 dynamic-slice_bitcast_fusion
  537.8 1.3 slice_bitcast_fusion.1
  539.2 1.1 copy.65
  540.4 1.1 copy.64
  541.5 1.1 copy.63
  542.6 1.5 collective-permute-start
  544.1 11.8 %convolution_bitcast_fusion.2 = f32[1,2048,704]{1,2,0:T(8,128)} fusion(bf16[2048,2048]{1,0:T(8,128)(2,1)} %bitcast.82, bf16[2048,768]{1,0:T(8,128)(2,1)} %bitcast.88), kind=kOutput, calls=%fused_computation.2 | convolution fusion | flops 5905580032 | bytes 17301504 | tf_op jit(solution)/shard_map/dot_general | solution.py:67
  555.9 8.3 %convolution_bitcast_fusion.1 = f32[1,2048,704]{1,2,0:T(8,128)} fusion(bf16[2048,2048]{1,0:T(8,128)(2,1)S(1)} %bitcast.85, bf16[2048,768]{1,0:T(8,128)(2,1)S(1)} %bitcast.87), kind=kOutput, calls=%fused_computation.1 | convolution fusion | flops 5905580032 | bytes 17301504 | tf_op jit(solution)/shard_map/dot_general | solution.py:67
  564.2 10.5 %convolution_bitcast_fusion = f32[1,2048,704]{1,2,0:T(8,128)} fusion(bf16[2048,2048]{1,0:T(8,128)(2,1)} %bitcast.81, bf16[2048,768]{1,0:T(8,128)(2,1)S(1)} %bitcast.86), kind=kOutput, calls=%fused_computation | convolution fusion | flops 5905580032 | bytes 17301504 | tf_op jit(solution)/shard_map/dot_general | solution.py:67
  574.7 1.4 add_convert_fusion
  576.2 0.4 copy-done.1
  576.6 1.3 copy.76
  577.9 0.9 copy.77
  578.8 0.7 copy.78
  579.5 0.7 copy.79
  580.2 0.8 copy.80
  (36 shorter events, 1.2 us)
Async XLA Ops:
  7.2 535.4 %reduce-scatter.2.cloned.1.call-start = ((), (), s32[]{:S(2)}) async-start(), calls=%async_computation.2 | async-start | bytes 17825792 | tf_op jit(solution)/shard_map/reduce_scatter | solution.py:1939
  10.4 4.3 copy-start.8
  226.4 1.4 copy-start.4
  229.3 309.7 %all-to-all-start = ((bf16[16,128,264]{1,2,0:T(8,128)(2,1)}), bf16[16,128,264]{1,2,0:T(8,128)(2,1)S(1)}, u32[]{:S(2)}, u32[]{:S(2)}) async-start(bf16[16,128,264]{1,2,0:T(8,128)(2,1)} %copy.62), calls=%async_computation.1 | async-start | bytes 2162688 | tf_op jit(solution)/shard_map/all_to_all | solution.py:1877
  542.6 13.3 %slice-start = ((s8[8388608]{0:T(1024)(128)(4,1)}), s8[4194304]{0:T(1024)(128)(4,1)S(1)}, s32[]{:S(2)}) async-start(s8[8388608]{0:T(1024)(128)(4,1)} %bitcast.83), calls=%async_computation.3 | async-start | bytes 8388608
  542.6 13.3 %slice-start.1 = ((s8[8388608]{0:T(1024)(128)(4,1)}), s8[4194304]{0:T(1024)(128)(4,1)S(1)}, s32[]{:S(2)}) async-start(s8[8388608]{0:T(1024)(128)(4,1)} %bitcast.83), calls=%async_computation.4 | async-start | bytes 8388608
  542.6 13.3 %copy-start.10 = (bf16[8,256,768]{2,1,0:T(8,128)(2,1)S(1)}, bf16[8,256,768]{2,1,0:T(8,128)(2,1)}, u32[]{:S(2)}) copy-start(bf16[8,256,768]{2,1,0:T(8,128)(2,1)} %get-tuple-element.70) | copy-start | bytes 9437188
  542.6 32.1 %collective-permute-start = (bf16[256,2048]{1,0:T(8,128)(2,1)}, bf16[256,2048]{1,0:T(8,128)(2,1)S(1)}, u32[]{:S(2)}, u32[]{:S(2)}) collective-permute-start(bf16[256,2048]{1,0:T(8,128)(2,1)} %reduce-scatter.2.cloned.1.call-done), channel_id=1, source_target_pairs={{0,1},{1,0},{2,3},{3,2},{4,5},{5,4},{6,7},{7,6},{8,9},{9,8},{10,11... | collective-permute-start | bytes 3145736 | tf_op jit(solution)/shard_map/ppermute | solution.py:1961
  555.9 8.3 %copy-start.9 = (bf16[8,256,768]{2,1,0:T(8,128)(2,1)S(1)}, bf16[8,256,768]{2,1,0:T(8,128)(2,1)}, u32[]{:S(2)}) copy-start(bf16[8,256,768]{2,1,0:T(8,128)(2,1)} %get-tuple-element.68) | copy-start | bytes 9437188
  564.2 10.5 %copy-start = (f32[256,2048]{1,0:T(8,128)S(1)}, f32[256,2048]{1,0:T(8,128)}, u32[]{:S(2)}) copy-start(f32[256,2048]{1,0:T(8,128)} %get-tuple-element.50.hidden) | copy-start | bytes 6291460
  564.2 10.5 %copy-start.2 = (bf16[256,2048]{1,0:T(8,128)(2,1)S(1)}, bf16[256,2048]{1,0:T(8,128)(2,1)}, u32[]{:S(2)}) copy-start(bf16[256,2048]{1,0:T(8,128)(2,1)} %reduce-scatter.2.cloned.1.call-done) | copy-start | bytes 3145732
  574.7 1.9 copy-start.1
  576.2 1.7 copy-start.3
  576.2 2.6 copy-start.7
  576.2 3.3 copy-start.6
  576.6 3.6 copy-start.5
Sparse Core Ops, SparseCore 0:
  226.5 242.4 reduce-scatter.1
